TPU v7x, 512 devices: a whole 4x8x8 slice. The times are simulated.
512 devices in a mesh: dp: 16 (over z_lo, x), ctx: 32 (over y, z_hi, core).
Axes of the slice: x: 4, y: 8, z: 8 (z_hi: 2, z_lo: 4; z = z_hi * 4 + z_lo), core: 2. Of those that a mesh axis runs over, the one named last changes fastest.
Arguments:
- queries: bfloat16 [16, 4096, 512], P('dp', 'ctx'), may hold values from -6 to 6
- key_states: bfloat16 [16, 4096, 512], P('dp', 'ctx'), may hold values from -6 to 6
- value_states: bfloat16 [16, 4096, 512], P('dp', 'ctx'), may hold values from -6 to 6
- gate_states: bfloat16 [16, 4096, 512], P('dp', 'ctx'), may hold values from -6 to 6
- out_grad: bfloat16 [16, 4096, 512], P('dp', 'ctx'), may hold values from -6 to 6
- segment_ids: int32 [16, 4096], P('dp'), may hold values from 0 to 3, never falling along the last dimension, each value on 1 to 2048 neighbouring positions
- norm_gain: float32 [512], replicated, may hold values from 0.1 to 1.9
Outputs:
- layer_out: bfloat16 [16, 4096, 512], P('dp', 'ctx')
- query_grad: bfloat16 [16, 4096, 512], P('dp', 'ctx')
- key_grad: bfloat16 [16, 4096, 512], P('dp', 'ctx')
- value_grad: bfloat16 [16, 4096, 512], P('dp', 'ctx')
- gate_grad: bfloat16 [16, 4096, 512], P('dp', 'ctx')
- gain_grad: float32 [512], replicated
Inputs may be any that keep to these rules, and one draw needn't show every extreme that they name: `segment_ids`: in each sample the history numbers never fall, each of the 4 histories has 1 to 2048 positions and one has exactly 2048.
All inputs are finite; a program needn't handle non-finite values.
Results may differ from a plain program's by a relative error of at most 0.0058.
Values may be sent and summed in bfloat16 or wider, within the bound.
No kernel may reach another device: no remote copies, remote signals or barrier semaphores. Data moves between devices by JAX's collectives and lax.ppermute only.
A program may use at most 64 MiB of HBM per device.

v0:
```python
import math

import jax
import jax.numpy as jnp
from jax import lax
from jax.sharding import PartitionSpec as P

HEADS = 4
HSIZE = 128


def head_dot(left_rows, right_rows):
    left_heads = left_rows.reshape(left_rows.shape[0], HEADS, HSIZE)
    right_heads = right_rows.reshape(right_rows.shape[0], HEADS, HSIZE)
    return jnp.einsum("qhd,khd->hqk", left_heads, right_heads, preferred_element_type=jnp.float32)


def head_product(weights, rows):
    rows_heads = rows.reshape(rows.shape[0], HEADS, HSIZE)
    result = jnp.einsum("hqk,khd->qhd", weights, rows_heads, preferred_element_type=jnp.float32)
    return result.reshape(result.shape[0], HEADS * HSIZE)


def head_product_back(weights, rows):
    rows_heads = rows.reshape(rows.shape[0], HEADS, HSIZE)
    result = jnp.einsum("hqk,qhd->khd", weights, rows_heads, preferred_element_type=jnp.float32)
    return result.reshape(result.shape[0], HEADS * HSIZE)


def visible_pairs(query_seg, key_seg):
    return (query_seg[:, None] == key_seg[None, :])[None]


def silu_slope(scores):
    sigmoid = jax.nn.sigmoid(scores)
    return sigmoid * (1.0 + scores * (1.0 - sigmoid))


def per_device(queries, key_states, value_states, gate_states, out_grad, segment_ids, norm_gain):
    scale = HSIZE ** (-0.5)
    tok_rows = queries.shape[1]
    hidden = queries.shape[2]
    seq_len = segment_ids.shape[1]
    segs = segment_ids[0]
    my_first = lax.axis_index("ctx") * tok_rows
    own_seg = lax.dynamic_slice_in_dim(segs, my_first, tok_rows, 0)
    own_query = queries[0]
    own_key = key_states[0]
    own_value = value_states[0]
    all_keys, all_values = (
        lax.all_gather(key_states, "ctx", axis=1, tiled=True),
        lax.all_gather(value_states, "ctx", axis=1, tiled=True),
    )
    all_keys = all_keys[0]
    all_values = all_values[0]
    block = math.gcd(seq_len, 512)
    blocks_count = seq_len // block

    def forward_step(block_id, running):
        key_first = block_id * block
        key_block = lax.dynamic_slice_in_dim(all_keys, key_first, block, 0)
        value_block = lax.dynamic_slice_in_dim(all_values, key_first, block, 0)
        key_seg = lax.dynamic_slice_in_dim(segs, key_first, block, 0)
        scores = scale * head_dot(own_query, key_block)
        visible = visible_pairs(own_seg, key_seg)
        weights = jnp.where(visible, jax.nn.silu(scores), 0.0).astype(jnp.bfloat16)
        return running + head_product(weights, value_block)

    attended = lax.fori_loop(
        0, blocks_count, forward_step, jnp.zeros((tok_rows, hidden), jnp.float32)
    )
    inv_rms = lax.rsqrt(jnp.mean(attended * attended, axis=1, keepdims=True) + 1e-06)
    normed = attended * inv_rms
    gain_row = norm_gain[None, :]
    gate_f = gate_states[0].astype(jnp.float32)
    grad_f = out_grad[0].astype(jnp.float32)
    layer_out = (normed * gain_row * gate_f).astype(jnp.bfloat16)
    gate_grad = (grad_f * normed * gain_row).astype(jnp.bfloat16)
    gain_part = jnp.sum(grad_f * normed * gate_f, axis=0)
    total_rows = lax.axis_size("dp") * lax.axis_size("ctx") * tok_rows
    gain_grad = lax.psum(gain_part, ("dp", "ctx")) / math.sqrt(total_rows)
    normed_grad = grad_f * gain_row * gate_f
    attn_grad = (
        inv_rms * (normed_grad - normed * jnp.mean(normed * normed_grad, axis=1, keepdims=True))
    ).astype(jnp.bfloat16)

    def query_step(block_id, running):
        key_first = block_id * block
        key_block = lax.dynamic_slice_in_dim(all_keys, key_first, block, 0)
        value_block = lax.dynamic_slice_in_dim(all_values, key_first, block, 0)
        key_seg = lax.dynamic_slice_in_dim(segs, key_first, block, 0)
        scores = scale * head_dot(own_query, key_block)
        visible = visible_pairs(own_seg, key_seg)
        value_dot = head_dot(attn_grad, value_block)
        slopes = jnp.where(visible, scale * value_dot * silu_slope(scores), 0.0).astype(
            jnp.bfloat16
        )
        return running + head_product(slopes, key_block)

    query_grad = lax.fori_loop(
        0, blocks_count, query_step, jnp.zeros((tok_rows, hidden), jnp.float32)
    )
    zeros_block = jnp.zeros((tok_rows, hidden), jnp.float32)
    grad_piece = attn_grad[None]
    query_rows = lax.all_gather(queries, "ctx", axis=1, tiled=True)[0]
    grad_rows = lax.all_gather(grad_piece, "ctx", axis=1, tiled=True)[0]
    row_count = grad_rows.shape[0]
    step_rows = math.gcd(row_count, 512)

    def key_step(block_id, totals):
        row_first = block_id * step_rows
        query_block = lax.dynamic_slice_in_dim(query_rows, row_first, step_rows, 0)
        grad_block = lax.dynamic_slice_in_dim(grad_rows, row_first, step_rows, 0)
        query_seg = lax.dynamic_slice_in_dim(segs, row_first, step_rows, 0)
        scores = scale * head_dot(query_block, own_key)
        visible = visible_pairs(query_seg, own_seg)
        weights = jnp.where(visible, jax.nn.silu(scores), 0.0).astype(jnp.bfloat16)
        value_dot = head_dot(grad_block, own_value)
        slopes = jnp.where(visible, scale * value_dot * silu_slope(scores), 0.0).astype(
            jnp.bfloat16
        )
        return (
            totals[0] + head_product_back(slopes, query_block),
            totals[1] + head_product_back(weights, grad_block),
        )

    key_grad, value_grad = lax.fori_loop(
        0, row_count // step_rows, key_step, (zeros_block, zeros_block)
    )
    return (
        layer_out[None],
        query_grad.astype(jnp.bfloat16)[None],
        key_grad.astype(jnp.bfloat16)[None],
        value_grad.astype(jnp.bfloat16)[None],
        gate_grad[None],
        gain_grad,
    )


def solution(mesh):
    return jax.shard_map(
        per_device,
        mesh=mesh,
        in_specs=(
            P("dp", "ctx", None),
            P("dp", "ctx", None),
            P("dp", "ctx", None),
            P("dp", "ctx", None),
            P("dp", "ctx", None),
            P("dp", None),
            P(),
        ),
        out_specs=(
            P("dp", "ctx", None),
            P("dp", "ctx", None),
            P("dp", "ctx", None),
            P("dp", "ctx", None),
            P("dp", "ctx", None),
            P(),
        ),
        check_vma=False,
    )
```

profile of v0, /device:TPU:1, one launch (start us, length us, event | category | flops | bytes accessed | tf_op | source)
XLA Modules:
  0.0 511.9 jit_solution(14382006248976778904)
XLA Ops:
  7.2 1.7 copy.34
  9.7 1.7 copy.38
  15.6 111.8 %all-gather.8.cloned.1.call-done = bf16[1,4096,512]{1,2,0:T(8,128)(2,1)} async-done(((bf16[1,128,512]{1,2,0:T(8,128)(2,1)}), bf16[1,4096,512]{1,2,0:T(8,128)(2,1)}) %all-gather.8.cloned.1.call-update) | async-done | bytes 4194320 | tf_op jit(solution)/shard_map/all_gather | solution.py:51
  127.4 104.0 %all-gather.6.cloned.1.call-done = bf16[1,4096,512]{2,1,0:T(8,128)(2,1)} async-done(((bf16[1,128,512]{2,1,0:T(8,128)(2,1)}), bf16[1,4096,512]{2,1,0:T(8,128)(2,1)}) %all-gather.6.cloned.1.call-update) | async-done | bytes 4194320 | tf_op jit(solution)/shard_map/all_gather | solution.py:52
  231.4 32.6 %while.47 = (s32[]{:T(128)}, f32[128,512]{0,1:T(8,128)S(1)}, bf16[4096,512]{1,0:T(8,128)(2,1)}, s32[128]{0:T(128)S(1)}, s32[4096]{0:T(1024)}, /*index=5*/bf16[40...) while((s32[]{:T(128)}, f32[128,512]{0,1:T(8,128)S(1)}, ...), condition=%wide.wide.region_1.2_spmd.clone, body=%wide.wide.region_0.1_spmd.clone.sunk | while | flops 136249344 | bytes 5511865 | solution.py:69
  265.9 41.7 %while.48 = (s32[]{:T(128)}, f32[128,512]{0,1:T(8,128)S(1)}, bf16[4096,512]{0,1:T(8,128)(2,1)}, s32[128]{0:T(128)S(1)}, s32[4096]{0:T(1024)}, /*index=5*/bf16[40...) while((s32[]{:T(128)}, f32[128,512]{0,1:T(8,128)S(1)}, ...), condition=%wide.wide.region_5.6_spmd.clone, body=%wide.wide.region_4.5_spmd.clone.sunk | while | flops 204668928 | bytes 6429377 | solution.py:100
  269.4 1.7 fusion.118
  274.6 1.7 fusion.118
  279.8 1.7 fusion.118
  285.1 1.7 fusion.118
  290.3 1.7 fusion.118
  295.5 1.7 fusion.118
  300.7 1.7 fusion.118
  305.9 1.7 fusion.118
  308.5 101.4 %psum.7 = f32[512]{0:T(512)S(1)} all-reduce(f32[512]{0:T(512)S(1)} %get-tuple-element.541), channel_id=1, replica_groups=mesh['dp'=16,'ctx'=32] {'dp','ctx'}, use_global_device_ids=true, to_apply=%region_9.10 | all-reduce | flops 512 | bytes 4096 | tf_op jit(solution)/shard_map/psum | solution.py:81
  410.4 32.7 %all-gather.12.cloned.1.call-done = bf16[4096,512]{1,0:T(8,128)(2,1)} async-done(((bf16[128,512]{1,0:T(8,128)(2,1)}), bf16[4096,512]{1,0:T(8,128)(2,1)}) %all-gather.12.cloned.1.call-update) | async-done | bytes 4194320 | tf_op jit(solution)/shard_map/all_gather | solution.py:106
  443.1 60.7 %while.49 = (s32[]{:T(128)}, f32[128,512]{0,1:T(8,128)S(1)}, f32[128,512]{0,1:T(8,128)S(1)}, bf16[4096,512]{0,1:T(8,128)(2,1)}, s32[4096]{0:T(1024)}, /*index=5*...) while((s32[]{:T(128)}, f32[128,512]{0,1:T(8,128)S(1)}, ...), condition=%wide.wide.region_7.8_spmd.clone, body=%wide.wide.region_6.7_spmd.clone.sunk | while | flops 273481728 | bytes 11475685 | solution.py:127
  456.0 1.6 fusion.126
  463.6 1.6 fusion.126
  471.2 1.6 fusion.126
  478.8 1.6 fusion.126
  486.4 1.6 fusion.126
  494.0 1.6 fusion.126
  501.6 1.6 fusion.126
  (228 shorter events, 118.1 us)
Async XLA Ops:
  7.2 120.3 %all-gather.8.cloned.1.call-start = ((), (), s32[]{:S(2)}) async-start(), calls=%async_computation.1 | async-start | bytes 4325376 | tf_op jit(solution)/shard_map/all_gather | solution.py:51
  8.9 222.5 %all-gather.6.cloned.1.call-start = ((), (), s32[]{:S(2)}) async-start(), calls=%async_computation | async-start | bytes 4325376 | tf_op jit(solution)/shard_map/all_gather | solution.py:52
  9.7 400.7 %all-gather.10.cloned.1.call-start = ((), (), s32[]{:S(2)}) async-start(), calls=%async_computation.2 | async-start | bytes 4325376 | tf_op jit(solution)/shard_map/all_gather | solution.py:105
  11.4 431.7 %all-gather.12.cloned.1.call-start = ((), (), s32[]{:S(2)}) async-start(), calls=%async_computation.3 | async-start | bytes 4325376 | tf_op jit(solution)/shard_map/all_gather | solution.py:106
  231.4 32.8 %copy-start.2 = (bf16[1,128,512]{2,1,0:T(8,128)(2,1)S(1)}, bf16[1,128,512]{2,1,0:T(8,128)(2,1)}, u32[]{:S(2)}) copy-start(bf16[1,128,512]{2,1,0:T(8,128)(2,1)} %param.17) | copy-start | bytes 393220
  231.4 32.8 %copy-start.3 = (bf16[1,128,512]{2,1,0:T(8,128)(2,1)S(1)}, bf16[1,128,512]{2,1,0:T(8,128)(2,1)}, u32[]{:S(2)}) copy-start(bf16[1,128,512]{2,1,0:T(8,128)(2,1)} %param.16) | copy-start | bytes 393220
  231.4 32.8 %copy-start.4 = (f32[512]{0:T(512)S(1)}, f32[512]{0:T(512)}, u32[]{:S(2)}) copy-start(f32[512]{0:T(512)} %param.19) | copy-start | bytes 6148
  265.9 177.2 %copy-start = (bf16[1,128,512]{2,1,0:T(8,128)(2,1)S(1)}, bf16[1,128,512]{2,1,0:T(8,128)(2,1)}, u32[]{:S(2)}) copy-start(bf16[1,128,512]{2,1,0:T(8,128)(2,1)} %param.15) | copy-start | bytes 393220
  448.3 1.7 copy-start.1
  455.9 1.7 copy-start.1
  463.5 1.7 copy-start.1
  471.1 1.7 copy-start.1
  478.7 1.7 copy-start.1
  486.3 1.7 copy-start.1
  493.8 1.7 copy-start.1
  501.4 1.7 copy-start.1
Sparse Core Ops, SparseCore 0:
  11.7 115.6 all-gather.7
  130.8 100.6 all-gather.5
  235.1 103.4 all-gather.9
  342.4 100.7 all-gather.11
where the time goes:
time: 516 us; the launch traced here: 512 us
  waiting for transfers between devices  249 us (48%)
  blocking collectives  101 us (20%)
  local copies, waits for them, and re-layouts  84.2 us (16%)
  matrix products  48.8 us (9%)
  between operations  13.9 us (3%)
  other arithmetic  12.6 us (2%)
    all_gather x1, waiting for transfers between devices, per_device(): lax.all_gather(key_states, 'ctx', axis=1, tiled=True)  112 us
    all_gather x1, waiting for transfers between devices, per_device(): lax.all_gather(value_states, 'ctx', axis=1, tiled=True)  104 us
    psum x1, blocking collectives, per_device(): gain_grad = lax.psum(gain_part, ('dp', 'ctx')) / math.sqrt(total_rows)  101 us
    all_gather x1, waiting for transfers between devices, per_device(): grad_rows = lax.all_gather(grad_piece, 'ctx', axis=1, tiled=True)[0]  32.7 us
    dot_general x16, matrix products, head_product(): jnp.einsum('hqk,khd->qhd', weights, rows_heads, preferred_element_type=jn...  19.3 us
    dot_general x16, matrix products, head_product_back(): jnp.einsum('hqk,qhd->khd', weights, rows_heads, preferred_element_type=jn...  16.7 us
    dot_general x16, matrix products, head_dot(): jnp.einsum('qhd,khd->hqk', left_heads, right_heads, preferred_element_typ...  12.8 us
    dynamic_slice x16, local copies, waits for them, and re-layouts, forward_step(): value_block = lax.dynamic_slice_in_dim(all_values, key_first, block, 0)  10.4 us
  transfers between devices with their start and end apart: 4, of which 3 were waited for; matrix products, arithmetic and copies ran while one was open for 16% of the time, Pallas kernels for 0%

commit v1 on v0

v1 whole, which is shorter than its diff:
```python
import functools
import math

import jax
import jax.numpy as jnp
from jax import lax
from jax.experimental import pallas as pl
from jax.experimental.pallas import tpu as pltpu
from jax.sharding import PartitionSpec as P

HEADS = 4
HSIZE = 128
HD = 512
ROWS = 128
QUAD = 4
RING = 8
TILE = QUAD * ROWS
HALF = TILE // 2
SCALE = HSIZE ** (-0.5)
CHUNK = 256
NT = (((1,), (1,)), ((), ()))
NN = (((1,), (0,)), ((), ()))
TN = (((0,), (0,)), ((), ()))
VMEM_LIMIT = 48 * 1024 * 1024
OFFSETS = (0, -1, 1, -2, 2, -3, 3, 4)


def dot(left, right, dims):
    return lax.dot_general(left, right, dims, preferred_element_type=jnp.float32)


def along_y(value, step):
    return lax.ppermute(
        value,
        "ctx",
        [
            (y * QUAD + c, ((y + step) % RING) * QUAD + c)
            for y in range(RING)
            for c in range(QUAD)
        ],
    )


def in_quad(value, flip):
    return lax.ppermute(
        value,
        "ctx",
        [(y * QUAD + c, y * QUAD + (c ^ flip)) for y in range(RING) for c in range(QUAD)],
    )


def block_of(refs, offset, which):
    if offset < 7:
        return refs[offset][which]
    return jnp.concatenate([refs[7][which], refs[8][which]], axis=0)


def head(h):
    return slice(h * HSIZE, (h + 1) * HSIZE)


def forward_kernel(info, qseg, kseg, q, *rest):
    kv, (keep, send, acc) = rest[:9], rest[9:]
    y = info[0]
    acc[...] = jnp.zeros_like(acc)
    for r, off in enumerate(OFFSETS):
        yy = lax.rem(y + (off + RING), RING)

        @pl.when(info[1 + r] > 0)
        def _(r=r, yy=yy):
            krow = kseg[pl.ds(yy, 1), :]
            for h in range(HEADS):
                kb = block_of(kv, r, 0)[:, head(h)]
                vb = block_of(kv, r, 1)[:, head(h)]
                for c in range(TILE // CHUNK):
                    rows = slice(c * CHUNK, (c + 1) * CHUNK)
                    half = dot(q[rows, head(h)], kb, NT) * (0.5 * SCALE)
                    silu = half + half * jnp.tanh(half)
                    w = jnp.where(qseg[rows, :] == krow, silu, 0.0).astype(jnp.bfloat16)
                    acc[rows, head(h)] += dot(w, vb, NN)

    keep[...] = acc[:HALF, :]
    send[...] = acc[HALF:, :].astype(jnp.bfloat16)


def norm_kernel(mine, other, gate, grad, gain, out, gate_grad, attn_grad, part):
    att = mine[...] + other[...].astype(jnp.float32)
    inv = lax.rsqrt(jnp.mean(att * att, axis=1, keepdims=True) + 1e-06)
    normed = att * inv
    g = gain[...]
    gate_f = gate[0].astype(jnp.float32)
    grad_f = grad[0].astype(jnp.float32)
    out[0] = (normed * g * gate_f).astype(jnp.bfloat16)
    gate_grad[0] = (grad_f * normed * g).astype(jnp.bfloat16)
    both = grad_f * gate_f
    part[...] = jnp.broadcast_to(jnp.sum(both * normed, axis=0, keepdims=True), part.shape)
    ng = both * g
    mean = jnp.mean(normed * ng, axis=1, keepdims=True)
    attn_grad[...] = (inv * (ng - normed * mean)).astype(jnp.bfloat16)


def backward_kernel(info, qseg, kseg, q, da, *rest):
    kv, (keep, send, dkv, acc, dk, dv) = rest[:9], rest[9:]
    y = info[0]
    acc[...] = jnp.zeros_like(acc)
    for r, off in enumerate(OFFSETS):
        yy = lax.rem(y + (off + RING), RING)

        @pl.when(info[1 + r] > 0)
        def _(r=r, yy=yy):
            krow = kseg[pl.ds(yy, 1), :]
            for h in range(HEADS):
                kb = block_of(kv, r, 0)[:, head(h)]
                vb = block_of(kv, r, 1)[:, head(h)]
                for c in range(TILE // CHUNK):
                    rows = slice(c * CHUNK, (c + 1) * CHUNK)
                    qb = q[rows, head(h)]
                    db = da[rows, head(h)]
                    half = dot(qb, kb, NT) * (0.5 * SCALE)
                    vd = dot(db, vb, NT)
                    t = jnp.tanh(half)
                    seen = qseg[rows, :] == krow
                    w = jnp.where(seen, half + half * t, 0.0).astype(jnp.bfloat16)
                    bend = 1.0 + half * (1.0 - t)
                    slope = (0.5 * SCALE) * vd * (1.0 + t) * bend
                    slope = jnp.where(seen, slope, 0.0).astype(jnp.bfloat16)
                    acc[rows, head(h)] += dot(slope, kb, NN)
                    dk_part = dot(slope, qb, TN)
                    dv_part = dot(w, db, TN)
                    if c == 0:
                        dk[:, head(h)] = dk_part
                        dv[:, head(h)] = dv_part
                    else:
                        dk[:, head(h)] += dk_part
                        dv[:, head(h)] += dv_part
            dkv[yy, 0] = dk[...].astype(jnp.bfloat16)
            dkv[yy, 1] = dv[...].astype(jnp.bfloat16)

        @pl.when(info[1 + r] == 0)
        def _(yy=yy):
            dkv[yy] = jnp.zeros((2, ROWS, HD), jnp.bfloat16)

    keep[...] = acc[:HALF, :]
    send[...] = acc[HALF:, :].astype(jnp.bfloat16)


def vmem(count):
    return [pl.BlockSpec(memory_space=pltpu.VMEM)] * count


def smem():
    return [pl.BlockSpec(memory_space=pltpu.SMEM)]


def params():
    return pltpu.CompilerParams(vmem_limit_bytes=VMEM_LIMIT)


def per_device(queries, key_states, value_states, gate_states, out_grad, segment_ids, norm_gain):
    place = lax.axis_index("ctx")
    y, quad = place // QUAD, lax.rem(place, QUAD)
    kv = jnp.concatenate([key_states, value_states], axis=0)

    q_pair = jnp.concatenate([queries[0], in_quad(queries[0], 2)], axis=0)
    q_tile = jnp.concatenate([q_pair, in_quad(q_pair, 1)], axis=0)

    up = down = kv
    blocks = [kv]
    for _ in range(3):
        up, down = along_y(up, 1), along_y(down, -1)
        blocks += [up, down]
    blocks += [along_y(up[:, : ROWS // 2], 1), along_y(down[:, ROWS // 2 :], -1)]

    segs = segment_ids.reshape(RING, QUAD, ROWS)
    kseg = lax.dynamic_index_in_dim(segs, quad, 1, keepdims=False)
    own = lax.dynamic_index_in_dim(segs, y, 0, keepdims=False)
    qseg = jnp.concatenate(
        [lax.dynamic_index_in_dim(own, quad ^ flip, 0, keepdims=False) for flip in (0, 2, 1, 3)]
    )
    low, high = own[0, 0], own[QUAD - 1, ROWS - 1]
    qseg = jnp.broadcast_to(qseg[:, None], (TILE, HSIZE))
    seen = ((kseg[:, 0] <= high) & (kseg[:, ROWS - 1] >= low)).astype(jnp.int32)
    seen = jnp.stack(
        [lax.dynamic_index_in_dim(seen, lax.rem(y + (off + RING), RING), 0, False) for off in OFFSETS]
    )
    info = jnp.concatenate([y.astype(jnp.int32)[None], seen])

    keep, send = pl.pallas_call(
        forward_kernel,
        out_shape=(
            jax.ShapeDtypeStruct((HALF, HD), jnp.float32),
            jax.ShapeDtypeStruct((HALF, HD), jnp.bfloat16),
        ),
        in_specs=smem() + vmem(12),
        out_specs=tuple(vmem(2)),
        scratch_shapes=[pltpu.VMEM((TILE, HD), jnp.float32)],
        compiler_params=params(),
        name="forward_tile",
    )(info, qseg, kseg, q_tile, *blocks)
    keep = keep + in_quad(send, 1).astype(jnp.float32)
    mine, send = keep[:ROWS], keep[ROWS:].astype(jnp.bfloat16)
    other = in_quad(send, 2)

    row = jax.ShapeDtypeStruct((1, ROWS, HD), jnp.bfloat16)
    layer_out, gate_grad, attn_grad, part = pl.pallas_call(
        norm_kernel,
        out_shape=(
            row,
            row,
            jax.ShapeDtypeStruct((ROWS, HD), jnp.bfloat16),
            jax.ShapeDtypeStruct((8, HD), jnp.float32),
        ),
        in_specs=vmem(5),
        out_specs=tuple(vmem(4)),
        compiler_params=params(),
        name="norm_rows",
    )(mine, other, gate_states, out_grad, norm_gain[None, :])

    grad_pair = jnp.concatenate([attn_grad, in_quad(attn_grad, 2)], axis=0)
    grad_tile = jnp.concatenate([grad_pair, in_quad(grad_pair, 1)], axis=0)

    keep, send, dkv = pl.pallas_call(
        backward_kernel,
        out_shape=(
            jax.ShapeDtypeStruct((HALF, HD), jnp.float32),
            jax.ShapeDtypeStruct((HALF, HD), jnp.bfloat16),
            jax.ShapeDtypeStruct((RING, 2, ROWS, HD), jnp.bfloat16),
        ),
        in_specs=smem() + vmem(13),
        out_specs=tuple(vmem(3)),
        scratch_shapes=[
            pltpu.VMEM((TILE, HD), jnp.float32),
            pltpu.VMEM((ROWS, HD), jnp.float32),
            pltpu.VMEM((ROWS, HD), jnp.float32),
        ],
        compiler_params=params(),
        name="backward_tile",
    )(info, qseg, kseg, q_tile, grad_tile, *blocks)

    parts = lax.all_to_all(
        dkv,
        "ctx",
        split_axis=0,
        concat_axis=0,
        tiled=True,
        axis_index_groups=[[y * QUAD + c for y in range(RING)] for c in range(QUAD)],
    )
    keep = keep + in_quad(send, 1).astype(jnp.float32)
    mine, send = keep[:ROWS], keep[ROWS:].astype(jnp.bfloat16)
    query_grad = (mine + in_quad(send, 2).astype(jnp.float32)).astype(jnp.bfloat16)
    total = jnp.sum(parts.astype(jnp.float32), axis=0).astype(jnp.bfloat16)

    gain_sum = part[:1]
    for flip in (1, 2):
        gain_sum = gain_sum + in_quad(gain_sum, flip)
    for flip in (1, 2, 4):
        gain_sum = gain_sum + lax.ppermute(
            gain_sum,
            "ctx",
            [(i, i ^ (flip * QUAD)) for i in range(RING * QUAD)],
        )
    dp = lax.axis_size("dp")
    flip = 1
    while flip < dp:
        gain_sum = gain_sum + lax.ppermute(gain_sum, "dp", [(i, i ^ flip) for i in range(dp)])
        flip *= 2
    gain_grad = gain_sum[0] / math.sqrt(dp * RING * QUAD * ROWS)

    return (
        layer_out,
        query_grad[None],
        total[:1],
        total[1:],
        gate_grad,
        gain_grad,
    )


def solution(mesh):
    rows = P("dp", "ctx", None)
    return jax.shard_map(
        per_device,
        mesh=mesh,
        in_specs=(rows, rows, rows, rows, rows, P("dp", None), P()),
        out_specs=(rows, rows, rows, rows, rows, P()),
        check_vma=False,
    )
```

time: 516 us -> 216 us (0.42)
  the two profiles are of different devices: /device:TPU:1 before, /device:TPU:40 now
where the time goes in v1:
time: 216 us; the launch traced here: 215 us
  starting transfers between devices  105 us (49%)
  waiting for transfers between devices  82.9 us (38%)
  local copies, waits for them, and re-layouts  11.4 us (5%)
  Pallas kernels  9.99 us (5%)
  other arithmetic  5.13 us (2%)
    ppermute x3, waiting for transfers between devices, per_device(): lax.ppermute(gain_sum, 'ctx', [(i, i ^ flip * QUAD) for i in range(RING *...  40.6 us
    ppermute x10, starting transfers between devices, in_quad(): lax.ppermute(value, 'ctx', [(y * QUAD + c, y * QUAD + (c ^ flip)) for y i...  35.4 us
    ppermute x10, waiting for transfers between devices, in_quad(): lax.ppermute(value, 'ctx', [(y * QUAD + c, y * QUAD + (c ^ flip)) for y i...  31.1 us
    ppermute x8, starting transfers between devices, along_y(): lax.ppermute(value, 'ctx', [(y * QUAD + c, (y + step) % RING * QUAD + c)...  23.1 us
    all_to_all x1, starting transfers between devices, per_device(): lax.all_to_all(dkv, 'ctx', split_axis=0, concat_axis=0, tiled=True, axis_...  21.7 us
    ppermute x4, starting transfers between devices, per_device(): lax.ppermute(gain_sum, 'dp', [(i, i ^ flip) for i in range(dp)])  16.7 us
    ppermute x4, waiting for transfers between devices, per_device(): lax.ppermute(gain_sum, 'dp', [(i, i ^ flip) for i in range(dp)])  8.23 us
    ppermute x3, starting transfers between devices, per_device(): lax.ppermute(gain_sum, 'ctx', [(i, i ^ flip * QUAD) for i in range(RING *...  7.73 us
  transfers between devices with their start and end apart: 26, of which 15 were waited for; matrix products, arithmetic and copies ran while one was open for 6% of the time, Pallas kernels for 0%

profile of v1, /device:TPU:40, one launch (start us, length us, event | category | flops | bytes accessed | tf_op | source)
XLA Modules:
  0.0 215.2 jit_solution(14552408715867153642)
XLA Ops:
  2.5 3.3 %collective-permute-start.3 = (bf16[2,128,512]{2,1,0:T(8,128)(2,1)S(1)}, bf16[2,128,512]{2,1,0:T(8,128)(2,1)S(1)}, u32[]{:S(2)}, u32[]{:S(2)}) collective-permute-start(bf16[2,128,512]{2,1,0:T(8,128)(2,1)S(1)} %constant_dynamic-update-slice_fusion.rest_0_), channel_id=1, source_target_pairs={{0,28},{1,29},{2,30},{3,31},{4,0},{5,1},{6,2},{7,3},{8,4},{9,5},{1... | collective-permute-start | bytes 786440 | tf_op jit(solution)/shard_map/ppermute | solution.py:33
  8.3 10.9 %collective-permute-start = (bf16[128,512]{1,0:T(8,128)(2,1)}, bf16[128,512]{1,0:T(8,128)(2,1)S(1)}, u32[]{:S(2)}, u32[]{:S(2)}) collective-permute-start(bf16[128,512]{1,0:T(8,128)(2,1)} %bitcast.32), channel_id=1, source_target_pairs={{0,2},{1,3},{2,0},{3,1},{4,6},{5,7},{6,4},{7,5},{8,10},{9,11},{10,... | collective-permute-start | bytes 393224 | tf_op jit(solution)/shard_map/ppermute | solution.py:45
  20.0 3.3 %collective-permute-start.5 = (bf16[2,128,512]{2,1,0:T(8,128)(2,1)S(1)}, bf16[2,128,512]{2,1,0:T(8,128)(2,1)S(1)}, u32[]{:S(2)}, u32[]{:S(2)}) collective-permute-start(bf16[2,128,512]{2,1,0:T(8,128)(2,1)S(1)} %collective-permute-done.3.rest_2_), channel_id=1, source_target_pairs={{0,28},{1,29},{2,30},{3,31},{4,0},{5,1},{6,2},{7,3},{8,4},{9,5},{1... | collective-permute-start | bytes 786440 | tf_op jit(solution)/shard_map/ppermute | solution.py:33
  30.0 3.3 %collective-permute-start.7 = (bf16[2,128,512]{2,1,0:T(8,128)(2,1)S(1)}, bf16[2,128,512]{2,1,0:T(8,128)(2,1)S(1)}, u32[]{:S(2)}, u32[]{:S(2)}) collective-permute-start(bf16[2,128,512]{2,1,0:T(8,128)(2,1)S(1)} %collective-permute-done.5.rest_4_), channel_id=1, source_target_pairs={{0,28},{1,29},{2,30},{3,31},{4,0},{5,1},{6,2},{7,3},{8,4},{9,5},{1... | collective-permute-start | bytes 786440 | tf_op jit(solution)/shard_map/ppermute | solution.py:33
  40.6 3.6 %collective-permute-start.9 = (bf16[2,64,512]{2,1,0:T(8,128)(2,1)S(1)}, bf16[2,64,512]{2,1,0:T(8,128)(2,1)S(1)}, u32[]{:S(2)}, u32[]{:S(2)}) collective-permute-start(bf16[2,64,512]{2,1,0:T(8,128)(2,1)S(1)} %slice.55), channel_id=1, source_target_pairs={{0,28},{1,29},{2,30},{3,31},{4,0},{5,1},{6,2},{7,3},{8,4},{9,5},{1... | collective-permute-start | bytes 393224 | tf_op jit(solution)/shard_map/ppermute | solution.py:33
  47.5 5.2 %concatenate.23.info = s32[9]{0:T(128)S(1)} concatenate(s32[1]{0:T(128)} %bitcast, s32[1]{0:T(128)} %bitcast.6, s32[1]{0:T(128)} %bitcast.7, s32[1]{0:T(128)} %bitcast.8, s32[1]{0:T(128)} %bitcast.9, s32[1]{0:T(128)} %bitcast.10, s32[1]{0:T(128)} %bitcast.11, s32[1]{0:T(128)} %bitcast.12, s32[1]{0:T(128)} %bitcast.13), dimensions={0} | concatenate | bytes 72 | tf_op jit(solution)/shard_map/concatenate | solution.py:186
  59.3 4.9 %collective-permute-start.11 = (bf16[128,512]{1,0:T(8,128)(2,1)S(1)}, bf16[128,512]{1,0:T(8,128)(2,1)S(1)}, u32[]{:S(2)}, u32[]{:S(2)}) collective-permute-start(bf16[128,512]{1,0:T(8,128)(2,1)S(1)} %slice.79), channel_id=1, source_target_pairs={{0,2},{1,3},{2,0},{3,1},{4,6},{5,7},{6,4},{7,5},{8,10},{9,11},{10,... | collective-permute-start | bytes 393224 | tf_op jit(solution)/shard_map/ppermute | solution.py:45
  64.3 6.5 %collective-permute-done.11.other = bf16[128,512]{1,0:T(8,128)(2,1)S(1)} collective-permute-done((bf16[128,512]{1,0:T(8,128)(2,1)S(1)}, bf16[128,512]{1,0:T(8,128)(2,1)S(1)}, u32[]{:S(2)}, u32[]{:S(2)}) %collective-permute-start.11) | collective-permute-done | bytes 131104 | tf_op jit(solution)/shard_map/ppermute | solution.py:45
  71.6 4.9 %collective-permute-start.12 = (bf16[128,512]{1,0:T(8,128)(2,1)S(1)}, bf16[128,512]{1,0:T(8,128)(2,1)S(1)}, u32[]{:S(2)}, u32[]{:S(2)}) collective-permute-start(bf16[128,512]{1,0:T(8,128)(2,1)S(1)} %get-tuple-element.18), channel_id=1, source_target_pairs={{0,2},{1,3},{2,0},{3,1},{4,6},{5,7},{6,4},{7,5},{8,10},{9,11},{10,... | collective-permute-start | bytes 393224 | tf_op jit(solution)/shard_map/ppermute | solution.py:45
  76.6 5.8 %collective-permute-done.12 = bf16[128,512]{1,0:T(8,128)(2,1)S(1)} collective-permute-done((bf16[128,512]{1,0:T(8,128)(2,1)S(1)}, bf16[128,512]{1,0:T(8,128)(2,1)S(1)}, u32[]{:S(2)}, u32[]{:S(2)}) %collective-permute-start.12) | collective-permute-done | bytes 131104 | tf_op jit(solution)/shard_map/ppermute | solution.py:45
  85.9 7.1 %backward_tile.1 = (f32[256,512]{1,0:T(8,128)S(1)}, bf16[256,512]{1,0:T(8,128)(2,1)S(1)}, bf16[8,2,128,512]{3,2,1,0:T(8,128)(2,1)}) custom-call(s32[9]{0:T(128)S(1)} %concatenate.23.info, s32[512,128]{1,0:T(8,128)S(1)} %broadcast_in_dim.16.qseg, s32[8,128]{1,0:T(8,128)S(1)} %bitcast.30, bf16[512,512]{1,0:T(8,128)(2,1)S(1)} %pad_maximum_fusion.q, ...), custom_call_target="tpu_custom_call" | custom-call | tf_op jit(solution)/shard_map/backward_tile/pallas_call | solution.py:222
  93.0 21.7 %all-to-all-start = ((bf16[8,2,128,512]{3,2,1,0:T(8,128)(2,1)}), bf16[8,2,128,512]{3,2,1,0:T(8,128)(2,1)S(1)}, u32[]{:S(2)}, u32[]{:S(2)}) async-start(bf16[8,2,128,512]{3,2,1,0:T(8,128)(2,1)} %get-tuple-element.21), calls=%async_computation | async-start | bytes 4194304 | tf_op jit(solution)/shard_map/all_to_all | solution.py:240
  119.8 2.7 %collective-permute-start.17 = (f32[1,512]{1,0:T(1,128)S(1)}, f32[1,512]{1,0:T(1,128)S(1)}, u32[]{:S(2)}, u32[]{:S(2)}) collective-permute-start(f32[1,512]{1,0:T(1,128)S(1)} %slice_add_fusion.1), channel_id=1, source_target_pairs={{0,2},{1,3},{2,0},{3,1},{4,6},{5,7},{6,4},{7,5},{8,10},{9,11},{10,... | collective-permute-start | bytes 6152 | tf_op jit(solution)/shard_map/ppermute | solution.py:45
  122.5 6.7 %collective-permute-done.17 = f32[1,512]{1,0:T(1,128)S(1)} collective-permute-done((f32[1,512]{1,0:T(1,128)S(1)}, f32[1,512]{1,0:T(1,128)S(1)}, u32[]{:S(2)}, u32[]{:S(2)}) %collective-permute-start.17) | collective-permute-done | bytes 2080 | tf_op jit(solution)/shard_map/ppermute | solution.py:45
  129.2 3.4 %collective-permute-start.18 = (f32[1,512]{1,0:T(1,128)S(1)}, f32[1,512]{1,0:T(1,128)S(1)}, u32[]{:S(2)}, u32[]{:S(2)}) collective-permute-start(f32[1,512]{1,0:T(1,128)S(1)} %add.139), channel_id=1, source_target_pairs={{0,4},{1,5},{2,6},{3,7},{4,0},{5,1},{6,2},{7,3},{8,12},{9,13},{10,... | collective-permute-start | bytes 6152 | tf_op jit(solution)/shard_map/ppermute | solution.py:257
  132.6 29.2 %collective-permute-done.18 = f32[1,512]{1,0:T(1,128)S(1)} collective-permute-done((f32[1,512]{1,0:T(1,128)S(1)}, f32[1,512]{1,0:T(1,128)S(1)}, u32[]{:S(2)}, u32[]{:S(2)}) %collective-permute-start.18) | collective-permute-done | bytes 2080 | tf_op jit(solution)/shard_map/ppermute | solution.py:257
  164.3 3.9 %collective-permute-done.19 = f32[1,512]{1,0:T(1,128)S(1)} collective-permute-done((f32[1,512]{1,0:T(1,128)S(1)}, f32[1,512]{1,0:T(1,128)S(1)}, u32[]{:S(2)}, u32[]{:S(2)}) %collective-permute-start.19) | collective-permute-done | bytes 2080 | tf_op jit(solution)/shard_map/ppermute | solution.py:257
  170.1 7.5 %collective-permute-done.20 = f32[1,512]{1,0:T(1,128)S(1)} collective-permute-done((f32[1,512]{1,0:T(1,128)S(1)}, f32[1,512]{1,0:T(1,128)S(1)}, u32[]{:S(2)}, u32[]{:S(2)}) %collective-permute-start.20) | collective-permute-done | bytes 2080 | tf_op jit(solution)/shard_map/ppermute | solution.py:257
  179.6 3.4 %collective-permute-done.21 = f32[1,512]{1,0:T(1,128)S(1)} collective-permute-done((f32[1,512]{1,0:T(1,128)S(1)}, f32[1,512]{1,0:T(1,128)S(1)}, u32[]{:S(2)}, u32[]{:S(2)}) %collective-permute-start.21) | collective-permute-done | bytes 2080 | tf_op jit(solution)/shard_map/ppermute | solution.py:265
  183.0 3.9 %collective-permute-start.22 = (f32[1,512]{1,0:T(1,128)S(1)}, f32[1,512]{1,0:T(1,128)S(1)}, u32[]{:S(2)}, u32[]{:S(2)}) collective-permute-start(f32[1,512]{1,0:T(1,128)S(1)} %add.143), channel_id=1, source_target_pairs={{0,64},{32,96},{64,0},{96,32},{128,192},{160,224},{192,128},{224,1... | collective-permute-start | bytes 6152 | tf_op jit(solution)/shard_map/ppermute | solution.py:265
  186.9 3.1 %collective-permute-done.22 = f32[1,512]{1,0:T(1,128)S(1)} collective-permute-done((f32[1,512]{1,0:T(1,128)S(1)}, f32[1,512]{1,0:T(1,128)S(1)}, u32[]{:S(2)}, u32[]{:S(2)}) %collective-permute-start.22) | collective-permute-done | bytes 2080 | tf_op jit(solution)/shard_map/ppermute | solution.py:265
  190.0 3.7 %collective-permute-start.23 = (f32[1,512]{1,0:T(1,128)S(1)}, f32[1,512]{1,0:T(1,128)S(1)}, u32[]{:S(2)}, u32[]{:S(2)}) collective-permute-start(f32[1,512]{1,0:T(1,128)S(1)} %add.144), channel_id=1, source_target_pairs={{0,128},{32,160},{64,192},{96,224},{128,0},{160,32},{192,64},{224,... | collective-permute-start | bytes 6152 | tf_op jit(solution)/shard_map/ppermute | solution.py:265
  195.5 7.0 %collective-permute-start.24 = (f32[1,512]{1,0:T(1,128)S(1)}, f32[1,512]{1,0:T(1,128)S(1)}, u32[]{:S(2)}, u32[]{:S(2)}) collective-permute-start(f32[1,512]{1,0:T(1,128)S(1)} %add.145), channel_id=1, source_target_pairs={{0,256},{32,288},{64,320},{96,352},{128,384},{160,416},{192,448},{... | collective-permute-start | bytes 6152 | tf_op jit(solution)/shard_map/ppermute | solution.py:265
  205.2 8.2 %collective-permute-done.15 = bf16[128,512]{1,0:T(8,128)(2,1)S(1)} collective-permute-done((bf16[128,512]{1,0:T(8,128)(2,1)S(1)}, bf16[128,512]{1,0:T(8,128)(2,1)S(1)}, u32[]{:S(2)}, u32[]{:S(2)}) %collective-permute-start.15) | collective-permute-done | bytes 131104 | tf_op jit(solution)/shard_map/ppermute | solution.py:45
  (72 shorter events, 51.0 us)
Async XLA Ops:
  2.5 17.5 %collective-permute-start.3 = (bf16[2,128,512]{2,1,0:T(8,128)(2,1)S(1)}, bf16[2,128,512]{2,1,0:T(8,128)(2,1)S(1)}, u32[]{:S(2)}, u32[]{:S(2)}) collective-permute-start(bf16[2,128,512]{2,1,0:T(8,128)(2,1)S(1)} %constant_dynamic-update-slice_fusion.rest_0_), channel_id=1, source_target_pairs={{0,28},{1,29},{2,30},{3,31},{4,0},{5,1},{6,2},{7,3},{8,4},{9,5},{1... | collective-permute-start | bytes 786440 | tf_op jit(solution)/shard_map/ppermute | solution.py:33
  5.7 17.5 %collective-permute-start.2 = (bf16[2,128,512]{2,1,0:T(8,128)(2,1)S(1)}, bf16[2,128,512]{2,1,0:T(8,128)(2,1)S(1)}, u32[]{:S(2)}, u32[]{:S(2)}) collective-permute-start(bf16[2,128,512]{2,1,0:T(8,128)(2,1)S(1)} %constant_dynamic-update-slice_fusion.rest_0_), channel_id=1, source_target_pairs={{0,4},{1,5},{2,6},{3,7},{4,8},{5,9},{6,10},{7,11},{8,12},{9,13},{1... | collective-permute-start | bytes 786440 | tf_op jit(solution)/shard_map/ppermute | solution.py:33
  8.3 18.8 %collective-permute-start = (bf16[128,512]{1,0:T(8,128)(2,1)}, bf16[128,512]{1,0:T(8,128)(2,1)S(1)}, u32[]{:S(2)}, u32[]{:S(2)}) collective-permute-start(bf16[128,512]{1,0:T(8,128)(2,1)} %bitcast.32), channel_id=1, source_target_pairs={{0,2},{1,3},{2,0},{3,1},{4,6},{5,7},{6,4},{7,5},{8,10},{9,11},{10,... | collective-permute-start | bytes 393224 | tf_op jit(solution)/shard_map/ppermute | solution.py:45
  20.0 10.0 %collective-permute-start.5 = (bf16[2,128,512]{2,1,0:T(8,128)(2,1)S(1)}, bf16[2,128,512]{2,1,0:T(8,128)(2,1)S(1)}, u32[]{:S(2)}, u32[]{:S(2)}) collective-permute-start(bf16[2,128,512]{2,1,0:T(8,128)(2,1)S(1)} %collective-permute-done.3.rest_2_), channel_id=1, source_target_pairs={{0,28},{1,29},{2,30},{3,31},{4,0},{5,1},{6,2},{7,3},{8,4},{9,5},{1... | collective-permute-start | bytes 786440 | tf_op jit(solution)/shard_map/ppermute | solution.py:33
  23.3 10.0 %collective-permute-start.4 = (bf16[2,128,512]{2,1,0:T(8,128)(2,1)S(1)}, bf16[2,128,512]{2,1,0:T(8,128)(2,1)S(1)}, u32[]{:S(2)}, u32[]{:S(2)}) collective-permute-start(bf16[2,128,512]{2,1,0:T(8,128)(2,1)S(1)} %collective-permute-done.2.rest_1_), channel_id=1, source_target_pairs={{0,4},{1,5},{2,6},{3,7},{4,8},{5,9},{6,10},{7,11},{8,12},{9,13},{1... | collective-permute-start | bytes 786440 | tf_op jit(solution)/shard_map/ppermute | solution.py:33
  28.1 24.5 %collective-permute-start.1 = (bf16[256,512]{1,0:T(8,128)(2,1)S(1)}, bf16[256,512]{1,0:T(8,128)(2,1)S(1)}, u32[]{:S(2)}, u32[]{:S(2)}) collective-permute-start(bf16[256,512]{1,0:T(8,128)(2,1)S(1)} %pad_maximum_fusion.2), channel_id=1, source_target_pairs={{0,1},{1,0},{2,3},{3,2},{4,5},{5,4},{6,7},{7,6},{8,9},{9,8},{10,11... | collective-permute-start | bytes 786440 | tf_op jit(solution)/shard_map/ppermute | solution.py:45
  30.0 10.6 %collective-permute-start.7 = (bf16[2,128,512]{2,1,0:T(8,128)(2,1)S(1)}, bf16[2,128,512]{2,1,0:T(8,128)(2,1)S(1)}, u32[]{:S(2)}, u32[]{:S(2)}) collective-permute-start(bf16[2,128,512]{2,1,0:T(8,128)(2,1)S(1)} %collective-permute-done.5.rest_4_), channel_id=1, source_target_pairs={{0,28},{1,29},{2,30},{3,31},{4,0},{5,1},{6,2},{7,3},{8,4},{9,5},{1... | collective-permute-start | bytes 786440 | tf_op jit(solution)/shard_map/ppermute | solution.py:33
  33.3 11.5 %collective-permute-start.6 = (bf16[2,128,512]{2,1,0:T(8,128)(2,1)S(1)}, bf16[2,128,512]{2,1,0:T(8,128)(2,1)S(1)}, u32[]{:S(2)}, u32[]{:S(2)}) collective-permute-start(bf16[2,128,512]{2,1,0:T(8,128)(2,1)S(1)} %collective-permute-done.4.rest_3_), channel_id=1, source_target_pairs={{0,4},{1,5},{2,6},{3,7},{4,8},{5,9},{6,10},{7,11},{8,12},{9,13},{1... | collective-permute-start | bytes 786440 | tf_op jit(solution)/shard_map/ppermute | solution.py:33
  40.6 12.9 %collective-permute-start.9 = (bf16[2,64,512]{2,1,0:T(8,128)(2,1)S(1)}, bf16[2,64,512]{2,1,0:T(8,128)(2,1)S(1)}, u32[]{:S(2)}, u32[]{:S(2)}) collective-permute-start(bf16[2,64,512]{2,1,0:T(8,128)(2,1)S(1)} %slice.55), channel_id=1, source_target_pairs={{0,28},{1,29},{2,30},{3,31},{4,0},{5,1},{6,2},{7,3},{8,4},{9,5},{1... | collective-permute-start | bytes 393224 | tf_op jit(solution)/shard_map/ppermute | solution.py:33
  44.8 8.8 %collective-permute-start.8 = (bf16[2,64,512]{2,1,0:T(8,128)(2,1)S(1)}, bf16[2,64,512]{2,1,0:T(8,128)(2,1)S(1)}, u32[]{:S(2)}, u32[]{:S(2)}) collective-permute-start(bf16[2,64,512]{2,1,0:T(8,128)(2,1)S(1)} %slice.54), channel_id=1, source_target_pairs={{0,4},{1,5},{2,6},{3,7},{4,8},{5,9},{6,10},{7,11},{8,12},{9,13},{1... | collective-permute-start | bytes 393224 | tf_op jit(solution)/shard_map/ppermute | solution.py:33
  59.3 11.4 %collective-permute-start.11 = (bf16[128,512]{1,0:T(8,128)(2,1)S(1)}, bf16[128,512]{1,0:T(8,128)(2,1)S(1)}, u32[]{:S(2)}, u32[]{:S(2)}) collective-permute-start(bf16[128,512]{1,0:T(8,128)(2,1)S(1)} %slice.79), channel_id=1, source_target_pairs={{0,2},{1,3},{2,0},{3,1},{4,6},{5,7},{6,4},{7,5},{8,10},{9,11},{10,... | collective-permute-start | bytes 393224 | tf_op jit(solution)/shard_map/ppermute | solution.py:45
  71.6 10.8 %collective-permute-start.12 = (bf16[128,512]{1,0:T(8,128)(2,1)S(1)}, bf16[128,512]{1,0:T(8,128)(2,1)S(1)}, u32[]{:S(2)}, u32[]{:S(2)}) collective-permute-start(bf16[128,512]{1,0:T(8,128)(2,1)S(1)} %get-tuple-element.18), channel_id=1, source_target_pairs={{0,2},{1,3},{2,0},{3,1},{4,6},{5,7},{6,4},{7,5},{8,10},{9,11},{10,... | collective-permute-start | bytes 393224 | tf_op jit(solution)/shard_map/ppermute | solution.py:45
  82.4 3.4 %collective-permute-start.13 = (bf16[256,512]{1,0:T(8,128)(2,1)S(1)}, bf16[256,512]{1,0:T(8,128)(2,1)S(1)}, u32[]{:S(2)}, u32[]{:S(2)}) collective-permute-start(bf16[256,512]{1,0:T(8,128)(2,1)S(1)} %pad_maximum_fusion.3), channel_id=1, source_target_pairs={{0,1},{1,0},{2,3},{3,2},{4,5},{5,4},{6,7},{7,6},{8,9},{9,8},{10,11... | collective-permute-start | bytes 786440 | tf_op jit(solution)/shard_map/ppermute | solution.py:45
  93.0 121.1 %all-to-all-start = ((bf16[8,2,128,512]{3,2,1,0:T(8,128)(2,1)}), bf16[8,2,128,512]{3,2,1,0:T(8,128)(2,1)S(1)}, u32[]{:S(2)}, u32[]{:S(2)}) async-start(bf16[8,2,128,512]{3,2,1,0:T(8,128)(2,1)} %get-tuple-element.21), calls=%async_computation | async-start | bytes 4194304 | tf_op jit(solution)/shard_map/all_to_all | solution.py:240
  114.7 87.8 %collective-permute-start.14 = (bf16[256,512]{1,0:T(8,128)(2,1)S(1)}, bf16[256,512]{1,0:T(8,128)(2,1)S(1)}, u32[]{:S(2)}, u32[]{:S(2)}) collective-permute-start(bf16[256,512]{1,0:T(8,128)(2,1)S(1)} %get-tuple-element.20), channel_id=1, source_target_pairs={{0,1},{1,0},{2,3},{3,2},{4,5},{5,4},{6,7},{7,6},{8,9},{9,8},{10,11... | collective-permute-start | bytes 786440 | tf_op jit(solution)/shard_map/ppermute | solution.py:45
  119.8 9.4 %collective-permute-start.17 = (f32[1,512]{1,0:T(1,128)S(1)}, f32[1,512]{1,0:T(1,128)S(1)}, u32[]{:S(2)}, u32[]{:S(2)}) collective-permute-start(f32[1,512]{1,0:T(1,128)S(1)} %slice_add_fusion.1), channel_id=1, source_target_pairs={{0,2},{1,3},{2,0},{3,1},{4,6},{5,7},{6,4},{7,5},{8,10},{9,11},{10,... | collective-permute-start | bytes 6152 | tf_op jit(solution)/shard_map/ppermute | solution.py:45
  129.2 32.6 %collective-permute-start.18 = (f32[1,512]{1,0:T(1,128)S(1)}, f32[1,512]{1,0:T(1,128)S(1)}, u32[]{:S(2)}, u32[]{:S(2)}) collective-permute-start(f32[1,512]{1,0:T(1,128)S(1)} %add.139), channel_id=1, source_target_pairs={{0,4},{1,5},{2,6},{3,7},{4,0},{5,1},{6,2},{7,3},{8,12},{9,13},{10,... | collective-permute-start | bytes 6152 | tf_op jit(solution)/shard_map/ppermute | solution.py:257
  161.8 6.4 %collective-permute-start.19 = (f32[1,512]{1,0:T(1,128)S(1)}, f32[1,512]{1,0:T(1,128)S(1)}, u32[]{:S(2)}, u32[]{:S(2)}) collective-permute-start(f32[1,512]{1,0:T(1,128)S(1)} %add.140), channel_id=1, source_target_pairs={{0,8},{1,9},{2,10},{3,11},{4,12},{5,13},{6,14},{7,15},{8,0},{9,1},... | collective-permute-start | bytes 6152 | tf_op jit(solution)/shard_map/ppermute | solution.py:257
  168.2 9.4 %collective-permute-start.20 = (f32[1,512]{1,0:T(1,128)S(1)}, f32[1,512]{1,0:T(1,128)S(1)}, u32[]{:S(2)}, u32[]{:S(2)}) collective-permute-start(f32[1,512]{1,0:T(1,128)S(1)} %add.141), channel_id=1, source_target_pairs={{0,16},{1,17},{2,18},{3,19},{4,20},{5,21},{6,22},{7,23},{8,24},{9,... | collective-permute-start | bytes 6152 | tf_op jit(solution)/shard_map/ppermute | solution.py:257
  177.5 5.5 %collective-permute-start.21 = (f32[1,512]{1,0:T(1,128)S(1)}, f32[1,512]{1,0:T(1,128)S(1)}, u32[]{:S(2)}, u32[]{:S(2)}) collective-permute-start(f32[1,512]{1,0:T(1,128)S(1)} %add.142), channel_id=1, source_target_pairs={{0,32},{32,0},{64,96},{96,64},{128,160},{160,128},{192,224},{224,1... | collective-permute-start | bytes 6152 | tf_op jit(solution)/shard_map/ppermute | solution.py:265
  183.0 7.0 %collective-permute-start.22 = (f32[1,512]{1,0:T(1,128)S(1)}, f32[1,512]{1,0:T(1,128)S(1)}, u32[]{:S(2)}, u32[]{:S(2)}) collective-permute-start(f32[1,512]{1,0:T(1,128)S(1)} %add.143), channel_id=1, source_target_pairs={{0,64},{32,96},{64,0},{96,32},{128,192},{160,224},{192,128},{224,1... | collective-permute-start | bytes 6152 | tf_op jit(solution)/shard_map/ppermute | solution.py:265
  190.0 5.5 %collective-permute-start.23 = (f32[1,512]{1,0:T(1,128)S(1)}, f32[1,512]{1,0:T(1,128)S(1)}, u32[]{:S(2)}, u32[]{:S(2)}) collective-permute-start(f32[1,512]{1,0:T(1,128)S(1)} %add.144), channel_id=1, source_target_pairs={{0,128},{32,160},{64,192},{96,224},{128,0},{160,32},{192,64},{224,... | collective-permute-start | bytes 6152 | tf_op jit(solution)/shard_map/ppermute | solution.py:265
  195.5 9.1 %collective-permute-start.24 = (f32[1,512]{1,0:T(1,128)S(1)}, f32[1,512]{1,0:T(1,128)S(1)}, u32[]{:S(2)}, u32[]{:S(2)}) collective-permute-start(f32[1,512]{1,0:T(1,128)S(1)} %add.145), channel_id=1, source_target_pairs={{0,256},{32,288},{64,320},{96,352},{128,384},{160,416},{192,448},{... | collective-permute-start | bytes 6152 | tf_op jit(solution)/shard_map/ppermute | solution.py:265
  202.6 10.8 %collective-permute-start.15 = (bf16[128,512]{1,0:T(8,128)(2,1)S(1)}, bf16[128,512]{1,0:T(8,128)(2,1)S(1)}, u32[]{:S(2)}, u32[]{:S(2)}) collective-permute-start(bf16[128,512]{1,0:T(8,128)(2,1)S(1)} %slice.78), channel_id=1, source_target_pairs={{0,2},{1,3},{2,0},{3,1},{4,6},{5,7},{6,4},{7,5},{8,10},{9,11},{10,... | collective-permute-start | bytes 393224 | tf_op jit(solution)/shard_map/ppermute | solution.py:45
  (5 other events, 57.7 us)

commit v2 on v1

v2 whole, which is shorter than its diff:
```python
import math

import jax
import jax.numpy as jnp
from jax import lax
from jax.experimental import pallas as pl
from jax.experimental.pallas import tpu as pltpu
from jax.sharding import PartitionSpec as P

HEADS = 4
HSIZE = 128
HD = 512
ROWS = 128
QUAD = 4
RING = 8
CTX = QUAD * RING
TILE = QUAD * ROWS
HALF = TILE // 2
CUT = ROWS // 2
SCALE = HSIZE ** (-0.5)
CHUNK = 256
CORE, ZHI = 1, 2
NT = (((1,), (1,)), ((), ()))
NN = (((1,), (0,)), ((), ()))
TN = (((0,), (0,)), ((), ()))
VMEM_LIMIT = 16 * 1024 * 1024
BF16, F32 = jnp.bfloat16, jnp.float32
OFFSETS = (0, -1, 1, -2, 2, -3, 3, 4)
QUADS = [[y * QUAD + c for c in range(QUAD)] for y in range(RING)]
RINGS = [[y * QUAD + c for y in range(RING)] for c in range(QUAD)]


def dot(left, right, dims):
    return lax.dot_general(left, right, dims, preferred_element_type=F32)


def along(value, step):
    return lax.ppermute(value, "ctx", [(i, (i + step * QUAD) % CTX) for i in range(CTX)])


def swap(value, flip):
    return lax.ppermute(value, "ctx", [(i, i ^ flip) for i in range(CTX)])


def everywhere(value, axis, groups, size):
    value = jnp.broadcast_to(value, (size,) + value.shape[1:])
    return lax.all_to_all(value, axis, 0, 0, tiled=True, axis_index_groups=groups)


def head(h):
    return slice(h * HSIZE, (h + 1) * HSIZE)


def block_of(kv, r, which):
    if r < RING - 1:
        return kv[r][which]
    return jnp.concatenate([kv[RING - 1][which], kv[RING][which]], axis=0)


def meets(ends, place, block):
    first = (place // QUAD) * QUAD
    return (ends[block, 0] <= ends[first + QUAD - 1, 1]) & (ends[block, 1] >= ends[first, 0])


def key_block(place, offset):
    return lax.rem(place + (offset + RING) * QUAD, CTX)


def pack_kernel(queries, keys, values, kv, twice, sems):
    copies = [
        pltpu.make_async_copy(source.at[0], target, sems.at[i])
        for i, (source, target) in enumerate(
            ((keys, kv.at[0]), (values, kv.at[1]), (queries, twice.at[0]), (queries, twice.at[1]))
        )
    ]
    for copy in copies:
        copy.start()
    for copy in copies:
        copy.wait()


def order_kernel(place, segs, queries, qseg, q):
    for i, flip in enumerate((0, ZHI, CORE, CORE + ZHI)):
        rows = slice(i * ROWS, (i + 1) * ROWS)
        row = segs[pl.ds(place[0] ^ flip, 1), :]
        qseg[rows, :] = jnp.broadcast_to(row, (ROWS, ROWS)).T
        q[rows, :] = queries[lax.rem(place[0], QUAD) ^ flip, 0]


def forward_kernel(place, ends, qseg, segs, q, *rest):
    kv, (keep, send, acc) = rest[: RING + 1], rest[RING + 1 :]
    acc[...] = jnp.zeros_like(acc)
    for r, offset in enumerate(OFFSETS):
        block = key_block(place[0], offset)

        @pl.when(meets(ends, place[0], block))
        def _(r=r, block=block):
            krow = segs[pl.ds(block, 1), :]
            for h in range(HEADS):
                kb = block_of(kv, r, 0)[:, head(h)]
                vb = block_of(kv, r, 1)[:, head(h)]
                for c in range(TILE // CHUNK):
                    rows = slice(c * CHUNK, (c + 1) * CHUNK)
                    half = dot(q[rows, head(h)], kb, NT) * (0.5 * SCALE)
                    silu = half + half * jnp.tanh(half)
                    w = jnp.where(qseg[rows, :] == krow, silu, 0.0).astype(BF16)
                    acc[rows, head(h)] += dot(w, vb, NN)

    keep[...] = acc[:HALF, :]
    send[...] = acc[HALF:, :].astype(BF16)


def norm_kernel(kept, came, gate, grad, gain, out, gate_grad, attn_grad, part):
    g = gain[...]
    att = kept[...] + came[...].astype(F32)
    inv = lax.rsqrt(jnp.mean(att * att, axis=1, keepdims=True) + 1e-06)
    normed = att * inv
    gate_f = gate[0].astype(F32)
    grad_f = grad[0].astype(F32)
    both = grad_f * gate_f
    out[0] = (normed * g * gate_f).astype(BF16)
    gate_grad[0] = (grad_f * normed * g).astype(BF16)
    part[...] = jnp.sum(both * normed, axis=0, keepdims=True)
    ng = both * g
    mean = jnp.mean(normed * ng, axis=1, keepdims=True)
    attn_grad[...] = (inv * (ng - normed * mean)).astype(BF16)


def backward_kernel(place, ends, qseg, segs, q, da, *rest):
    kv, (keep, send, dkv, acc, dk, dv) = rest[: RING + 1], rest[RING + 1 :]
    acc[...] = jnp.zeros_like(acc)
    for r, offset in enumerate(OFFSETS):
        block = key_block(place[0], offset)
        row = pl.multiple_of((block // QUAD) * (2 * ROWS), 2 * ROWS)
        seen = meets(ends, place[0], block)

        @pl.when(seen)
        def _(r=r, block=block, row=row):
            krow = segs[pl.ds(block, 1), :]
            for h in range(HEADS):
                kb = block_of(kv, r, 0)[:, head(h)]
                vb = block_of(kv, r, 1)[:, head(h)]
                for c in range(TILE // CHUNK):
                    rows = slice(c * CHUNK, (c + 1) * CHUNK)
                    qb, db = q[rows, head(h)], da[rows, head(h)]
                    half = dot(qb, kb, NT) * (0.5 * SCALE)
                    vd = dot(db, vb, NT)
                    t = jnp.tanh(half)
                    same = qseg[rows, :] == krow
                    w = jnp.where(same, half + half * t, 0.0).astype(BF16)
                    slope = (0.5 * SCALE) * vd * (1.0 + t) * (1.0 + half * (1.0 - t))
                    slope = jnp.where(same, slope, 0.0).astype(BF16)
                    acc[rows, head(h)] += dot(slope, kb, NN)
                    dk_part = dot(slope, qb, TN)
                    dv_part = dot(w, db, TN)
                    if c == 0:
                        dk[:, head(h)] = dk_part
                        dv[:, head(h)] = dv_part
                    else:
                        dk[:, head(h)] += dk_part
                        dv[:, head(h)] += dv_part
            dkv[pl.ds(row, ROWS), :] = dk[...].astype(BF16)
            dkv[pl.ds(row + ROWS, ROWS), :] = dv[...].astype(BF16)

        @pl.when(jnp.logical_not(seen))
        def _(row=row):
            dkv[pl.ds(row, 2 * ROWS), :] = jnp.zeros((2 * ROWS, HD), BF16)

    keep[...] = acc[:HALF, :]
    send[...] = acc[HALF:, :].astype(BF16)


def call(kernel, name, outs, operands, scalars=0, scratch=(), us=1):
    return pl.pallas_call(
        kernel,
        out_shape=tuple(jax.ShapeDtypeStruct(shape, dtype) for shape, dtype in outs),
        in_specs=[pl.BlockSpec(memory_space=pltpu.SMEM)] * scalars
        + [pl.BlockSpec(memory_space=pltpu.VMEM)] * (len(operands) - scalars),
        out_specs=(pl.BlockSpec(memory_space=pltpu.VMEM),) * len(outs),
        scratch_shapes=[pltpu.VMEM(shape, F32) for shape in scratch],
        compiler_params=pltpu.CompilerParams(vmem_limit_bytes=VMEM_LIMIT),
        cost_estimate=pl.CostEstimate(
            flops=us * 500_000_000, bytes_accessed=us * 1_000_000, transcendentals=0
        ),
        name=name,
    )(*operands)


def after(value, *others):
    return lax.optimization_barrier((value, *others))[0]


def sum_quad(keep, send):
    keep = keep + swap(send, CORE).astype(F32)
    return keep[:ROWS], swap(keep[ROWS:].astype(BF16), ZHI)


def per_device(queries, key_states, value_states, gate_states, out_grad, segment_ids, norm_gain):
    place = lax.axis_index("ctx").astype(jnp.int32)
    rows, tile, half = (1, ROWS, HD), (TILE, HD), (HALF, HD)
    pair = jax.ShapeDtypeStruct((2, ROWS, HD), BF16)
    kv, twice = pl.pallas_call(
        pack_kernel,
        out_shape=(pair, pair),
        in_specs=[pl.BlockSpec(memory_space=pl.ANY)] * 3,
        out_specs=(pl.BlockSpec(memory_space=pltpu.VMEM),) * 2,
        scratch_shapes=[pltpu.SemaphoreType.DMA((4,))],
        compiler_params=pltpu.CompilerParams(vmem_limit_bytes=VMEM_LIMIT),
        name="pack_rows",
    )(queries, key_states, value_states)
    gathered = lax.all_gather(twice, "ctx", axis_index_groups=QUADS)

    up = down = kv
    blocks = [kv]
    for _ in range(2):
        up, down = along(up, 1), along(down, -1)
        blocks += [up, down]
    blocks += [along(up, 1), along(down, -1), along(up[:, :CUT], 2), along(down[:, CUT:], -2)]

    segs = segment_ids.reshape(CTX, ROWS)
    ends = segs[:, :: ROWS - 1]
    qseg, q_tile = call(
        order_kernel,
        "order_rows",
        [((TILE, ROWS), jnp.int32), (tile, BF16)],
        (place[None], segs, gathered),
        1,
    )
    shared = (place[None], ends, qseg, segs, q_tile)

    keep, send = call(
        forward_kernel,
        "forward_tile",
        [(half, F32), (half, BF16)],
        (*shared, *blocks),
        2,
        [tile],
        us=3,
    )
    mine, came = sum_quad(keep, send)
    layer_out, gate_grad, attn_grad, part = call(
        norm_kernel,
        "norm_rows",
        [(rows, BF16), (rows, BF16), ((ROWS, HD), BF16), ((1, HD), F32)],
        (mine, came, gate_states, out_grad, norm_gain[None, :]),
    )
    part = jnp.sum(everywhere(part, "ctx", RINGS, RING), axis=0, keepdims=True)
    grad_tile = jnp.concatenate([attn_grad, swap(attn_grad, ZHI)], axis=0)
    grad_tile = after(grad_tile, part)
    grad_tile = jnp.concatenate([grad_tile, swap(grad_tile, CORE)], axis=0)

    keep, send, dkv = call(
        backward_kernel,
        "backward_tile",
        [(half, F32), (half, BF16), ((RING * 2 * ROWS, HD), BF16)],
        (*shared, grad_tile, *blocks),
        2,
        [tile, (ROWS, HD), (ROWS, HD)],
        us=9,
    )
    dkv_sum = lax.psum_scatter(dkv, "ctx", tiled=True, axis_index_groups=RINGS)
    mine, came = sum_quad(keep, send)
    query_grad = (mine + came.astype(F32)).astype(BF16)

    dp = lax.axis_size("dp")
    part = after(part, query_grad)
    part = jnp.sum(everywhere(part, "ctx", QUADS, QUAD), axis=0, keepdims=True)
    part = jnp.sum(everywhere(part, "dp", None, dp), axis=0)
    gain_grad = part / math.sqrt(dp * CTX * ROWS)

    return (
        layer_out,
        query_grad[None],
        dkv_sum[None, :ROWS],
        dkv_sum[None, ROWS:],
        gate_grad,
        gain_grad,
    )


def solution(mesh):
    rows = P("dp", "ctx", None)
    return jax.shard_map(
        per_device,
        mesh=mesh,
        in_specs=(rows, rows, rows, rows, rows, P("dp", None), P()),
        out_specs=(rows, rows, rows, rows, rows, P()),
        check_vma=False,
    )
```

time: 216 us -> 171 us (0.79)
  the two profiles are of different devices: /device:TPU:40 before, /device:TPU:16 now
where the time goes in v2:
time: 171 us; the launch traced here: 170 us
  starting transfers between devices  58.6 us (34%)
  blocking collectives  46.6 us (27%)
  waiting for transfers between devices  28.6 us (17%)
  between operations  14.4 us (8%)
  Pallas kernels  12.2 us (7%)
  local copies, waits for them, and re-layouts  8.21 us (5%)
    all_to_all x3, blocking collectives, everywhere(): lax.all_to_all(value, axis, 0, 0, tiled=True, axis_index_groups=groups)  46.6 us
    ppermute x6, starting transfers between devices, swap(): return lax.ppermute(value, 'ctx', [(i, i ^ flip) for i in range(CTX)])  31.4 us
    ppermute x8, starting transfers between devices, along(): lax.ppermute(value, 'ctx', [(i, (i + step * QUAD) % CTX) for i in range(C...  27 us
    ppermute x6, waiting for transfers between devices, swap(): return lax.ppermute(value, 'ctx', [(i, i ^ flip) for i in range(CTX)])  17 us
    pallas_call x4, Pallas kernels, call(): pl.pallas_call(kernel, out_shape=tuple((jax.ShapeDtypeStruct(shape, dtype...  10.8 us
    ppermute x8, waiting for transfers between devices, along(): lax.ppermute(value, 'ctx', [(i, (i + step * QUAD) % CTX) for i in range(C...  7.7 us
    unnamed x22, local copies, waits for them, and re-layouts  5.62 us
    all_gather x1, waiting for transfers between devices, per_device(): gathered = lax.all_gather(twice, 'ctx', axis_index_groups=QUADS)  3.8 us
  transfers between devices with their start and end apart: 16, of which 9 were waited for; matrix products, arithmetic and copies ran while one was open for 1% of the time, Pallas kernels for 0%

profile of v2, /device:TPU:16, one launch (start us, length us, event | category | flops | bytes accessed | tf_op | source)
XLA Modules:
  0.0 170.1 jit_solution(10778436554297112124)
XLA Ops:
  11.4 2.4 %collective-permute-start.1 = (bf16[2,128,512]{2,1,0:T(8,128)(2,1)S(1)}, bf16[2,128,512]{2,1,0:T(8,128)(2,1)S(1)}, u32[]{:S(2)}, u32[]{:S(2)}) collective-permute-start(bf16[2,128,512]{2,1,0:T(8,128)(2,1)S(1)} %get-tuple-element.24.rest_0_), channel_id=1, source_target_pairs={{0,28},{1,29},{2,30},{3,31},{4,0},{5,1},{6,2},{7,3},{8,4},{9,5},{1... | collective-permute-start | bytes 786440 | tf_op jit(solution)/shard_map/ppermute | solution.py:38
  13.8 3.5 %collective-permute-start = (bf16[2,128,512]{2,1,0:T(8,128)(2,1)S(1)}, bf16[2,128,512]{2,1,0:T(8,128)(2,1)S(1)}, u32[]{:S(2)}, u32[]{:S(2)}) collective-permute-start(bf16[2,128,512]{2,1,0:T(8,128)(2,1)S(1)} %get-tuple-element.24.rest_0_), channel_id=1, source_target_pairs={{0,4},{1,5},{2,6},{3,7},{4,8},{5,9},{6,10},{7,11},{8,12},{9,13},{1... | collective-permute-start | bytes 786440 | tf_op jit(solution)/shard_map/ppermute | solution.py:38
  17.3 4.1 %collective-permute-done.1.rest_2_ = bf16[2,128,512]{2,1,0:T(8,128)(2,1)S(1)} collective-permute-done((bf16[2,128,512]{2,1,0:T(8,128)(2,1)S(1)}, bf16[2,128,512]{2,1,0:T(8,128)(2,1)S(1)}, u32[]{:S(2)}, u32[]{:S(2)}) %collective-permute-start.1) | collective-permute-done | bytes 262176 | tf_op jit(solution)/shard_map/ppermute | solution.py:38
  21.3 4.4 %collective-permute-start.3 = (bf16[2,128,512]{2,1,0:T(8,128)(2,1)S(1)}, bf16[2,128,512]{2,1,0:T(8,128)(2,1)S(1)}, u32[]{:S(2)}, u32[]{:S(2)}) collective-permute-start(bf16[2,128,512]{2,1,0:T(8,128)(2,1)S(1)} %collective-permute-done.1.rest_2_), channel_id=1, source_target_pairs={{0,28},{1,29},{2,30},{3,31},{4,0},{5,1},{6,2},{7,3},{8,4},{9,5},{1... | collective-permute-start | bytes 786440 | tf_op jit(solution)/shard_map/ppermute | solution.py:38
  25.8 2.1 %collective-permute-start.2 = (bf16[2,128,512]{2,1,0:T(8,128)(2,1)S(1)}, bf16[2,128,512]{2,1,0:T(8,128)(2,1)S(1)}, u32[]{:S(2)}, u32[]{:S(2)}) collective-permute-start(bf16[2,128,512]{2,1,0:T(8,128)(2,1)S(1)} %collective-permute-done.rest_1_), channel_id=1, source_target_pairs={{0,4},{1,5},{2,6},{3,7},{4,8},{5,9},{6,10},{7,11},{8,12},{9,13},{1... | collective-permute-start | bytes 786440 | tf_op jit(solution)/shard_map/ppermute | solution.py:38
  28.0 3.5 %collective-permute-done.3.rest_4_ = bf16[2,128,512]{2,1,0:T(8,128)(2,1)S(1)} collective-permute-done((bf16[2,128,512]{2,1,0:T(8,128)(2,1)S(1)}, bf16[2,128,512]{2,1,0:T(8,128)(2,1)S(1)}, u32[]{:S(2)}, u32[]{:S(2)}) %collective-permute-start.3) | collective-permute-done | bytes 262176 | tf_op jit(solution)/shard_map/ppermute | solution.py:38
  31.4 3.6 %collective-permute-start.5 = (bf16[2,128,512]{2,1,0:T(8,128)(2,1)S(1)}, bf16[2,128,512]{2,1,0:T(8,128)(2,1)S(1)}, u32[]{:S(2)}, u32[]{:S(2)}) collective-permute-start(bf16[2,128,512]{2,1,0:T(8,128)(2,1)S(1)} %collective-permute-done.3.rest_4_), channel_id=1, source_target_pairs={{0,28},{1,29},{2,30},{3,31},{4,0},{5,1},{6,2},{7,3},{8,4},{9,5},{1... | collective-permute-start | bytes 786440 | tf_op jit(solution)/shard_map/ppermute | solution.py:38
  35.1 3.1 %collective-permute-start.4 = (bf16[2,128,512]{2,1,0:T(8,128)(2,1)S(1)}, bf16[2,128,512]{2,1,0:T(8,128)(2,1)S(1)}, u32[]{:S(2)}, u32[]{:S(2)}) collective-permute-start(bf16[2,128,512]{2,1,0:T(8,128)(2,1)S(1)} %collective-permute-done.2.rest_3_), channel_id=1, source_target_pairs={{0,4},{1,5},{2,6},{3,7},{4,8},{5,9},{6,10},{7,11},{8,12},{9,13},{1... | collective-permute-start | bytes 786440 | tf_op jit(solution)/shard_map/ppermute | solution.py:38
  38.3 4.6 %collective-permute-start.7 = (bf16[2,64,512]{2,1,0:T(8,128)(2,1)S(1)}, bf16[2,64,512]{2,1,0:T(8,128)(2,1)S(1)}, u32[]{:S(2)}, u32[]{:S(2)}) collective-permute-start(bf16[2,64,512]{2,1,0:T(8,128)(2,1)S(1)} %slice.39), channel_id=1, source_target_pairs={{0,24},{1,25},{2,26},{3,27},{4,28},{5,29},{6,30},{7,31},{8,0},{9,1... | collective-permute-start | bytes 393224 | tf_op jit(solution)/shard_map/ppermute | solution.py:38
  42.9 3.3 %collective-permute-start.6 = (bf16[2,64,512]{2,1,0:T(8,128)(2,1)S(1)}, bf16[2,64,512]{2,1,0:T(8,128)(2,1)S(1)}, u32[]{:S(2)}, u32[]{:S(2)}) collective-permute-start(bf16[2,64,512]{2,1,0:T(8,128)(2,1)S(1)} %slice.38), channel_id=1, source_target_pairs={{0,8},{1,9},{2,10},{3,11},{4,12},{5,13},{6,14},{7,15},{8,16},{9,17... | collective-permute-start | bytes 393224 | tf_op jit(solution)/shard_map/ppermute | solution.py:38
  47.0 3.8 %all-gather.3.cloned.1.call-done = bf16[8,128,512]{2,1,0:T(8,128)(2,1)} async-done(((bf16[2,128,512]{2,1,0:T(8,128)(2,1)}), bf16[8,128,512]{2,1,0:T(8,128)(2,1)}) %all-gather.3.cloned.1.call-update) | async-done | bytes 1048592 | tf_op jit(solution)/shard_map/all_gather | solution.py:211
  53.0 2.4 %forward_tile.1 = (f32[256,512]{1,0:T(8,128)S(1)}, bf16[256,512]{1,0:T(8,128)(2,1)S(1)}) custom-call(s32[1]{0:T(128)} %bitcast.place, s32[32,2]{1,0:T(8,128)S(1)} %slice.29.ends, s32[512,128]{1,0:T(8,128)S(1)} %get-tuple-element.22.qseg, s32[32,128]{1,0:T(8,128)S(1)} %bitcast.14, bf16[512,512]{1,0:T(8,128)(2,1)S(1)} %get-tuple-element.23.q, ...), custom_call_target="tpu_custom_call" | custom-call | flops 1500000000 | bytes 3000000 | tf_op jit(solution)/shard_map/forward_tile/pallas_call | solution.py:174
  55.4 3.0 %collective-permute-start.8 = (bf16[256,512]{1,0:T(8,128)(2,1)S(1)}, bf16[256,512]{1,0:T(8,128)(2,1)S(1)}, u32[]{:S(2)}, u32[]{:S(2)}) collective-permute-start(bf16[256,512]{1,0:T(8,128)(2,1)S(1)} %get-tuple-element.26), channel_id=1, source_target_pairs={{0,1},{1,0},{2,3},{3,2},{4,5},{5,4},{6,7},{7,6},{8,9},{9,8},{10,11... | collective-permute-start | bytes 786440 | tf_op jit(solution)/shard_map/ppermute | solution.py:42
  59.6 9.7 %collective-permute-start.9 = (bf16[128,512]{1,0:T(8,128)(2,1)S(1)}, bf16[128,512]{1,0:T(8,128)(2,1)S(1)}, u32[]{:S(2)}, u32[]{:S(2)}) collective-permute-start(bf16[128,512]{1,0:T(8,128)(2,1)S(1)} %slice.54), channel_id=1, source_target_pairs={{0,2},{1,3},{2,0},{3,1},{4,6},{5,7},{6,4},{7,5},{8,10},{9,11},{10,... | collective-permute-start | bytes 393224 | tf_op jit(solution)/shard_map/ppermute | solution.py:42
  69.4 3.8 %collective-permute-done.9.came = bf16[128,512]{1,0:T(8,128)(2,1)S(1)} collective-permute-done((bf16[128,512]{1,0:T(8,128)(2,1)S(1)}, bf16[128,512]{1,0:T(8,128)(2,1)S(1)}, u32[]{:S(2)}, u32[]{:S(2)}) %collective-permute-start.9) | collective-permute-done | bytes 131104 | tf_op jit(solution)/shard_map/ppermute | solution.py:42
  74.2 10.3 %collective-permute-start.10 = (bf16[128,512]{1,0:T(8,128)(2,1)S(1)}, bf16[128,512]{1,0:T(8,128)(2,1)S(1)}, u32[]{:S(2)}, u32[]{:S(2)}) collective-permute-start(bf16[128,512]{1,0:T(8,128)(2,1)S(1)} %get-tuple-element.28), channel_id=1, source_target_pairs={{0,2},{1,3},{2,0},{3,1},{4,6},{5,7},{6,4},{7,5},{8,10},{9,11},{10,... | collective-permute-start | bytes 393224 | tf_op jit(solution)/shard_map/ppermute | solution.py:42
  84.5 13.5 %all_to_all.18 = f32[8,1,512]{2,1,0:T(1,128)S(1)} all-to-all(f32[8,1,512]{2,1,0:T(1,128)S(1)} %broadcast_in_dim.37), channel_id=1, replica_groups={{0,4,8,12,16,20,24,28},{1,5,9,13,17,21,25,29},{2,6,10,14,18,22,26,30},{..., dimensions={0} | all-to-all | bytes 32768 | tf_op jit(solution)/shard_map/all_to_all | solution.py:47
  98.0 1.9 %collective-permute-start.11 = (bf16[256,512]{1,0:T(8,128)(2,1)S(1)}, bf16[256,512]{1,0:T(8,128)(2,1)S(1)}, u32[]{:S(2)}, u32[]{:S(2)}) collective-permute-start(bf16[256,512]{1,0:T(8,128)(2,1)S(1)} %pad_maximum_fusion.1), channel_id=1, source_target_pairs={{0,1},{1,0},{2,3},{3,2},{4,5},{5,4},{6,7},{7,6},{8,9},{9,8},{10,11... | collective-permute-start | bytes 786440 | tf_op jit(solution)/shard_map/ppermute | solution.py:42
  102.4 7.4 %backward_tile.1 = (f32[256,512]{1,0:T(8,128)S(1)}, bf16[256,512]{1,0:T(8,128)(2,1)S(1)}, bf16[2048,512]{1,0:T(8,128)(2,1)}) custom-call(s32[1]{0:T(128)} %bitcast.place, s32[32,2]{1,0:T(8,128)S(1)} %slice.29.ends, s32[512,128]{1,0:T(8,128)S(1)} %copy-done.10, s32[32,128]{1,0:T(8,128)S(1)} %bitcast.15, bf16[512,512]{1,0:T(8,128)(2,1)S(1)} %get-tuple-element.23.q, ...), custom_call_target="tpu_custom_call" | custom-call | flops 4499999744 | bytes 9000000 | tf_op jit(solution)/shard_map/backward_tile/pallas_call | solution.py:174
  109.8 4.4 %collective-permute-start.12 = (bf16[256,512]{1,0:T(8,128)(2,1)S(1)}, bf16[256,512]{1,0:T(8,128)(2,1)S(1)}, u32[]{:S(2)}, u32[]{:S(2)}) collective-permute-start(bf16[256,512]{1,0:T(8,128)(2,1)S(1)} %get-tuple-element.32), channel_id=1, source_target_pairs={{0,1},{1,0},{2,3},{3,2},{4,5},{5,4},{6,7},{7,6},{8,9},{9,8},{10,11... | collective-permute-start | bytes 786440 | tf_op jit(solution)/shard_map/ppermute | solution.py:42
  115.5 2.2 %collective-permute-start.13 = (bf16[128,512]{1,0:T(8,128)(2,1)S(1)}, bf16[128,512]{1,0:T(8,128)(2,1)S(1)}, u32[]{:S(2)}, u32[]{:S(2)}) collective-permute-start(bf16[128,512]{1,0:T(8,128)(2,1)S(1)} %slice.53), channel_id=1, source_target_pairs={{0,2},{1,3},{2,0},{3,1},{4,6},{5,7},{6,4},{7,5},{8,10},{9,11},{10,... | collective-permute-start | bytes 393224 | tf_op jit(solution)/shard_map/ppermute | solution.py:42
  117.6 9.4 %collective-permute-done.13 = bf16[128,512]{1,0:T(8,128)(2,1)S(1)} collective-permute-done((bf16[128,512]{1,0:T(8,128)(2,1)S(1)}, bf16[128,512]{1,0:T(8,128)(2,1)S(1)}, u32[]{:S(2)}, u32[]{:S(2)}) %collective-permute-start.13) | collective-permute-done | bytes 131104 | tf_op jit(solution)/shard_map/ppermute | solution.py:42
  127.7 10.0 %all_to_all.19 = f32[4,1,512]{2,1,0:T(1,128)S(1)} all-to-all(f32[4,1,512]{2,1,0:T(1,128)S(1)} %broadcast_in_dim.42), channel_id=1, replica_groups={{0,1,2,3},{4,5,6,7},{8,9,10,11},{12,13,14,15},{16,17,18,19},{20,21,22,2..., dimensions={0} | all-to-all | bytes 16384 | tf_op jit(solution)/shard_map/all_to_all | solution.py:47
  137.8 23.1 %all_to_all.20 = f32[16,1,512]{2,1,0:T(1,128)S(1)} all-to-all(f32[16,1,512]{2,1,0:T(1,128)S(1)} %broadcast_in_dim.43), channel_id=1, replica_groups=mesh['dp'=16,'ctx'=32] {'dp'}, dimensions={0} | all-to-all | bytes 65536 | tf_op jit(solution)/shard_map/all_to_all | solution.py:47
  (59 shorter events, 16.2 us)
Async XLA Ops:
  7.2 43.7 %all-gather.3.cloned.1.call-start = ((), (), s32[]{:S(2)}) async-start(), calls=%async_computation.5 | async-start | bytes 1310720 | tf_op jit(solution)/shard_map/all_gather | solution.py:211
  7.2 0.9 copy-start
  9.9 43.0 %copy-start.4 = (s32[1,4096]{1,0:T(1,128)S(1)}, s32[1,4096]{1,0:T(1,128)}, u32[]{:S(2)}) copy-start(s32[1,4096]{1,0:T(1,128)} %param.12) | copy-start | bytes 49156
  11.3 150.2 %reduce-scatter.2.cloned.1.call-start = ((), (), s32[]{:S(2)}) async-start(), calls=%async_computation.4 | async-start | bytes 2359296 | tf_op jit(solution)/shard_map/reduce_scatter | solution.py:261
  11.4 9.9 %collective-permute-start.1 = (bf16[2,128,512]{2,1,0:T(8,128)(2,1)S(1)}, bf16[2,128,512]{2,1,0:T(8,128)(2,1)S(1)}, u32[]{:S(2)}, u32[]{:S(2)}) collective-permute-start(bf16[2,128,512]{2,1,0:T(8,128)(2,1)S(1)} %get-tuple-element.24.rest_0_), channel_id=1, source_target_pairs={{0,28},{1,29},{2,30},{3,31},{4,0},{5,1},{6,2},{7,3},{8,4},{9,5},{1... | collective-permute-start | bytes 786440 | tf_op jit(solution)/shard_map/ppermute | solution.py:38
  13.8 12.1 %collective-permute-start = (bf16[2,128,512]{2,1,0:T(8,128)(2,1)S(1)}, bf16[2,128,512]{2,1,0:T(8,128)(2,1)S(1)}, u32[]{:S(2)}, u32[]{:S(2)}) collective-permute-start(bf16[2,128,512]{2,1,0:T(8,128)(2,1)S(1)} %get-tuple-element.24.rest_0_), channel_id=1, source_target_pairs={{0,4},{1,5},{2,6},{3,7},{4,8},{5,9},{6,10},{7,11},{8,12},{9,13},{1... | collective-permute-start | bytes 786440 | tf_op jit(solution)/shard_map/ppermute | solution.py:38
  21.3 10.1 %collective-permute-start.3 = (bf16[2,128,512]{2,1,0:T(8,128)(2,1)S(1)}, bf16[2,128,512]{2,1,0:T(8,128)(2,1)S(1)}, u32[]{:S(2)}, u32[]{:S(2)}) collective-permute-start(bf16[2,128,512]{2,1,0:T(8,128)(2,1)S(1)} %collective-permute-done.1.rest_2_), channel_id=1, source_target_pairs={{0,28},{1,29},{2,30},{3,31},{4,0},{5,1},{6,2},{7,3},{8,4},{9,5},{1... | collective-permute-start | bytes 786440 | tf_op jit(solution)/shard_map/ppermute | solution.py:38
  25.8 9.3 %collective-permute-start.2 = (bf16[2,128,512]{2,1,0:T(8,128)(2,1)S(1)}, bf16[2,128,512]{2,1,0:T(8,128)(2,1)S(1)}, u32[]{:S(2)}, u32[]{:S(2)}) collective-permute-start(bf16[2,128,512]{2,1,0:T(8,128)(2,1)S(1)} %collective-permute-done.rest_1_), channel_id=1, source_target_pairs={{0,4},{1,5},{2,6},{3,7},{4,8},{5,9},{6,10},{7,11},{8,12},{9,13},{1... | collective-permute-start | bytes 786440 | tf_op jit(solution)/shard_map/ppermute | solution.py:38
  31.4 21.5 %collective-permute-start.5 = (bf16[2,128,512]{2,1,0:T(8,128)(2,1)S(1)}, bf16[2,128,512]{2,1,0:T(8,128)(2,1)S(1)}, u32[]{:S(2)}, u32[]{:S(2)}) collective-permute-start(bf16[2,128,512]{2,1,0:T(8,128)(2,1)S(1)} %collective-permute-done.3.rest_4_), channel_id=1, source_target_pairs={{0,28},{1,29},{2,30},{3,31},{4,0},{5,1},{6,2},{7,3},{8,4},{9,5},{1... | collective-permute-start | bytes 786440 | tf_op jit(solution)/shard_map/ppermute | solution.py:38
  35.1 17.9 %collective-permute-start.4 = (bf16[2,128,512]{2,1,0:T(8,128)(2,1)S(1)}, bf16[2,128,512]{2,1,0:T(8,128)(2,1)S(1)}, u32[]{:S(2)}, u32[]{:S(2)}) collective-permute-start(bf16[2,128,512]{2,1,0:T(8,128)(2,1)S(1)} %collective-permute-done.2.rest_3_), channel_id=1, source_target_pairs={{0,4},{1,5},{2,6},{3,7},{4,8},{5,9},{6,10},{7,11},{8,12},{9,13},{1... | collective-permute-start | bytes 786440 | tf_op jit(solution)/shard_map/ppermute | solution.py:38
  38.3 14.7 %collective-permute-start.7 = (bf16[2,64,512]{2,1,0:T(8,128)(2,1)S(1)}, bf16[2,64,512]{2,1,0:T(8,128)(2,1)S(1)}, u32[]{:S(2)}, u32[]{:S(2)}) collective-permute-start(bf16[2,64,512]{2,1,0:T(8,128)(2,1)S(1)} %slice.39), channel_id=1, source_target_pairs={{0,24},{1,25},{2,26},{3,27},{4,28},{5,29},{6,30},{7,31},{8,0},{9,1... | collective-permute-start | bytes 393224 | tf_op jit(solution)/shard_map/ppermute | solution.py:38
  42.9 10.0 %collective-permute-start.6 = (bf16[2,64,512]{2,1,0:T(8,128)(2,1)S(1)}, bf16[2,64,512]{2,1,0:T(8,128)(2,1)S(1)}, u32[]{:S(2)}, u32[]{:S(2)}) collective-permute-start(bf16[2,64,512]{2,1,0:T(8,128)(2,1)S(1)} %slice.38), channel_id=1, source_target_pairs={{0,8},{1,9},{2,10},{3,11},{4,12},{5,13},{6,14},{7,15},{8,16},{9,17... | collective-permute-start | bytes 393224 | tf_op jit(solution)/shard_map/ppermute | solution.py:38
  51.6 1.2 copy-start.5
  52.9 2.5 %copy-start.9 = (s32[512,128]{1,0:T(8,128)}, s32[512,128]{1,0:T(8,128)S(1)}, u32[]{:S(2)}) copy-start(s32[512,128]{1,0:T(8,128)S(1)} %get-tuple-element.22.qseg) | copy-start | bytes 786436
  55.4 17.8 %copy-start.6 = (bf16[1,128,512]{2,1,0:T(8,128)(2,1)S(1)}, bf16[1,128,512]{2,1,0:T(8,128)(2,1)}, u32[]{:S(2)}) copy-start(bf16[1,128,512]{2,1,0:T(8,128)(2,1)} %gate.1) | copy-start | bytes 393220
  55.4 17.8 %copy-start.7 = (bf16[1,128,512]{2,1,0:T(8,128)(2,1)S(1)}, bf16[1,128,512]{2,1,0:T(8,128)(2,1)}, u32[]{:S(2)}) copy-start(bf16[1,128,512]{2,1,0:T(8,128)(2,1)} %grad.1) | copy-start | bytes 393220
  55.4 17.8 %copy-start.8 = (f32[512]{0:T(512)S(1)}, f32[512]{0:T(512)}, u32[]{:S(2)}) copy-start(f32[512]{0:T(512)} %param.13) | copy-start | bytes 6148
  55.4 4.1 %collective-permute-start.8 = (bf16[256,512]{1,0:T(8,128)(2,1)S(1)}, bf16[256,512]{1,0:T(8,128)(2,1)S(1)}, u32[]{:S(2)}, u32[]{:S(2)}) collective-permute-start(bf16[256,512]{1,0:T(8,128)(2,1)S(1)} %get-tuple-element.26), channel_id=1, source_target_pairs={{0,1},{1,0},{2,3},{3,2},{4,5},{5,4},{6,7},{7,6},{8,9},{9,8},{10,11... | collective-permute-start | bytes 786440 | tf_op jit(solution)/shard_map/ppermute | solution.py:42
  59.6 13.6 %collective-permute-start.9 = (bf16[128,512]{1,0:T(8,128)(2,1)S(1)}, bf16[128,512]{1,0:T(8,128)(2,1)S(1)}, u32[]{:S(2)}, u32[]{:S(2)}) collective-permute-start(bf16[128,512]{1,0:T(8,128)(2,1)S(1)} %slice.54), channel_id=1, source_target_pairs={{0,2},{1,3},{2,0},{3,1},{4,6},{5,7},{6,4},{7,5},{8,10},{9,11},{10,... | collective-permute-start | bytes 393224 | tf_op jit(solution)/shard_map/ppermute | solution.py:42
  74.2 23.8 %collective-permute-start.10 = (bf16[128,512]{1,0:T(8,128)(2,1)S(1)}, bf16[128,512]{1,0:T(8,128)(2,1)S(1)}, u32[]{:S(2)}, u32[]{:S(2)}) collective-permute-start(bf16[128,512]{1,0:T(8,128)(2,1)S(1)} %get-tuple-element.28), channel_id=1, source_target_pairs={{0,2},{1,3},{2,0},{3,1},{4,6},{5,7},{6,4},{7,5},{8,10},{9,11},{10,... | collective-permute-start | bytes 393224 | tf_op jit(solution)/shard_map/ppermute | solution.py:42
  98.0 3.4 %collective-permute-start.11 = (bf16[256,512]{1,0:T(8,128)(2,1)S(1)}, bf16[256,512]{1,0:T(8,128)(2,1)S(1)}, u32[]{:S(2)}, u32[]{:S(2)}) collective-permute-start(bf16[256,512]{1,0:T(8,128)(2,1)S(1)} %pad_maximum_fusion.1), channel_id=1, source_target_pairs={{0,1},{1,0},{2,3},{3,2},{4,5},{5,4},{6,7},{7,6},{8,9},{9,8},{10,11... | collective-permute-start | bytes 786440 | tf_op jit(solution)/shard_map/ppermute | solution.py:42
  101.5 1.0 copy-start.10
  109.8 5.5 %collective-permute-start.12 = (bf16[256,512]{1,0:T(8,128)(2,1)S(1)}, bf16[256,512]{1,0:T(8,128)(2,1)S(1)}, u32[]{:S(2)}, u32[]{:S(2)}) collective-permute-start(bf16[256,512]{1,0:T(8,128)(2,1)S(1)} %get-tuple-element.32), channel_id=1, source_target_pairs={{0,1},{1,0},{2,3},{3,2},{4,5},{5,4},{6,7},{7,6},{8,9},{9,8},{10,11... | collective-permute-start | bytes 786440 | tf_op jit(solution)/shard_map/ppermute | solution.py:42
  115.5 11.6 %collective-permute-start.13 = (bf16[128,512]{1,0:T(8,128)(2,1)S(1)}, bf16[128,512]{1,0:T(8,128)(2,1)S(1)}, u32[]{:S(2)}, u32[]{:S(2)}) collective-permute-start(bf16[128,512]{1,0:T(8,128)(2,1)S(1)} %slice.53), channel_id=1, source_target_pairs={{0,2},{1,3},{2,0},{3,1},{4,6},{5,7},{6,4},{7,5},{8,10},{9,11},{10,... | collective-permute-start | bytes 393224 | tf_op jit(solution)/shard_map/ppermute | solution.py:42
  (3 other events, 2.5 us)
Sparse Core Ops, SparseCore 0:
  11.5 39.3 all-gather.2
  110.0 49.2 reduce-scatter.1

commit v3 on v2

v3 whole, which is shorter than its diff:
```python
import math

import jax
import jax.numpy as jnp
from jax import lax
from jax.experimental import pallas as pl
from jax.experimental.pallas import tpu as pltpu
from jax.sharding import PartitionSpec as P

HEADS = 4
HSIZE = 128
HD = 512
ROWS = 128
QUAD = 4
RING = 8
CTX = QUAD * RING
TILE = QUAD * ROWS
HALF = TILE // 2
CUT = ROWS // 2
SCALE = HSIZE ** (-0.5)
CHUNK = 256
CORE, ZHI = 1, 2
NT = (((1,), (1,)), ((), ()))
NN = (((1,), (0,)), ((), ()))
TN = (((0,), (0,)), ((), ()))
VMEM_LIMIT = 16 * 1024 * 1024
BF16, F32 = jnp.bfloat16, jnp.float32
EXTRA = 16
PAIRS = (((0, 0), (-1, 1)), ((1, 2), (2, 4)), ((-2, 3), (-3, 5)), ((3, 6), (4, 7)))
QUADS = [[y * QUAD + c for c in range(QUAD)] for y in range(RING)]
ZPAIRS = [[y * QUAD + z * ZHI + c for z in range(2)] for y in range(RING) for c in range(2)]
RINGS = [[y * QUAD + c for y in range(RING)] for c in range(QUAD)]


def dot(left, right, dims):
    return lax.dot_general(left, right, dims, preferred_element_type=F32)


def along(value, step):
    return lax.ppermute(value, "ctx", [(i, (i + step * QUAD) % CTX) for i in range(CTX)])


def swap(value, flip):
    return lax.ppermute(value, "ctx", [(i, i ^ flip) for i in range(CTX)])


def everywhere(value, axis, groups, size):
    value = jnp.broadcast_to(value, (size,) + value.shape[1:])
    return lax.all_to_all(value, axis, 0, 0, tiled=True, axis_index_groups=groups)


def head(h):
    return slice(h * HSIZE, (h + 1) * HSIZE)


def pair_of(kv, pair, which, h):
    parts = []
    for _, at in PAIRS[pair]:
        for ref in kv[at:] if at == RING - 1 else kv[at : at + 1]:
            parts.append(ref[which, :, head(h)])
    return jnp.concatenate(parts, axis=0)


def key_blocks(place, pair):
    return [lax.rem(place + (offset + RING) * QUAD, CTX) for offset, _ in PAIRS[pair]]


def meets(ends, place, c, blocks):
    first = (place // QUAD) * QUAD + c * (CHUNK // ROWS)
    low, high = ends[first, 0], ends[first + CHUNK // ROWS - 1, 1]
    hits = [(ends[block, 0] <= high) & (ends[block, 1] >= low) for block in blocks]
    return hits[0] | hits[1]


def same_history(qseg, segs, rows, blocks):
    krow = jnp.concatenate([segs[pl.ds(block, 1), :] for block in blocks], axis=1)
    return jnp.concatenate([qseg[rows, :]] * 2, axis=1) == krow


def rows_of(place, flip):
    quad = lax.rem(place, QUAD) ^ flip
    return pl.ds(pl.multiple_of(quad * ROWS, ROWS), ROWS)


def share_out(place, acc, keep, send):
    for i, flip in enumerate((0, ZHI)):
        rows = slice(i * ROWS, (i + 1) * ROWS)
        keep[rows, :] = acc[rows_of(place, flip), :]
        send[rows, :] = acc[rows_of(place, flip ^ CORE), :].astype(BF16)


def segment_kernel(place, segs, qseg):
    first = (place[0] // QUAD) * QUAD
    for i in range(QUAD):
        row = segs[pl.ds(first + i, 1), :]
        qseg[i * ROWS : (i + 1) * ROWS, :] = jnp.broadcast_to(row, (ROWS, ROWS)).T


def queries_of(q, c, h):
    return q[2 * c : 2 * c + 2, 0, :, head(h)].reshape(CHUNK, HSIZE)


def forward_kernel(place, ends, qseg, segs, q, *rest):
    kv, (keep, send, acc) = rest[: RING + 1], rest[RING + 1 :]
    acc[...] = jnp.zeros_like(acc)
    for pair in range(len(PAIRS)):
        blocks = key_blocks(place[0], pair)
        for c in range(TILE // CHUNK):

            @pl.when(meets(ends, place[0], c, blocks))
            def _(pair=pair, blocks=blocks, c=c):
                rows = slice(c * CHUNK, (c + 1) * CHUNK)
                same = same_history(qseg, segs, rows, blocks)
                for h in range(HEADS):
                    keys, values = pair_of(kv, pair, 0, h), pair_of(kv, pair, 1, h)
                    half = dot(queries_of(q, c, h), keys, NT) * (0.5 * SCALE)
                    silu = half + half * jnp.tanh(half)
                    w = jnp.where(same, silu, 0.0).astype(BF16)
                    acc[rows, head(h)] += dot(w, values, NN)

    share_out(place[0], acc, keep, send)


def norm_kernel(place, kept, came, gate, grad, gain, out, gate_grad, attn_grad):
    g = gain[...]
    att = kept[...] + came[1 - lax.rem(place[0], QUAD) // ZHI].astype(F32)
    inv = lax.rsqrt(jnp.mean(att * att, axis=1, keepdims=True) + 1e-06)
    normed = att * inv
    gate_f = gate[0].astype(F32)
    grad_f = grad[0].astype(F32)
    both = grad_f * gate_f
    out[0] = (normed * g * gate_f).astype(BF16)
    gate_grad[0] = (grad_f * normed * g).astype(BF16)
    ng = both * g
    mean = jnp.mean(normed * ng, axis=1, keepdims=True)
    attn_grad[:ROWS, :] = (inv * (ng - normed * mean)).astype(BF16)
    part = jnp.sum(both * normed, axis=0, keepdims=True)
    high = part.astype(BF16).astype(F32)
    line = lax.broadcasted_iota(jnp.int32, (EXTRA, HD), 0)
    extra = jnp.where(line == 0, high, jnp.where(line == 1, part - high, 0.0))
    attn_grad[ROWS:, :] = extra.astype(BF16)


def backward_kernel(place, ends, qseg, segs, q, da, *rest):
    kv, (keep, send, part, dkv, acc, dk, dv) = rest[: RING + 1], rest[RING + 1 :]
    acc[...] = jnp.zeros_like(acc)
    extra = [da[i, ROWS:, :].astype(F32) for i in range(QUAD)]
    terms = [rows[0:1] + rows[1:2] for rows in extra]
    part[...] = (terms[0] + terms[1]) + (terms[2] + terms[3])
    for pair in range(len(PAIRS)):
        blocks = key_blocks(place[0], pair)
        dk[...] = jnp.zeros_like(dk)
        dv[...] = jnp.zeros_like(dv)
        for c in range(TILE // CHUNK):

            @pl.when(meets(ends, place[0], c, blocks))
            def _(pair=pair, blocks=blocks, c=c):
                rows = slice(c * CHUNK, (c + 1) * CHUNK)
                same = same_history(qseg, segs, rows, blocks)
                for h in range(HEADS):
                    keys, values = pair_of(kv, pair, 0, h), pair_of(kv, pair, 1, h)
                    qb = queries_of(q, c, h)
                    db = da[2 * c : 2 * c + 2, :ROWS, head(h)].reshape(CHUNK, HSIZE)
                    half = dot(qb, keys, NT) * (0.5 * SCALE)
                    vd = dot(db, values, NT)
                    t = jnp.tanh(half)
                    w = jnp.where(same, half + half * t, 0.0).astype(BF16)
                    slope = (0.5 * SCALE) * vd * (1.0 + t) * (1.0 + half * (1.0 - t))
                    slope = jnp.where(same, slope, 0.0).astype(BF16)
                    acc[rows, head(h)] += dot(slope, keys, NN)
                    dk[:, head(h)] += dot(slope, qb, TN)
                    dv[:, head(h)] += dot(w, db, TN)

        for i, block in enumerate(blocks):
            rows = slice(i * ROWS, (i + 1) * ROWS)
            at = pl.multiple_of((block // QUAD) * (2 * ROWS), 2 * ROWS)
            dkv[pl.ds(at, ROWS), :] = dk[rows, :].astype(BF16)
            dkv[pl.ds(at + ROWS, ROWS), :] = dv[rows, :].astype(BF16)

    share_out(place[0], acc, keep, send)


def call(kernel, name, outs, operands, scalars=0, scratch=(), us=1):
    return pl.pallas_call(
        kernel,
        out_shape=tuple(jax.ShapeDtypeStruct(shape, dtype) for shape, dtype in outs),
        in_specs=[pl.BlockSpec(memory_space=pltpu.SMEM)] * scalars
        + [pl.BlockSpec(memory_space=pltpu.VMEM)] * (len(operands) - scalars),
        out_specs=(pl.BlockSpec(memory_space=pltpu.VMEM),) * len(outs),
        scratch_shapes=[pltpu.VMEM(shape, F32) for shape in scratch],
        compiler_params=pltpu.CompilerParams(vmem_limit_bytes=VMEM_LIMIT),
        cost_estimate=pl.CostEstimate(
            flops=us * 500_000_000, bytes_accessed=us * 1_000_000, transcendentals=0
        ),
        name=name,
    )(*operands)


def after(value, *others):
    return lax.optimization_barrier((value, *others))[0]


def sum_quad(keep, send):
    keep = keep + swap(send, CORE).astype(F32)
    return keep[:ROWS], lax.all_gather(keep[ROWS:].astype(BF16), "ctx", axis_index_groups=ZPAIRS)


def per_device(queries, key_states, value_states, gate_states, out_grad, segment_ids, norm_gain):
    place = lax.axis_index("ctx").astype(jnp.int32)
    rows, tile, half = (1, ROWS, HD), (TILE, HD), (HALF, HD)
    kv = jnp.concatenate([key_states, value_states], axis=0)
    first, kv = lax.optimization_barrier((queries, kv))
    gathered = lax.all_gather(
        jnp.pad(first, ((0, 1), (0, 0), (0, 0))), "ctx", axis_index_groups=QUADS
    )

    up = down = kv
    blocks = [kv]
    for _ in range(2):
        up, down = along(up, 1), along(down, -1)
        blocks += [up, down]
    blocks += [along(up, 1), along(down, -1), along(up[:, :CUT], 2), along(down[:, CUT:], -2)]

    segs = segment_ids.reshape(CTX, ROWS)
    ends = segs[:, :: ROWS - 1]
    (qseg,) = call(
        segment_kernel, "query_segments", [((TILE, ROWS), jnp.int32)], (place[None], segs), 1
    )
    shared = (place[None], ends, qseg, segs, gathered)

    keep, send = call(
        forward_kernel,
        "forward_tile",
        [(half, F32), (half, BF16)],
        (*shared, *blocks),
        2,
        [tile],
        us=3,
    )
    mine, came = sum_quad(keep, send)
    layer_out, gate_grad, attn_grad = call(
        norm_kernel,
        "norm_rows",
        [(rows, BF16), (rows, BF16), ((ROWS + EXTRA, HD), BF16)],
        (place[None], mine, came, gate_states, out_grad, norm_gain[None, :]),
        1,
    )
    grads = lax.all_gather(attn_grad, "ctx", axis_index_groups=QUADS)

    keep, send, part, dkv = call(
        backward_kernel,
        "backward_tile",
        [(half, F32), (half, BF16), ((1, HD), F32), ((RING * 2 * ROWS, HD), BF16)],
        (*shared, grads, *blocks),
        2,
        [tile, half, half],
        us=9,
    )
    dkv_sum = lax.psum_scatter(dkv, "ctx", tiled=True, axis_index_groups=RINGS)
    mine, came = sum_quad(keep, send)
    came = lax.dynamic_index_in_dim(came, 1 - lax.rem(place, QUAD) // ZHI, 0, keepdims=False)
    query_grad = (mine + came.astype(F32)).astype(BF16)

    dp = lax.axis_size("dp")
    part = after(part, query_grad)
    part = jnp.sum(everywhere(part, "dp", None, dp), axis=0, keepdims=True)
    part = jnp.sum(everywhere(part, "ctx", RINGS, RING), axis=0)
    gain_grad = part / math.sqrt(dp * CTX * ROWS)

    return (
        layer_out,
        query_grad[None],
        dkv_sum[None, :ROWS],
        dkv_sum[None, ROWS:],
        gate_grad,
        gain_grad,
    )


def solution(mesh):
    rows = P("dp", "ctx", None)
    return jax.shard_map(
        per_device,
        mesh=mesh,
        in_specs=(rows, rows, rows, rows, rows, P("dp", None), P()),
        out_specs=(rows, rows, rows, rows, rows, P()),
        check_vma=False,
    )
```

time: 171 us -> 159 us (0.930)
  the two profiles are of different devices: /device:TPU:16 before, /device:TPU:4 now
where the time goes in v3:
time: 159 us; the launch traced here: 158 us
  blocking collectives  69.9 us (44%)
  starting transfers between devices  33.7 us (21%)
  waiting for transfers between devices  17.1 us (11%)
  Pallas kernels  14.4 us (9%)
  between operations  14.3 us (9%)
  local copies, waits for them, and re-layouts  6.18 us (4%)
  other arithmetic  2.47 us (2%)
    all_to_all x2, blocking collectives, everywhere(): lax.all_to_all(value, axis, 0, 0, tiled=True, axis_index_groups=groups)  31.3 us
    ppermute x8, starting transfers between devices, along(): lax.ppermute(value, 'ctx', [(i, (i + step * QUAD) % CTX) for i in range(C...  29.3 us
    all_gather x2, blocking collectives, sum_quad(): lax.all_gather(keep[ROWS:].astype(BF16), 'ctx', axis_index_groups=ZPAIRS)  25.4 us
    pallas_call x4, Pallas kernels, call(): pl.pallas_call(kernel, out_shape=tuple((jax.ShapeDtypeStruct(shape, dtype...  14.4 us
    all_gather x1, blocking collectives, per_device(): grads = lax.all_gather(attn_grad, 'ctx', axis_index_groups=QUADS)  13.2 us
    ppermute x8, waiting for transfers between devices, along(): lax.ppermute(value, 'ctx', [(i, (i + step * QUAD) % CTX) for i in range(C...  11.8 us
    ppermute x2, starting transfers between devices, swap(): return lax.ppermute(value, 'ctx', [(i, i ^ flip) for i in range(CTX)])  4.3 us
  transfers between devices with their start and end apart: 12, of which 6 were waited for; matrix products, arithmetic and copies ran while one was open for 1% of the time, Pallas kernels for 0%

profile of v3, /device:TPU:4, one launch (start us, length us, event | category | flops | bytes accessed | tf_op | source)
XLA Modules:
  0.0 158.1 jit_solution(3068413854543768595)
XLA Ops:
  8.2 1.6 %pad.4 = bf16[2,128,512]{2,1,0:T(8,128)(2,1)} pad(bf16[1,128,512]{2,1,0:T(8,128)(2,1)} %param.7, bf16[]{:T(256)} %constant.29.clone.1), padding=0_1x0_0x0_0 | pad | bytes 393218 | tf_op jit(solution)/shard_map/jit(_pad)/pad | solution.py:214
  9.9 3.5 %collective-permute-start = (bf16[2,128,512]{2,1,0:T(8,128)(2,1)S(1)}, bf16[2,128,512]{2,1,0:T(8,128)(2,1)S(1)}, u32[]{:S(2)}, u32[]{:S(2)}) collective-permute-start(bf16[2,128,512]{2,1,0:T(8,128)(2,1)S(1)} %pad_maximum_fusion.rest_0_), channel_id=1, source_target_pairs={{0,4},{1,5},{2,6},{3,7},{4,8},{5,9},{6,10},{7,11},{8,12},{9,13},{1... | collective-permute-start | bytes 786440 | tf_op jit(solution)/shard_map/ppermute | solution.py:40
  13.4 3.8 %collective-permute-start.1 = (bf16[2,128,512]{2,1,0:T(8,128)(2,1)S(1)}, bf16[2,128,512]{2,1,0:T(8,128)(2,1)S(1)}, u32[]{:S(2)}, u32[]{:S(2)}) collective-permute-start(bf16[2,128,512]{2,1,0:T(8,128)(2,1)S(1)} %pad_maximum_fusion.rest_0_), channel_id=1, source_target_pairs={{0,28},{1,29},{2,30},{3,31},{4,0},{5,1},{6,2},{7,3},{8,4},{9,5},{1... | collective-permute-start | bytes 786440 | tf_op jit(solution)/shard_map/ppermute | solution.py:40
  17.2 4.4 %collective-permute-done.rest_1_ = bf16[2,128,512]{2,1,0:T(8,128)(2,1)S(1)} collective-permute-done((bf16[2,128,512]{2,1,0:T(8,128)(2,1)S(1)}, bf16[2,128,512]{2,1,0:T(8,128)(2,1)S(1)}, u32[]{:S(2)}, u32[]{:S(2)}) %collective-permute-start) | collective-permute-done | bytes 262176 | tf_op jit(solution)/shard_map/ppermute | solution.py:40
  21.6 1.9 %collective-permute-start.2 = (bf16[2,128,512]{2,1,0:T(8,128)(2,1)S(1)}, bf16[2,128,512]{2,1,0:T(8,128)(2,1)S(1)}, u32[]{:S(2)}, u32[]{:S(2)}) collective-permute-start(bf16[2,128,512]{2,1,0:T(8,128)(2,1)S(1)} %collective-permute-done.rest_1_), channel_id=1, source_target_pairs={{0,4},{1,5},{2,6},{3,7},{4,8},{5,9},{6,10},{7,11},{8,12},{9,13},{1... | collective-permute-start | bytes 786440 | tf_op jit(solution)/shard_map/ppermute | solution.py:40
  23.5 5.1 %collective-permute-start.3 = (bf16[2,128,512]{2,1,0:T(8,128)(2,1)S(1)}, bf16[2,128,512]{2,1,0:T(8,128)(2,1)S(1)}, u32[]{:S(2)}, u32[]{:S(2)}) collective-permute-start(bf16[2,128,512]{2,1,0:T(8,128)(2,1)S(1)} %collective-permute-done.1.rest_2_), channel_id=1, source_target_pairs={{0,28},{1,29},{2,30},{3,31},{4,0},{5,1},{6,2},{7,3},{8,4},{9,5},{1... | collective-permute-start | bytes 786440 | tf_op jit(solution)/shard_map/ppermute | solution.py:40
  28.7 3.5 %collective-permute-done.2.rest_3_ = bf16[2,128,512]{2,1,0:T(8,128)(2,1)S(1)} collective-permute-done((bf16[2,128,512]{2,1,0:T(8,128)(2,1)S(1)}, bf16[2,128,512]{2,1,0:T(8,128)(2,1)S(1)}, u32[]{:S(2)}, u32[]{:S(2)}) %collective-permute-start.2) | collective-permute-done | bytes 262176 | tf_op jit(solution)/shard_map/ppermute | solution.py:40
  32.2 1.9 %collective-permute-start.4 = (bf16[2,128,512]{2,1,0:T(8,128)(2,1)S(1)}, bf16[2,128,512]{2,1,0:T(8,128)(2,1)S(1)}, u32[]{:S(2)}, u32[]{:S(2)}) collective-permute-start(bf16[2,128,512]{2,1,0:T(8,128)(2,1)S(1)} %collective-permute-done.2.rest_3_), channel_id=1, source_target_pairs={{0,4},{1,5},{2,6},{3,7},{4,8},{5,9},{6,10},{7,11},{8,12},{9,13},{1... | collective-permute-start | bytes 786440 | tf_op jit(solution)/shard_map/ppermute | solution.py:40
  34.1 5.1 %collective-permute-start.5 = (bf16[2,128,512]{2,1,0:T(8,128)(2,1)S(1)}, bf16[2,128,512]{2,1,0:T(8,128)(2,1)S(1)}, u32[]{:S(2)}, u32[]{:S(2)}) collective-permute-start(bf16[2,128,512]{2,1,0:T(8,128)(2,1)S(1)} %collective-permute-done.3.rest_4_), channel_id=1, source_target_pairs={{0,28},{1,29},{2,30},{3,31},{4,0},{5,1},{6,2},{7,3},{8,4},{9,5},{1... | collective-permute-start | bytes 786440 | tf_op jit(solution)/shard_map/ppermute | solution.py:40
  39.3 1.9 %collective-permute-start.6 = (bf16[2,64,512]{2,1,0:T(8,128)(2,1)S(1)}, bf16[2,64,512]{2,1,0:T(8,128)(2,1)S(1)}, u32[]{:S(2)}, u32[]{:S(2)}) collective-permute-start(bf16[2,64,512]{2,1,0:T(8,128)(2,1)S(1)} %slice.38), channel_id=1, source_target_pairs={{0,8},{1,9},{2,10},{3,11},{4,12},{5,13},{6,14},{7,15},{8,16},{9,17... | collective-permute-start | bytes 393224 | tf_op jit(solution)/shard_map/ppermute | solution.py:40
  41.2 6.0 %collective-permute-start.7 = (bf16[2,64,512]{2,1,0:T(8,128)(2,1)S(1)}, bf16[2,64,512]{2,1,0:T(8,128)(2,1)S(1)}, u32[]{:S(2)}, u32[]{:S(2)}) collective-permute-start(bf16[2,64,512]{2,1,0:T(8,128)(2,1)S(1)} %slice.39), channel_id=1, source_target_pairs={{0,24},{1,25},{2,26},{3,27},{4,28},{5,29},{6,30},{7,31},{8,0},{9,1... | collective-permute-start | bytes 393224 | tf_op jit(solution)/shard_map/ppermute | solution.py:40
  48.9 3.9 %collective-permute-done.7.rest_8_ = bf16[2,64,512]{2,1,0:T(8,128)(2,1)S(1)} collective-permute-done((bf16[2,64,512]{2,1,0:T(8,128)(2,1)S(1)}, bf16[2,64,512]{2,1,0:T(8,128)(2,1)S(1)}, u32[]{:S(2)}, u32[]{:S(2)}) %collective-permute-start.7) | collective-permute-done | bytes 131104 | tf_op jit(solution)/shard_map/ppermute | solution.py:40
  54.1 3.8 %forward_tile.1 = (f32[256,512]{1,0:T(8,128)S(1)}, bf16[256,512]{1,0:T(8,128)(2,1)S(1)}) custom-call(s32[1]{0:T(128)} %bitcast.place, s32[32,2]{1,0:T(8,128)S(1)} %slice.29.ends, s32[512,128]{1,0:T(8,128)S(1)} %query_segments.1.qseg, s32[32,128]{1,0:T(8,128)S(1)} %bitcast.20, bf16[4,2,128,512]{3,2,1,0:T(8,128)(2,1)S(1)} %bitcast.23, ...), custom_call_target="tpu_custom_call" | custom-call | flops 1500000000 | bytes 3000000 | tf_op jit(solution)/shard_map/forward_tile/pallas_call | solution.py:184
  57.9 2.1 %collective-permute-start.8 = (bf16[256,512]{1,0:T(8,128)(2,1)S(1)}, bf16[256,512]{1,0:T(8,128)(2,1)S(1)}, u32[]{:S(2)}, u32[]{:S(2)}) collective-permute-start(bf16[256,512]{1,0:T(8,128)(2,1)S(1)} %get-tuple-element.21), channel_id=1, source_target_pairs={{0,1},{1,0},{2,3},{3,2},{4,5},{5,4},{6,7},{7,6},{8,9},{9,8},{10,11... | collective-permute-start | bytes 786440 | tf_op jit(solution)/shard_map/ppermute | solution.py:44
  59.9 1.5 collective-permute-done.8
  61.6 13.6 %all-gather.1 = bf16[256,512]{1,0:T(8,128)(2,1)S(1)} all-gather(bf16[128,512]{1,0:T(8,128)(2,1)S(1)} %slice.54), channel_id=3, replica_groups={{0,2},{1,3},{4,6},{5,7},{8,10},{9,11},{12,14},{13,15},{16,18},{17,19},{..., dimensions={0}, use_global_device_ids=true | all-gather | bytes 393216 | tf_op jit(solution)/shard_map/all_gather | solution.py:205
  76.1 13.2 %all-gather.2 = bf16[576,512]{1,0:T(8,128)(2,1)S(1)} all-gather(bf16[144,512]{1,0:T(8,128)(2,1)S(1)} %get-tuple-element.23), channel_id=4, replica_groups={{0,1,2,3},{4,5,6,7},{8,9,10,11},{12,13,14,15},{16,17,18,19},{20,21,22,2..., dimensions={0}, use_global_device_ids=true | all-gather | bytes 737280 | tf_op jit(solution)/shard_map/all_gather | solution.py:248
  89.3 9.6 %backward_tile.1 = (f32[256,512]{1,0:T(8,128)S(1)}, bf16[256,512]{1,0:T(8,128)(2,1)S(1)}, f32[1,512]{1,0:T(1,128)S(1)}, bf16[2048,512]{1,0:T(8,128)(2,1)}) custom-call(s32[1]{0:T(128)} %bitcast.place, s32[32,2]{1,0:T(8,128)S(1)} %slice.29.ends, s32[512,128]{1,0:T(8,128)S(1)} %query_segments.1.qseg, s32[32,128]{1,0:T(8,128)S(1)} %bitcast.21, ...), custom_call_target="tpu_custom_call" | custom-call | flops 4499999744 | bytes 9000000 | tf_op jit(solution)/shard_map/backward_tile/pallas_call | solution.py:184
  99.0 2.3 %collective-permute-start.9 = (bf16[256,512]{1,0:T(8,128)(2,1)S(1)}, bf16[256,512]{1,0:T(8,128)(2,1)S(1)}, u32[]{:S(2)}, u32[]{:S(2)}) collective-permute-start(bf16[256,512]{1,0:T(8,128)(2,1)S(1)} %get-tuple-element.25), channel_id=1, source_target_pairs={{0,1},{1,0},{2,3},{3,2},{4,5},{5,4},{6,7},{7,6},{8,9},{9,8},{10,11... | collective-permute-start | bytes 786440 | tf_op jit(solution)/shard_map/ppermute | solution.py:44
  102.5 11.9 %all-gather.3 = bf16[256,512]{1,0:T(8,128)(2,1)S(1)} all-gather(bf16[128,512]{1,0:T(8,128)(2,1)S(1)} %slice.53), channel_id=5, replica_groups={{0,2},{1,3},{4,6},{5,7},{8,10},{9,11},{12,14},{13,15},{16,18},{17,19},{..., dimensions={0}, use_global_device_ids=true | all-gather | bytes 393216 | tf_op jit(solution)/shard_map/all_gather | solution.py:205
  115.0 17.2 %all_to_all.12 = f32[16,1,512]{2,1,0:T(1,128)S(1)} all-to-all(f32[16,1,512]{2,1,0:T(1,128)S(1)} %broadcast_in_dim.33), channel_id=1, replica_groups=mesh['dp'=16,'ctx'=32] {'dp'}, dimensions={0} | all-to-all | bytes 65536 | tf_op jit(solution)/shard_map/all_to_all | solution.py:49
  132.3 14.1 %all_to_all.13 = f32[8,1,512]{2,1,0:T(1,128)S(1)} all-to-all(f32[8,1,512]{2,1,0:T(1,128)S(1)} %broadcast_in_dim.34), channel_id=1, replica_groups={{0,4,8,12,16,20,24,28},{1,5,9,13,17,21,25,29},{2,6,10,14,18,22,26,30},{..., dimensions={0} | all-to-all | bytes 32768 | tf_op jit(solution)/shard_map/all_to_all | solution.py:49
  147.0 2.6 %reduce-scatter.2.cloned.1.call-done = bf16[256,512]{1,0:T(8,128)(2,1)} async-done(((bf16[2048,512]{1,0:T(8,128)(2,1)}), bf16[256,512]{1,0:T(8,128)(2,1)}) %reduce-scatter.2.cloned.1.call-update) | async-done | bytes 262160 | tf_op jit(solution)/shard_map/reduce_scatter | solution.py:259
  149.6 1.7 %slice_bitcast_fusion = (bf16[1,128,512]{2,1,0:T(8,128)(2,1)}, bf16[1,128,512]{2,1,0:T(8,128)(2,1)}) fusion(bf16[256,512]{1,0:T(8,128)(2,1)} %reduce-scatter.2.cloned.1.call-done), kind=kLoop, calls=%fused_computation.7 | loop fusion | bytes 524288 | tf_op jit(solution)/shard_map/broadcast_in_dim | solution.py:274
  (42 shorter events, 7.6 us)
Async XLA Ops:
  7.2 45.7 %copy-start.1 = (s32[1,4096]{1,0:T(1,128)S(1)}, s32[1,4096]{1,0:T(1,128)}, u32[]{:S(2)}) copy-start(s32[1,4096]{1,0:T(1,128)} %param.12) | copy-start | bytes 49156
  7.2 45.6 %all-gather.6.cloned.1.call-start = ((), (), s32[]{:S(2)}) async-start(), calls=%async_computation.4 | async-start | bytes 1310720 | tf_op jit(solution)/shard_map/all_gather | solution.py:213
  9.9 139.7 %reduce-scatter.2.cloned.1.call-start = ((), (), s32[]{:S(2)}) async-start(), calls=%async_computation.3 | async-start | bytes 2359296 | tf_op jit(solution)/shard_map/reduce_scatter | solution.py:259
  9.9 11.7 %collective-permute-start = (bf16[2,128,512]{2,1,0:T(8,128)(2,1)S(1)}, bf16[2,128,512]{2,1,0:T(8,128)(2,1)S(1)}, u32[]{:S(2)}, u32[]{:S(2)}) collective-permute-start(bf16[2,128,512]{2,1,0:T(8,128)(2,1)S(1)} %pad_maximum_fusion.rest_0_), channel_id=1, source_target_pairs={{0,4},{1,5},{2,6},{3,7},{4,8},{5,9},{6,10},{7,11},{8,12},{9,13},{1... | collective-permute-start | bytes 786440 | tf_op jit(solution)/shard_map/ppermute | solution.py:40
  13.4 10.1 %collective-permute-start.1 = (bf16[2,128,512]{2,1,0:T(8,128)(2,1)S(1)}, bf16[2,128,512]{2,1,0:T(8,128)(2,1)S(1)}, u32[]{:S(2)}, u32[]{:S(2)}) collective-permute-start(bf16[2,128,512]{2,1,0:T(8,128)(2,1)S(1)} %pad_maximum_fusion.rest_0_), channel_id=1, source_target_pairs={{0,28},{1,29},{2,30},{3,31},{4,0},{5,1},{6,2},{7,3},{8,4},{9,5},{1... | collective-permute-start | bytes 786440 | tf_op jit(solution)/shard_map/ppermute | solution.py:40
  21.6 10.6 %collective-permute-start.2 = (bf16[2,128,512]{2,1,0:T(8,128)(2,1)S(1)}, bf16[2,128,512]{2,1,0:T(8,128)(2,1)S(1)}, u32[]{:S(2)}, u32[]{:S(2)}) collective-permute-start(bf16[2,128,512]{2,1,0:T(8,128)(2,1)S(1)} %collective-permute-done.rest_1_), channel_id=1, source_target_pairs={{0,4},{1,5},{2,6},{3,7},{4,8},{5,9},{6,10},{7,11},{8,12},{9,13},{1... | collective-permute-start | bytes 786440 | tf_op jit(solution)/shard_map/ppermute | solution.py:40
  23.5 10.6 %collective-permute-start.3 = (bf16[2,128,512]{2,1,0:T(8,128)(2,1)S(1)}, bf16[2,128,512]{2,1,0:T(8,128)(2,1)S(1)}, u32[]{:S(2)}, u32[]{:S(2)}) collective-permute-start(bf16[2,128,512]{2,1,0:T(8,128)(2,1)S(1)} %collective-permute-done.1.rest_2_), channel_id=1, source_target_pairs={{0,28},{1,29},{2,30},{3,31},{4,0},{5,1},{6,2},{7,3},{8,4},{9,5},{1... | collective-permute-start | bytes 786440 | tf_op jit(solution)/shard_map/ppermute | solution.py:40
  32.2 20.6 %collective-permute-start.4 = (bf16[2,128,512]{2,1,0:T(8,128)(2,1)S(1)}, bf16[2,128,512]{2,1,0:T(8,128)(2,1)S(1)}, u32[]{:S(2)}, u32[]{:S(2)}) collective-permute-start(bf16[2,128,512]{2,1,0:T(8,128)(2,1)S(1)} %collective-permute-done.2.rest_3_), channel_id=1, source_target_pairs={{0,4},{1,5},{2,6},{3,7},{4,8},{5,9},{6,10},{7,11},{8,12},{9,13},{1... | collective-permute-start | bytes 786440 | tf_op jit(solution)/shard_map/ppermute | solution.py:40
  34.1 18.7 %collective-permute-start.5 = (bf16[2,128,512]{2,1,0:T(8,128)(2,1)S(1)}, bf16[2,128,512]{2,1,0:T(8,128)(2,1)S(1)}, u32[]{:S(2)}, u32[]{:S(2)}) collective-permute-start(bf16[2,128,512]{2,1,0:T(8,128)(2,1)S(1)} %collective-permute-done.3.rest_4_), channel_id=1, source_target_pairs={{0,28},{1,29},{2,30},{3,31},{4,0},{5,1},{6,2},{7,3},{8,4},{9,5},{1... | collective-permute-start | bytes 786440 | tf_op jit(solution)/shard_map/ppermute | solution.py:40
  39.3 9.6 %collective-permute-start.6 = (bf16[2,64,512]{2,1,0:T(8,128)(2,1)S(1)}, bf16[2,64,512]{2,1,0:T(8,128)(2,1)S(1)}, u32[]{:S(2)}, u32[]{:S(2)}) collective-permute-start(bf16[2,64,512]{2,1,0:T(8,128)(2,1)S(1)} %slice.38), channel_id=1, source_target_pairs={{0,8},{1,9},{2,10},{3,11},{4,12},{5,13},{6,14},{7,15},{8,16},{9,17... | collective-permute-start | bytes 393224 | tf_op jit(solution)/shard_map/ppermute | solution.py:40
  41.2 11.6 %collective-permute-start.7 = (bf16[2,64,512]{2,1,0:T(8,128)(2,1)S(1)}, bf16[2,64,512]{2,1,0:T(8,128)(2,1)S(1)}, u32[]{:S(2)}, u32[]{:S(2)}) collective-permute-start(bf16[2,64,512]{2,1,0:T(8,128)(2,1)S(1)} %slice.39), channel_id=1, source_target_pairs={{0,24},{1,25},{2,26},{3,27},{4,28},{5,29},{6,30},{7,31},{8,0},{9,1... | collective-permute-start | bytes 393224 | tf_op jit(solution)/shard_map/ppermute | solution.py:40
  48.1 0.7 copy-start
  52.8 1.2 copy-start.2
  57.8 17.3 %copy-start.4 = (bf16[1,128,512]{2,1,0:T(8,128)(2,1)S(1)}, bf16[1,128,512]{2,1,0:T(8,128)(2,1)}, u32[]{:S(2)}) copy-start(bf16[1,128,512]{2,1,0:T(8,128)(2,1)} %gate.1) | copy-start | bytes 393220
  57.9 17.3 %copy-start.5 = (bf16[1,128,512]{2,1,0:T(8,128)(2,1)S(1)}, bf16[1,128,512]{2,1,0:T(8,128)(2,1)}, u32[]{:S(2)}) copy-start(bf16[1,128,512]{2,1,0:T(8,128)(2,1)} %grad.1) | copy-start | bytes 393220
  57.9 17.3 %copy-start.6 = (f32[512]{0:T(512)S(1)}, f32[512]{0:T(512)}, u32[]{:S(2)}) copy-start(f32[512]{0:T(512)} %param.13) | copy-start | bytes 6148
  57.9 3.6 %collective-permute-start.8 = (bf16[256,512]{1,0:T(8,128)(2,1)S(1)}, bf16[256,512]{1,0:T(8,128)(2,1)S(1)}, u32[]{:S(2)}, u32[]{:S(2)}) collective-permute-start(bf16[256,512]{1,0:T(8,128)(2,1)S(1)} %get-tuple-element.21), channel_id=1, source_target_pairs={{0,1},{1,0},{2,3},{3,2},{4,5},{5,4},{6,7},{7,6},{8,9},{9,8},{10,11... | collective-permute-start | bytes 786440 | tf_op jit(solution)/shard_map/ppermute | solution.py:44
  61.5 27.8 %copy-start.3 = (bf16[8,128,512]{2,1,0:T(8,128)(2,1)S(1)}, bf16[8,128,512]{2,1,0:T(8,128)(2,1)}, u32[]{:S(2)}) copy-start(bf16[8,128,512]{2,1,0:T(8,128)(2,1)} %all-gather.6.cloned.1.call-done) | copy-start | bytes 3145732
  99.0 3.4 %collective-permute-start.9 = (bf16[256,512]{1,0:T(8,128)(2,1)S(1)}, bf16[256,512]{1,0:T(8,128)(2,1)S(1)}, u32[]{:S(2)}, u32[]{:S(2)}) collective-permute-start(bf16[256,512]{1,0:T(8,128)(2,1)S(1)} %get-tuple-element.25), channel_id=1, source_target_pairs={{0,1},{1,0},{2,3},{3,2},{4,5},{5,4},{6,7},{7,6},{8,9},{9,8},{10,11... | collective-permute-start | bytes 786440 | tf_op jit(solution)/shard_map/ppermute | solution.py:44
Sparse Core Ops, SparseCore 0:
  10.1 39.4 all-gather.5
  99.1 50.4 reduce-scatter.1

commit v4 on v3

--- a/solution.py
+++ b/solution.py
@@ -28,6 +28,7 @@
 EXTRA = 16
 PAIRS = (((0, 0), (-1, 1)), ((1, 2), (2, 4)), ((-2, 3), (-3, 5)), ((3, 6), (4, 7)))
 QUADS = [[y * QUAD + c for c in range(QUAD)] for y in range(RING)]
+CORES = [[y * QUAD + z * ZHI + c for c in range(2)] for y in range(RING) for z in range(2)]
 ZPAIRS = [[y * QUAD + z * ZHI + c for z in range(2)] for y in range(RING) for c in range(2)]
 RINGS = [[y * QUAD + c for y in range(RING)] for c in range(QUAD)]
 
@@ -54,11 +55,7 @@
 
 
 def pair_of(kv, pair, which, h):
-    parts = []
-    for _, at in PAIRS[pair]:
-        for ref in kv[at:] if at == RING - 1 else kv[at : at + 1]:
-            parts.append(ref[which, :, head(h)])
-    return jnp.concatenate(parts, axis=0)
+    return jnp.concatenate([kv[at][which, :, head(h)] for _, at in PAIRS[pair]], axis=0)
 
 
 def key_blocks(place, pair):
@@ -89,7 +86,7 @@
         send[rows, :] = acc[rows_of(place, flip ^ CORE), :].astype(BF16)
 
 
-def segment_kernel(place, segs, qseg):
+def segment_rows(place, segs, qseg):
     first = (place[0] // QUAD) * QUAD
     for i in range(QUAD):
         row = segs[pl.ds(first + i, 1), :]
@@ -97,13 +94,12 @@
 
 
 def queries_of(q, c, h):
-    return q[2 * c : 2 * c + 2, 0, :, head(h)].reshape(CHUNK, HSIZE)
-
-
-def forward_kernel(place, ends, qseg, segs, q, *rest):
-    kv, (keep, send, acc) = rest[: RING + 1], rest[RING + 1 :]
-    acc[...] = jnp.zeros_like(acc)
-    for pair in range(len(PAIRS)):
+    return q[2 * c : 2 * c + 2, :, head(h)].reshape(CHUNK, HSIZE)
+
+
+def forward_pairs(pairs, place, ends, segs, q, kv, acc, qseg):
+    segment_rows(place, segs, qseg)
+    for pair in pairs:
         blocks = key_blocks(place[0], pair)
         for c in range(TILE // CHUNK):
 
@@ -118,35 +114,62 @@
                     w = jnp.where(same, silu, 0.0).astype(BF16)
                     acc[rows, head(h)] += dot(w, values, NN)
 
+
+def near_kernel(place, ends, segs, q, own, prev, next_, next2, acc, qseg):
+    acc[...] = jnp.zeros_like(acc)
+    kv = {0: own, 1: prev, 2: next_, 4: next2}
+    forward_pairs((0, 1), place, ends, segs, q, kv, acc, qseg)
+
+
+def far_kernel(place, ends, segs, q, begun, prev2, prev3, next3, low, high, *rest):
+    keep, send, far, acc, qseg = rest
+    far[:, :CUT, :] = low[...]
+    far[:, CUT:, :] = high[...]
+    acc[...] = begun[...]
+    kv = {3: prev2, 5: prev3, 6: next3, 7: far}
+    forward_pairs((2, 3), place, ends, segs, q, kv, acc, qseg)
     share_out(place[0], acc, keep, send)
 
 
-def norm_kernel(place, kept, came, gate, grad, gain, out, gate_grad, attn_grad):
-    g = gain[...]
-    att = kept[...] + came[1 - lax.rem(place[0], QUAD) // ZHI].astype(F32)
-    inv = lax.rsqrt(jnp.mean(att * att, axis=1, keepdims=True) + 1e-06)
-    normed = att * inv
-    gate_f = gate[0].astype(F32)
-    grad_f = grad[0].astype(F32)
-    both = grad_f * gate_f
-    out[0] = (normed * g * gate_f).astype(BF16)
-    gate_grad[0] = (grad_f * normed * g).astype(BF16)
-    ng = both * g
-    mean = jnp.mean(normed * ng, axis=1, keepdims=True)
-    attn_grad[:ROWS, :] = (inv * (ng - normed * mean)).astype(BF16)
-    part = jnp.sum(both * normed, axis=0, keepdims=True)
+def terms_of(part):
     high = part.astype(BF16).astype(F32)
     line = lax.broadcasted_iota(jnp.int32, (EXTRA, HD), 0)
-    extra = jnp.where(line == 0, high, jnp.where(line == 1, part - high, 0.0))
-    attn_grad[ROWS:, :] = extra.astype(BF16)
-
-
-def backward_kernel(place, ends, qseg, segs, q, da, *rest):
-    kv, (keep, send, part, dkv, acc, dk, dv) = rest[: RING + 1], rest[RING + 1 :]
+    return jnp.where(line == 0, high, jnp.where(line == 1, part - high, 0.0)).astype(BF16)
+
+
+def z_of(place):
+    return lax.rem(place, QUAD) // ZHI
+
+
+def norm_kernel(place, kept, came, gate, grad, product, gain, out, gate_grad, attn_grad):
+    g = gain[...]
+    other = came.at[1 - z_of(place[0])]
+    for i in range(2):
+        rows, theirs = slice(i * ROWS, (i + 1) * ROWS), slice((1 - i) * ROWS, (2 - i) * ROWS)
+        att = kept[rows, :] + other[theirs, :].astype(F32)
+        inv = lax.rsqrt(jnp.mean(att * att, axis=1, keepdims=True) + 1e-06)
+        normed = att * inv
+        if i == 0:
+            gate_f = gate[0].astype(F32)
+            grad_f = grad[0].astype(F32)
+            both = grad_f * gate_f
+            out[0] = (normed * g * gate_f).astype(BF16)
+            gate_grad[0] = (grad_f * normed * g).astype(BF16)
+            attn_grad[2 * ROWS :, :] = terms_of(jnp.sum(both * normed, axis=0, keepdims=True))
+        else:
+            both = product[...].astype(F32)
+        ng = both * g
+        mean = jnp.mean(normed * ng, axis=1, keepdims=True)
+        attn_grad[rows, :] = (inv * (ng - normed * mean)).astype(BF16)
+
+
+def backward_kernel(place, ends, segs, q, da, *rest):
+    kv, (keep, send, extra, dkv, acc, dk, dv, qseg) = rest[:RING], rest[RING:]
+    segment_rows(place, segs, qseg)
     acc[...] = jnp.zeros_like(acc)
-    extra = [da[i, ROWS:, :].astype(F32) for i in range(QUAD)]
-    terms = [rows[0:1] + rows[1:2] for rows in extra]
-    part[...] = (terms[0] + terms[1]) + (terms[2] + terms[3])
+    terms = [da[i, 2 * ROWS :, :].astype(F32) for i in range(2)]
+    sums = [rows[0:1] + rows[1:2] for rows in terms]
+    extra[...] = terms_of(sums[0] + sums[1])
     for pair in range(len(PAIRS)):
         blocks = key_blocks(place[0], pair)
         dk[...] = jnp.zeros_like(dk)
@@ -157,10 +180,11 @@
             def _(pair=pair, blocks=blocks, c=c):
                 rows = slice(c * CHUNK, (c + 1) * CHUNK)
                 same = same_history(qseg, segs, rows, blocks)
+                at = pl.multiple_of((z_of(place[0]) ^ c) * ROWS, ROWS)
                 for h in range(HEADS):
                     keys, values = pair_of(kv, pair, 0, h), pair_of(kv, pair, 1, h)
                     qb = queries_of(q, c, h)
-                    db = da[2 * c : 2 * c + 2, :ROWS, head(h)].reshape(CHUNK, HSIZE)
+                    db = da[:, pl.ds(at, ROWS), head(h)].reshape(CHUNK, HSIZE)
                     half = dot(qb, keys, NT) * (0.5 * SCALE)
                     vd = dot(db, values, NT)
                     t = jnp.tanh(half)
@@ -187,7 +211,9 @@
         in_specs=[pl.BlockSpec(memory_space=pltpu.SMEM)] * scalars
         + [pl.BlockSpec(memory_space=pltpu.VMEM)] * (len(operands) - scalars),
         out_specs=(pl.BlockSpec(memory_space=pltpu.VMEM),) * len(outs),
-        scratch_shapes=[pltpu.VMEM(shape, F32) for shape in scratch],
+        scratch_shapes=[
+            pltpu.VMEM(shape, jnp.int32 if shape[1] == ROWS else F32) for shape in scratch
+        ],
         compiler_params=pltpu.CompilerParams(vmem_limit_bytes=VMEM_LIMIT),
         cost_estimate=pl.CostEstimate(
             flops=us * 500_000_000, bytes_accessed=us * 1_000_000, transcendentals=0
@@ -200,18 +226,14 @@
     return lax.optimization_barrier((value, *others))[0]
 
 
-def sum_quad(keep, send):
-    keep = keep + swap(send, CORE).astype(F32)
-    return keep[:ROWS], lax.all_gather(keep[ROWS:].astype(BF16), "ctx", axis_index_groups=ZPAIRS)
-
-
 def per_device(queries, key_states, value_states, gate_states, out_grad, segment_ids, norm_gain):
     place = lax.axis_index("ctx").astype(jnp.int32)
     rows, tile, half = (1, ROWS, HD), (TILE, HD), (HALF, HD)
     kv = jnp.concatenate([key_states, value_states], axis=0)
     first, kv = lax.optimization_barrier((queries, kv))
+    product = (out_grad.astype(F32) * gate_states.astype(F32)).astype(BF16)
     gathered = lax.all_gather(
-        jnp.pad(first, ((0, 1), (0, 0), (0, 0))), "ctx", axis_index_groups=QUADS
+        jnp.concatenate([first, product], axis=0), "ctx", axis_index_groups=QUADS
     )
 
     up = down = kv
@@ -223,46 +245,56 @@
 
     segs = segment_ids.reshape(CTX, ROWS)
     ends = segs[:, :: ROWS - 1]
-    (qseg,) = call(
-        segment_kernel, "query_segments", [((TILE, ROWS), jnp.int32)], (place[None], segs), 1
-    )
-    shared = (place[None], ends, qseg, segs, gathered)
-
-    keep, send = call(
-        forward_kernel,
-        "forward_tile",
-        [(half, F32), (half, BF16)],
-        (*shared, *blocks),
+    product = lax.dynamic_index_in_dim(gathered, lax.rem(place, QUAD) ^ ZHI, 0, keepdims=False)[1]
+    shared = (place[None], ends, segs, gathered[:, 0])
+
+    (begun,) = call(
+        near_kernel,
+        "forward_near",
+        [(tile, F32)],
+        (*shared, *(blocks[at] for at in (0, 1, 2, 4))),
         2,
-        [tile],
-        us=3,
-    )
-    mine, came = sum_quad(keep, send)
+        [(TILE, ROWS)],
+        us=2,
+    )
+    keep, send, far = call(
+        far_kernel,
+        "forward_far",
+        [(half, F32), (half, BF16), ((2, ROWS, HD), BF16)],
+        (*shared, begun, *(blocks[at] for at in (3, 5, 6, 7, 8))),
+        2,
+        [tile, (TILE, ROWS)],
+        us=2,
+    )
+    keep = keep + swap(send, CORE).astype(F32)
+    came = lax.all_gather(keep.astype(BF16), "ctx", axis_index_groups=ZPAIRS)
     layer_out, gate_grad, attn_grad = call(
         norm_kernel,
         "norm_rows",
-        [(rows, BF16), (rows, BF16), ((ROWS + EXTRA, HD), BF16)],
-        (place[None], mine, came, gate_states, out_grad, norm_gain[None, :]),
+        [(rows, BF16), (rows, BF16), ((2 * ROWS + EXTRA, HD), BF16)],
+        (place[None], keep, came, gate_states, out_grad, product, norm_gain[None, :]),
         1,
     )
-    grads = lax.all_gather(attn_grad, "ctx", axis_index_groups=QUADS)
-
-    keep, send, part, dkv = call(
+    grads = lax.all_gather(attn_grad, "ctx", axis_index_groups=CORES)
+
+    keep, send, extra, dkv = call(
         backward_kernel,
         "backward_tile",
-        [(half, F32), (half, BF16), ((1, HD), F32), ((RING * 2 * ROWS, HD), BF16)],
-        (*shared, grads, *blocks),
+        [(half, F32), (half, BF16), ((EXTRA, HD), BF16), ((RING * 2 * ROWS, HD), BF16)],
+        (*shared, grads, *blocks[: RING - 1], far),
         2,
-        [tile, half, half],
+        [tile, half, half, (TILE, ROWS)],
         us=9,
     )
     dkv_sum = lax.psum_scatter(dkv, "ctx", tiled=True, axis_index_groups=RINGS)
-    mine, came = sum_quad(keep, send)
-    came = lax.dynamic_index_in_dim(came, 1 - lax.rem(place, QUAD) // ZHI, 0, keepdims=False)
-    query_grad = (mine + came.astype(F32)).astype(BF16)
+    keep = keep + swap(send, CORE).astype(F32)
+    send = jnp.concatenate([keep[ROWS:].astype(BF16), extra], axis=0)
+    came = lax.all_gather(send, "ctx", axis_index_groups=ZPAIRS)
+    theirs = lax.dynamic_index_in_dim(came, 1 - z_of(place), 0, keepdims=False)[:ROWS]
+    query_grad = (keep[:ROWS] + theirs.astype(F32)).astype(BF16)
 
     dp = lax.axis_size("dp")
-    part = after(part, query_grad)
+    part = jnp.sum(came[:, ROWS : ROWS + 2].astype(F32), axis=(0, 1))[None]
     part = jnp.sum(everywhere(part, "dp", None, dp), axis=0, keepdims=True)
     part = jnp.sum(everywhere(part, "ctx", RINGS, RING), axis=0)
     gain_grad = part / math.sqrt(dp * CTX * ROWS)

time: 159 us -> 155 us (0.975)
  the two profiles are of different devices: /device:TPU:4 before, /device:TPU:1 now
where the time goes in v4:
time: 155 us; the launch traced here: 153 us
  starting transfers between devices  47.1 us (30%)
  blocking collectives  33.9 us (22%)
  waiting for transfers between devices  25.4 us (16%)
  Pallas kernels  20 us (13%)
  between operations  14.3 us (9%)
  local copies, waits for them, and re-layouts  6.5 us (4%)
  other arithmetic  6.12 us (4%)
    ppermute x8, starting transfers between devices, along(): lax.ppermute(value, 'ctx', [(i, (i + step * QUAD) % CTX) for i in range(C...  29.1 us
    pallas_call x4, Pallas kernels, call(): pl.pallas_call(kernel, out_shape=tuple((jax.ShapeDtypeStruct(shape, dtype...  20 us
    all_gather x1, blocking collectives, per_device(): came = lax.all_gather(keep.astype(BF16), 'ctx', axis_index_groups=ZPAIRS)  15.6 us
    all_gather x1, blocking collectives, per_device(): came = lax.all_gather(send, 'ctx', axis_index_groups=ZPAIRS)  15.5 us
    all_to_all x2, starting transfers between devices, everywhere(): lax.all_to_all(value, axis, 0, 0, tiled=True, axis_index_groups=groups)  13.3 us
    all_to_all x2, waiting for transfers between devices, everywhere(): lax.all_to_all(value, axis, 0, 0, tiled=True, axis_index_groups=groups)  13 us
    all_gather x1, waiting for transfers between devices, per_device(): lax.all_gather(jnp.concatenate([first, product], axis=0), 'ctx', axis_ind...  8.89 us
    ppermute x2, starting transfers between devices, swap(): return lax.ppermute(value, 'ctx', [(i, i ^ flip) for i in range(CTX)])  4.59 us
  transfers between devices with their start and end apart: 14, of which 7 were waited for; matrix products, arithmetic and copies ran while one was open for 4% of the time, Pallas kernels for 2%

profile of v4, /device:TPU:1, one launch (start us, length us, event | category | flops | bytes accessed | tf_op | source)
XLA Modules:
  0.0 153.4 jit_solution(6854903889759284670)
XLA Ops:
  9.2 1.7 %pad_maximum_fusion.1 = bf16[2,128,512]{2,1,0:T(8,128)(2,1)} fusion(bf16[1,128,512]{2,1,0:T(8,128)(2,1)S(1)} %multiply_convert_fusion, bf16[1,128,512]{2,1,0:T(8,128)(2,1)} %param.7), kind=kLoop, calls=%fused_computation.7 | loop fusion | flops 131072 | bytes 524288 | tf_op jit(solution)/shard_map/concatenate | solution.py:236
  11.0 5.9 %collective-permute-start.1 = (bf16[2,128,512]{2,1,0:T(8,128)(2,1)S(1)}, bf16[2,128,512]{2,1,0:T(8,128)(2,1)S(1)}, u32[]{:S(2)}, u32[]{:S(2)}) collective-permute-start(bf16[2,128,512]{2,1,0:T(8,128)(2,1)S(1)} %pad_maximum_fusion.own.rest_0_), channel_id=1, source_target_pairs={{0,28},{1,29},{2,30},{3,31},{4,0},{5,1},{6,2},{7,3},{8,4},{9,5},{1... | collective-permute-start | bytes 786440 | tf_op jit(solution)/shard_map/ppermute | solution.py:41
  16.9 1.9 %collective-permute-start = (bf16[2,128,512]{2,1,0:T(8,128)(2,1)S(1)}, bf16[2,128,512]{2,1,0:T(8,128)(2,1)S(1)}, u32[]{:S(2)}, u32[]{:S(2)}) collective-permute-start(bf16[2,128,512]{2,1,0:T(8,128)(2,1)S(1)} %pad_maximum_fusion.own.rest_0_), channel_id=1, source_target_pairs={{0,4},{1,5},{2,6},{3,7},{4,8},{5,9},{6,10},{7,11},{8,12},{9,13},{1... | collective-permute-start | bytes 786440 | tf_op jit(solution)/shard_map/ppermute | solution.py:41
  18.8 1.4 collective-permute-done.1.next_.rest_2_
  20.2 5.0 %collective-permute-start.2 = (bf16[2,128,512]{2,1,0:T(8,128)(2,1)S(1)}, bf16[2,128,512]{2,1,0:T(8,128)(2,1)S(1)}, u32[]{:S(2)}, u32[]{:S(2)}) collective-permute-start(bf16[2,128,512]{2,1,0:T(8,128)(2,1)S(1)} %collective-permute-done.1.next_.rest_2_), channel_id=1, source_target_pairs={{0,28},{1,29},{2,30},{3,31},{4,0},{5,1},{6,2},{7,3},{8,4},{9,5},{1... | collective-permute-start | bytes 786440 | tf_op jit(solution)/shard_map/ppermute | solution.py:41
  25.2 1.9 %collective-permute-start.3 = (bf16[2,128,512]{2,1,0:T(8,128)(2,1)S(1)}, bf16[2,128,512]{2,1,0:T(8,128)(2,1)S(1)}, u32[]{:S(2)}, u32[]{:S(2)}) collective-permute-start(bf16[2,128,512]{2,1,0:T(8,128)(2,1)S(1)} %collective-permute-done.prev.rest_1_), channel_id=1, source_target_pairs={{0,4},{1,5},{2,6},{3,7},{4,8},{5,9},{6,10},{7,11},{8,12},{9,13},{1... | collective-permute-start | bytes 786440 | tf_op jit(solution)/shard_map/ppermute | solution.py:41
  28.5 6.2 %collective-permute-start.7 = (bf16[2,64,512]{2,1,0:T(8,128)(2,1)S(1)}, bf16[2,64,512]{2,1,0:T(8,128)(2,1)S(1)}, u32[]{:S(2)}, u32[]{:S(2)}) collective-permute-start(bf16[2,64,512]{2,1,0:T(8,128)(2,1)S(1)} %slice.49), channel_id=1, source_target_pairs={{0,24},{1,25},{2,26},{3,27},{4,28},{5,29},{6,30},{7,31},{8,0},{9,1... | collective-permute-start | bytes 393224 | tf_op jit(solution)/shard_map/ppermute | solution.py:41
  34.8 1.9 %collective-permute-start.6 = (bf16[2,64,512]{2,1,0:T(8,128)(2,1)S(1)}, bf16[2,64,512]{2,1,0:T(8,128)(2,1)S(1)}, u32[]{:S(2)}, u32[]{:S(2)}) collective-permute-start(bf16[2,64,512]{2,1,0:T(8,128)(2,1)S(1)} %slice.48), channel_id=1, source_target_pairs={{0,8},{1,9},{2,10},{3,11},{4,12},{5,13},{6,14},{7,15},{8,16},{9,17... | collective-permute-start | bytes 393224 | tf_op jit(solution)/shard_map/ppermute | solution.py:41
  36.7 4.2 %collective-permute-start.5 = (bf16[2,128,512]{2,1,0:T(8,128)(2,1)S(1)}, bf16[2,128,512]{2,1,0:T(8,128)(2,1)S(1)}, u32[]{:S(2)}, u32[]{:S(2)}) collective-permute-start(bf16[2,128,512]{2,1,0:T(8,128)(2,1)S(1)} %collective-permute-done.2.next2.rest_4_), channel_id=1, source_target_pairs={{0,28},{1,29},{2,30},{3,31},{4,0},{5,1},{6,2},{7,3},{8,4},{9,5},{1... | collective-permute-start | bytes 786440 | tf_op jit(solution)/shard_map/ppermute | solution.py:41
  41.0 1.9 %collective-permute-start.4 = (bf16[2,128,512]{2,1,0:T(8,128)(2,1)S(1)}, bf16[2,128,512]{2,1,0:T(8,128)(2,1)S(1)}, u32[]{:S(2)}, u32[]{:S(2)}) collective-permute-start(bf16[2,128,512]{2,1,0:T(8,128)(2,1)S(1)} %collective-permute-done.3.prev2.rest_3_), channel_id=1, source_target_pairs={{0,4},{1,5},{2,6},{3,7},{4,8},{5,9},{6,10},{7,11},{8,12},{9,13},{1... | collective-permute-start | bytes 786440 | tf_op jit(solution)/shard_map/ppermute | solution.py:41
  42.9 8.9 %all-gather.6.cloned.1.call-done = bf16[8,128,512]{2,1,0:T(8,128)(2,1)} async-done(((bf16[2,128,512]{2,1,0:T(8,128)(2,1)}), bf16[8,128,512]{2,1,0:T(8,128)(2,1)}) %all-gather.6.cloned.1.call-update) | async-done | bytes 1048592 | tf_op jit(solution)/shard_map/all_gather | solution.py:235
  52.9 3.7 %forward_near.1.begun = f32[512,512]{1,0:T(8,128)S(1)} custom-call(s32[1]{0:T(128)} %bitcast.place, s32[32,2]{1,0:T(8,128)S(1)} %slice.36.ends, s32[32,128]{1,0:T(8,128)S(1)} %bitcast.27, bf16[4,128,512]{2,1,0:T(8,128)(2,1)S(1)} %slice_bitcast_fusion.q, bf16[2,128,512]{2,1,0:T(8,128)(2,1)S(1)} %pad_maximum_fusion.own.rest_0_, ...), custom_call_target="tpu_custom_call" | custom-call | flops 1000000000 | bytes 2000000 | tf_op jit(solution)/shard_map/forward_near/pallas_call | solution.py:208
  56.6 2.4 %forward_far.1 = (f32[256,512]{1,0:T(8,128)S(1)}, bf16[256,512]{1,0:T(8,128)(2,1)S(1)}, bf16[2,128,512]{2,1,0:T(8,128)(2,1)S(1)}) custom-call(s32[1]{0:T(128)} %bitcast.place, s32[32,2]{1,0:T(8,128)S(1)} %slice.36.ends, s32[32,128]{1,0:T(8,128)S(1)} %bitcast.28, bf16[4,128,512]{2,1,0:T(8,128)(2,1)S(1)} %slice_bitcast_fusion.q, ...), custom_call_target="tpu_custom_call" | custom-call | flops 1000000000 | bytes 2000000 | tf_op jit(solution)/shard_map/forward_far/pallas_call | solution.py:208
  59.8 2.3 %collective-permute-start.8 = (bf16[256,512]{1,0:T(8,128)(2,1)S(1)}, bf16[256,512]{1,0:T(8,128)(2,1)}, u32[]{:S(2)}, u32[]{:S(2)}) collective-permute-start(bf16[256,512]{1,0:T(8,128)(2,1)S(1)} %get-tuple-element.21), channel_id=1, source_target_pairs={{0,1},{1,0},{2,3},{3,2},{4,5},{5,4},{6,7},{7,6},{8,9},{9,8},{10,11... | collective-permute-start | bytes 786440 | tf_op jit(solution)/shard_map/ppermute | solution.py:45
  64.5 15.6 %all-gather.1 = bf16[512,512]{1,0:T(8,128)(2,1)S(1)} all-gather(bf16[256,512]{1,0:T(8,128)(2,1)S(1)} %get-tuple-element.30), channel_id=3, replica_groups={{0,2},{1,3},{4,6},{5,7},{8,10},{9,11},{12,14},{13,15},{16,18},{17,19},{..., dimensions={0}, use_global_device_ids=true | all-gather | bytes 786432 | tf_op jit(solution)/shard_map/all_gather | solution.py:270
  81.1 2.8 %all-gather.2 = bf16[544,512]{1,0:T(8,128)(2,1)S(1)} all-gather(bf16[272,512]{1,0:T(8,128)(2,1)S(1)} %get-tuple-element.23), channel_id=4, replica_groups={{0,1},{2,3},{4,5},{6,7},{8,9},{10,11},{12,13},{14,15},{16,17},{18,19},{..., dimensions={0}, use_global_device_ids=true | all-gather | bytes 835584 | tf_op jit(solution)/shard_map/all_gather | solution.py:278
  83.9 13.0 %backward_tile.1 = (f32[256,512]{1,0:T(8,128)S(1)}, bf16[256,512]{1,0:T(8,128)(2,1)S(1)}, bf16[16,512]{1,0:T(8,128)(2,1)S(1)}, bf16[2048,512]{1,0:T(8,128)(2,1)}) custom-call(s32[1]{0:T(128)} %bitcast.place, s32[32,2]{1,0:T(8,128)S(1)} %slice.36.ends, s32[32,128]{1,0:T(8,128)S(1)} %bitcast.29, bf16[4,128,512]{2,1,0:T(8,128)(2,1)S(1)} %slice_bitcast_fusion.q, ...), custom_call_target="tpu_custom_call" | custom-call | flops 4499999744 | bytes 9000000 | tf_op jit(solution)/shard_map/backward_tile/pallas_call | solution.py:208
  96.9 2.3 %collective-permute-start.9 = (bf16[256,512]{1,0:T(8,128)(2,1)S(1)}, bf16[256,512]{1,0:T(8,128)(2,1)S(1)}, u32[]{:S(2)}, u32[]{:S(2)}) collective-permute-start(bf16[256,512]{1,0:T(8,128)(2,1)S(1)} %get-tuple-element.26), channel_id=1, source_target_pairs={{0,1},{1,0},{2,3},{3,2},{4,5},{5,4},{6,7},{7,6},{8,9},{9,8},{10,11... | collective-permute-start | bytes 786440 | tf_op jit(solution)/shard_map/ppermute | solution.py:45
  100.5 15.5 %all-gather.3 = bf16[288,512]{1,0:T(8,128)(2,1)S(1)} all-gather(bf16[144,512]{1,0:T(8,128)(2,1)S(1)} %pad_maximum_fusion.2), channel_id=5, replica_groups={{0,2},{1,3},{4,6},{5,7},{8,10},{9,11},{12,14},{13,15},{16,18},{17,19},{..., dimensions={0}, use_global_device_ids=true | all-gather | bytes 442368 | tf_op jit(solution)/shard_map/all_gather | solution.py:292
  116.6 9.2 %all-to-all-start = ((f32[16,1,512]{2,1,0:T(1,128)}), f32[16,1,512]{2,1,0:T(1,128)S(1)}, u32[]{:S(2)}, u32[]{:S(2)}) async-start(f32[16,1,512]{2,1,0:T(1,128)} %broadcast_in_dim.33), calls=%async_computation.1 | async-start | bytes 65536 | tf_op jit(solution)/shard_map/all_to_all | solution.py:50
  125.9 7.0 %all-to-all-done = f32[16,1,512]{2,1,0:T(1,128)S(1)} async-done(((f32[16,1,512]{2,1,0:T(1,128)}), f32[16,1,512]{2,1,0:T(1,128)S(1)}, u32[]{:S(2)}, u32[]{:S(2)}) %all-to-all-start) | async-done | bytes 32800 | tf_op jit(solution)/shard_map/all_to_all | solution.py:50
  133.5 4.1 %all-to-all-start.1 = ((f32[8,1,512]{2,1,0:T(1,128)}), f32[8,1,512]{2,1,0:T(1,128)S(1)}, u32[]{:S(2)}, u32[]{:S(2)}) async-start(f32[8,1,512]{2,1,0:T(1,128)} %broadcast_in_dim.34), calls=%async_computation.2 | async-start | bytes 32768 | tf_op jit(solution)/shard_map/all_to_all | solution.py:50
  138.3 6.0 %all-to-all-done.1 = f32[8,1,512]{2,1,0:T(1,128)S(1)} async-done(((f32[8,1,512]{2,1,0:T(1,128)}), f32[8,1,512]{2,1,0:T(1,128)S(1)}, u32[]{:S(2)}, u32[]{:S(2)}) %all-to-all-start.1) | async-done | bytes 16416 | tf_op jit(solution)/shard_map/all_to_all | solution.py:50
  144.9 1.7 %slice_bitcast_fusion.1 = (bf16[1,128,512]{2,1,0:T(8,128)(2,1)}, bf16[1,128,512]{2,1,0:T(8,128)(2,1)}) fusion(bf16[256,512]{1,0:T(8,128)(2,1)} %reduce-scatter.2.cloned.1.call-done), kind=kLoop, calls=%fused_computation.11 | loop fusion | bytes 524288 | tf_op jit(solution)/shard_map/broadcast_in_dim | solution.py:306
  (45 shorter events, 12.5 us)
Async XLA Ops:
  7.2 45.7 %copy-start.2 = (s32[1,4096]{1,0:T(1,128)S(1)}, s32[1,4096]{1,0:T(1,128)}, u32[]{:S(2)}) copy-start(s32[1,4096]{1,0:T(1,128)} %param.12) | copy-start | bytes 49156
  7.2 44.6 %all-gather.6.cloned.1.call-start = ((), (), s32[]{:S(2)}) async-start(), calls=%async_computation.4 | async-start | bytes 1310720 | tf_op jit(solution)/shard_map/all_gather | solution.py:235
  10.9 134.0 %reduce-scatter.2.cloned.1.call-start = ((), (), s32[]{:S(2)}) async-start(), calls=%async_computation.3 | async-start | bytes 2359296 | tf_op jit(solution)/shard_map/reduce_scatter | solution.py:289
  11.0 9.2 %collective-permute-start.1 = (bf16[2,128,512]{2,1,0:T(8,128)(2,1)S(1)}, bf16[2,128,512]{2,1,0:T(8,128)(2,1)S(1)}, u32[]{:S(2)}, u32[]{:S(2)}) collective-permute-start(bf16[2,128,512]{2,1,0:T(8,128)(2,1)S(1)} %pad_maximum_fusion.own.rest_0_), channel_id=1, source_target_pairs={{0,28},{1,29},{2,30},{3,31},{4,0},{5,1},{6,2},{7,3},{8,4},{9,5},{1... | collective-permute-start | bytes 786440 | tf_op jit(solution)/shard_map/ppermute | solution.py:41
  16.9 8.3 %collective-permute-start = (bf16[2,128,512]{2,1,0:T(8,128)(2,1)S(1)}, bf16[2,128,512]{2,1,0:T(8,128)(2,1)S(1)}, u32[]{:S(2)}, u32[]{:S(2)}) collective-permute-start(bf16[2,128,512]{2,1,0:T(8,128)(2,1)S(1)} %pad_maximum_fusion.own.rest_0_), channel_id=1, source_target_pairs={{0,4},{1,5},{2,6},{3,7},{4,8},{5,9},{6,10},{7,11},{8,12},{9,13},{1... | collective-permute-start | bytes 786440 | tf_op jit(solution)/shard_map/ppermute | solution.py:41
  20.2 8.3 %collective-permute-start.2 = (bf16[2,128,512]{2,1,0:T(8,128)(2,1)S(1)}, bf16[2,128,512]{2,1,0:T(8,128)(2,1)S(1)}, u32[]{:S(2)}, u32[]{:S(2)}) collective-permute-start(bf16[2,128,512]{2,1,0:T(8,128)(2,1)S(1)} %collective-permute-done.1.next_.rest_2_), channel_id=1, source_target_pairs={{0,28},{1,29},{2,30},{3,31},{4,0},{5,1},{6,2},{7,3},{8,4},{9,5},{1... | collective-permute-start | bytes 786440 | tf_op jit(solution)/shard_map/ppermute | solution.py:41
  25.2 9.6 %collective-permute-start.3 = (bf16[2,128,512]{2,1,0:T(8,128)(2,1)S(1)}, bf16[2,128,512]{2,1,0:T(8,128)(2,1)S(1)}, u32[]{:S(2)}, u32[]{:S(2)}) collective-permute-start(bf16[2,128,512]{2,1,0:T(8,128)(2,1)S(1)} %collective-permute-done.prev.rest_1_), channel_id=1, source_target_pairs={{0,4},{1,5},{2,6},{3,7},{4,8},{5,9},{6,10},{7,11},{8,12},{9,13},{1... | collective-permute-start | bytes 786440 | tf_op jit(solution)/shard_map/ppermute | solution.py:41
  28.5 28.1 %collective-permute-start.7 = (bf16[2,64,512]{2,1,0:T(8,128)(2,1)S(1)}, bf16[2,64,512]{2,1,0:T(8,128)(2,1)S(1)}, u32[]{:S(2)}, u32[]{:S(2)}) collective-permute-start(bf16[2,64,512]{2,1,0:T(8,128)(2,1)S(1)} %slice.49), channel_id=1, source_target_pairs={{0,24},{1,25},{2,26},{3,27},{4,28},{5,29},{6,30},{7,31},{8,0},{9,1... | collective-permute-start | bytes 393224 | tf_op jit(solution)/shard_map/ppermute | solution.py:41
  34.8 21.8 %collective-permute-start.6 = (bf16[2,64,512]{2,1,0:T(8,128)(2,1)S(1)}, bf16[2,64,512]{2,1,0:T(8,128)(2,1)S(1)}, u32[]{:S(2)}, u32[]{:S(2)}) collective-permute-start(bf16[2,64,512]{2,1,0:T(8,128)(2,1)S(1)} %slice.48), channel_id=1, source_target_pairs={{0,8},{1,9},{2,10},{3,11},{4,12},{5,13},{6,14},{7,15},{8,16},{9,17... | collective-permute-start | bytes 393224 | tf_op jit(solution)/shard_map/ppermute | solution.py:41
  36.7 19.9 %collective-permute-start.5 = (bf16[2,128,512]{2,1,0:T(8,128)(2,1)S(1)}, bf16[2,128,512]{2,1,0:T(8,128)(2,1)S(1)}, u32[]{:S(2)}, u32[]{:S(2)}) collective-permute-start(bf16[2,128,512]{2,1,0:T(8,128)(2,1)S(1)} %collective-permute-done.2.next2.rest_4_), channel_id=1, source_target_pairs={{0,28},{1,29},{2,30},{3,31},{4,0},{5,1},{6,2},{7,3},{8,4},{9,5},{1... | collective-permute-start | bytes 786440 | tf_op jit(solution)/shard_map/ppermute | solution.py:41
  41.0 15.6 %collective-permute-start.4 = (bf16[2,128,512]{2,1,0:T(8,128)(2,1)S(1)}, bf16[2,128,512]{2,1,0:T(8,128)(2,1)S(1)}, u32[]{:S(2)}, u32[]{:S(2)}) collective-permute-start(bf16[2,128,512]{2,1,0:T(8,128)(2,1)S(1)} %collective-permute-done.3.prev2.rest_3_), channel_id=1, source_target_pairs={{0,4},{1,5},{2,6},{3,7},{4,8},{5,9},{6,10},{7,11},{8,12},{9,13},{1... | collective-permute-start | bytes 786440 | tf_op jit(solution)/shard_map/ppermute | solution.py:41
  59.0 0.7 copy-start.4
  59.8 20.4 %copy-start = (bf16[1,128,512]{2,1,0:T(8,128)(2,1)S(1)}, bf16[1,128,512]{2,1,0:T(8,128)(2,1)}, u32[]{:S(2)}) copy-start(bf16[1,128,512]{2,1,0:T(8,128)(2,1)} %gate.1) | copy-start | bytes 393220
  59.8 20.4 %copy-start.1 = (bf16[1,128,512]{2,1,0:T(8,128)(2,1)S(1)}, bf16[1,128,512]{2,1,0:T(8,128)(2,1)}, u32[]{:S(2)}) copy-start(bf16[1,128,512]{2,1,0:T(8,128)(2,1)} %grad.1) | copy-start | bytes 393220
  59.8 20.4 %copy-start.3 = (f32[512]{0:T(512)S(1)}, f32[512]{0:T(512)}, u32[]{:S(2)}) copy-start(f32[512]{0:T(512)} %param.13) | copy-start | bytes 6148
  59.8 3.7 %collective-permute-start.8 = (bf16[256,512]{1,0:T(8,128)(2,1)S(1)}, bf16[256,512]{1,0:T(8,128)(2,1)}, u32[]{:S(2)}, u32[]{:S(2)}) collective-permute-start(bf16[256,512]{1,0:T(8,128)(2,1)S(1)} %get-tuple-element.21), channel_id=1, source_target_pairs={{0,1},{1,0},{2,3},{3,2},{4,5},{5,4},{6,7},{7,6},{8,9},{9,8},{10,11... | collective-permute-start | bytes 786440 | tf_op jit(solution)/shard_map/ppermute | solution.py:45
  64.5 19.4 %copy-start.5 = (bf16[2,128,512]{2,1,0:T(8,128)(2,1)S(1)}, bf16[2,128,512]{2,1,0:T(8,128)(2,1)}, u32[]{:S(2)}) copy-start(bf16[2,128,512]{2,1,0:T(8,128)(2,1)} %copy-done.4) | copy-start | bytes 786436
  96.9 3.4 %collective-permute-start.9 = (bf16[256,512]{1,0:T(8,128)(2,1)S(1)}, bf16[256,512]{1,0:T(8,128)(2,1)S(1)}, u32[]{:S(2)}, u32[]{:S(2)}) collective-permute-start(bf16[256,512]{1,0:T(8,128)(2,1)S(1)} %get-tuple-element.26), channel_id=1, source_target_pairs={{0,1},{1,0},{2,3},{3,2},{4,5},{5,4},{6,7},{7,6},{8,9},{9,8},{10,11... | collective-permute-start | bytes 786440 | tf_op jit(solution)/shard_map/ppermute | solution.py:45
  116.6 16.2 %all-to-all-start = ((f32[16,1,512]{2,1,0:T(1,128)}), f32[16,1,512]{2,1,0:T(1,128)S(1)}, u32[]{:S(2)}, u32[]{:S(2)}) async-start(f32[16,1,512]{2,1,0:T(1,128)} %broadcast_in_dim.33), calls=%async_computation.1 | async-start | bytes 65536 | tf_op jit(solution)/shard_map/all_to_all | solution.py:50
  133.5 10.8 %all-to-all-start.1 = ((f32[8,1,512]{2,1,0:T(1,128)}), f32[8,1,512]{2,1,0:T(1,128)S(1)}, u32[]{:S(2)}, u32[]{:S(2)}) async-start(f32[8,1,512]{2,1,0:T(1,128)} %broadcast_in_dim.34), calls=%async_computation.2 | async-start | bytes 32768 | tf_op jit(solution)/shard_map/all_to_all | solution.py:50
Sparse Core Ops, SparseCore 0:
  11.0 40.7 all-gather.5
  97.1 43.9 reduce-scatter.1

commit v5 on v4

--- a/solution.py
+++ b/solution.py
@@ -141,7 +141,13 @@
     return lax.rem(place, QUAD) // ZHI
 
 
-def norm_kernel(place, kept, came, gate, grad, product, gain, out, gate_grad, attn_grad):
+def norm_kernel(
+    place, kept, came, gate, grad, gain, gathered, out, gate_grad, attn_grad, product, sem
+):
+    copy = pltpu.make_async_copy(
+        gathered.at[lax.rem(place[0], QUAD) ^ ZHI, 1], product, sem
+    )
+    copy.start()
     g = gain[...]
     other = came.at[1 - z_of(place[0])]
     for i in range(2):
@@ -157,6 +163,7 @@
             gate_grad[0] = (grad_f * normed * g).astype(BF16)
             attn_grad[2 * ROWS :, :] = terms_of(jnp.sum(both * normed, axis=0, keepdims=True))
         else:
+            copy.wait()
             both = product[...].astype(F32)
         ng = both * g
         mean = jnp.mean(normed * ng, axis=1, keepdims=True)
@@ -245,7 +252,6 @@
 
     segs = segment_ids.reshape(CTX, ROWS)
     ends = segs[:, :: ROWS - 1]
-    product = lax.dynamic_index_in_dim(gathered, lax.rem(place, QUAD) ^ ZHI, 0, keepdims=False)[1]
     shared = (place[None], ends, segs, gathered[:, 0])
 
     (begun,) = call(
@@ -266,15 +272,27 @@
         [tile, (TILE, ROWS)],
         us=2,
     )
-    keep = keep + swap(send, CORE).astype(F32)
+    came = lax.all_gather(send, "ctx", axis_index_groups=CORES)
+    keep = keep + lax.dynamic_index_in_dim(came, 1 - place % 2, 0, keepdims=False).astype(F32)
     came = lax.all_gather(keep.astype(BF16), "ctx", axis_index_groups=ZPAIRS)
-    layer_out, gate_grad, attn_grad = call(
+    layer_out, gate_grad, attn_grad = pl.pallas_call(
         norm_kernel,
-        "norm_rows",
-        [(rows, BF16), (rows, BF16), ((2 * ROWS + EXTRA, HD), BF16)],
-        (place[None], keep, came, gate_states, out_grad, product, norm_gain[None, :]),
-        1,
-    )
+        out_shape=(
+            jax.ShapeDtypeStruct(rows, BF16),
+            jax.ShapeDtypeStruct(rows, BF16),
+            jax.ShapeDtypeStruct((2 * ROWS + EXTRA, HD), BF16),
+        ),
+        in_specs=[pl.BlockSpec(memory_space=pltpu.SMEM)]
+        + [pl.BlockSpec(memory_space=pltpu.VMEM)] * 5
+        + [pl.BlockSpec(memory_space=pl.ANY)],
+        out_specs=(pl.BlockSpec(memory_space=pltpu.VMEM),) * 3,
+        scratch_shapes=[pltpu.VMEM((ROWS, HD), BF16), pltpu.SemaphoreType.DMA],
+        compiler_params=pltpu.CompilerParams(vmem_limit_bytes=VMEM_LIMIT),
+        cost_estimate=pl.CostEstimate(
+            flops=500_000_000, bytes_accessed=1_000_000, transcendentals=0
+        ),
+        name="norm_rows",
+    )(place[None], keep, came, gate_states, out_grad, norm_gain[None, :], gathered)
     grads = lax.all_gather(attn_grad, "ctx", axis_index_groups=CORES)
 
     keep, send, extra, dkv = call(

time: 155 us -> 151 us (0.974)
  starting transfers between devices: 47.1 us -> 44 us
  blocking collectives: 33.9 us -> 36.1 us
  local copies, waits for them, and re-layouts: 6.5 us -> 4.88 us
    all_gather x0 -> x1, blocking collectives: none -> 2.31 us  [per_device(): came = lax.all_gather(send, 'ctx', axis_index_groups=CORES)]
    ppermute x2 -> x1, starting transfers between devices: 4.59 us -> 2.28 us  [swap(): return lax.ppermute(value, 'ctx', [(i, i ^ flip) for i in range(CTX)])]
    pallas_call x4 -> x3, Pallas kernels: 20 us -> 19.1 us  [call(): pl.pallas_call(kernel, out_shape=tuple((jax.ShapeDtypeStruct(shape, dtype...]
  transfers between devices with their start and end apart: 14 -> 13, of which waited for: 7 -> 6; matrix products, arithmetic and copies ran while one was open for 4% -> 3% of each run, Pallas kernels for 2% -> 2%
where the time goes in v5:
time: 151 us; the launch traced here: 150 us
  starting transfers between devices  44 us (29%)
  blocking collectives  36.1 us (24%)
  waiting for transfers between devices  24.9 us (16%)
  Pallas kernels  20.3 us (13%)
  between operations  14.4 us (10%)
  other arithmetic  5.17 us (3%)
  local copies, waits for them, and re-layouts  4.88 us (3%)
    ppermute x8, starting transfers between devices, along(): lax.ppermute(value, 'ctx', [(i, (i + step * QUAD) % CTX) for i in range(C...  29.1 us
    pallas_call x3, Pallas kernels, call(): pl.pallas_call(kernel, out_shape=tuple((jax.ShapeDtypeStruct(shape, dtype...  19.1 us
    all_gather x1, blocking collectives, per_device(): came = lax.all_gather(keep.astype(BF16), 'ctx', axis_index_groups=ZPAIRS)  15.5 us
    all_gather x1, blocking collectives, per_device(): came = lax.all_gather(send, 'ctx', axis_index_groups=ZPAIRS)  15.5 us
    all_to_all x2, waiting for transfers between devices, everywhere(): lax.all_to_all(value, axis, 0, 0, tiled=True, axis_index_groups=groups)  12.9 us
    all_to_all x2, starting transfers between devices, everywhere(): lax.all_to_all(value, axis, 0, 0, tiled=True, axis_index_groups=groups)  12.6 us
    all_gather x1, waiting for transfers between devices, per_device(): lax.all_gather(jnp.concatenate([first, product], axis=0), 'ctx', axis_ind...  8.89 us
  transfers between devices with their start and end apart: 13, of which 6 were waited for; matrix products, arithmetic and copies ran while one was open for 3% of the time, Pallas kernels for 2%

profile of v5, /device:TPU:1, one launch (start us, length us, event | category | flops | bytes accessed | tf_op | source)
XLA Modules:
  0.0 149.8 jit_solution(10751569219219513048)
XLA Ops:
  9.2 1.6 %pad_maximum_fusion.1 = bf16[2,128,512]{2,1,0:T(8,128)(2,1)} fusion(bf16[1,128,512]{2,1,0:T(8,128)(2,1)S(1)} %multiply_convert_fusion, bf16[1,128,512]{2,1,0:T(8,128)(2,1)} %param.7), kind=kLoop, calls=%fused_computation.7 | loop fusion | flops 131072 | bytes 524288 | tf_op jit(solution)/shard_map/concatenate | solution.py:243
  11.0 5.9 %collective-permute-start.1 = (bf16[2,128,512]{2,1,0:T(8,128)(2,1)S(1)}, bf16[2,128,512]{2,1,0:T(8,128)(2,1)S(1)}, u32[]{:S(2)}, u32[]{:S(2)}) collective-permute-start(bf16[2,128,512]{2,1,0:T(8,128)(2,1)S(1)} %pad_maximum_fusion.own.rest_0_), channel_id=1, source_target_pairs={{0,28},{1,29},{2,30},{3,31},{4,0},{5,1},{6,2},{7,3},{8,4},{9,5},{1... | collective-permute-start | bytes 786440 | tf_op jit(solution)/shard_map/ppermute | solution.py:41
  16.9 1.9 %collective-permute-start = (bf16[2,128,512]{2,1,0:T(8,128)(2,1)S(1)}, bf16[2,128,512]{2,1,0:T(8,128)(2,1)S(1)}, u32[]{:S(2)}, u32[]{:S(2)}) collective-permute-start(bf16[2,128,512]{2,1,0:T(8,128)(2,1)S(1)} %pad_maximum_fusion.own.rest_0_), channel_id=1, source_target_pairs={{0,4},{1,5},{2,6},{3,7},{4,8},{5,9},{6,10},{7,11},{8,12},{9,13},{1... | collective-permute-start | bytes 786440 | tf_op jit(solution)/shard_map/ppermute | solution.py:41
  18.8 1.4 collective-permute-done.1.next_.rest_2_
  20.2 5.0 %collective-permute-start.2 = (bf16[2,128,512]{2,1,0:T(8,128)(2,1)S(1)}, bf16[2,128,512]{2,1,0:T(8,128)(2,1)S(1)}, u32[]{:S(2)}, u32[]{:S(2)}) collective-permute-start(bf16[2,128,512]{2,1,0:T(8,128)(2,1)S(1)} %collective-permute-done.1.next_.rest_2_), channel_id=1, source_target_pairs={{0,28},{1,29},{2,30},{3,31},{4,0},{5,1},{6,2},{7,3},{8,4},{9,5},{1... | collective-permute-start | bytes 786440 | tf_op jit(solution)/shard_map/ppermute | solution.py:41
  25.2 1.9 %collective-permute-start.3 = (bf16[2,128,512]{2,1,0:T(8,128)(2,1)S(1)}, bf16[2,128,512]{2,1,0:T(8,128)(2,1)S(1)}, u32[]{:S(2)}, u32[]{:S(2)}) collective-permute-start(bf16[2,128,512]{2,1,0:T(8,128)(2,1)S(1)} %collective-permute-done.prev.rest_1_), channel_id=1, source_target_pairs={{0,4},{1,5},{2,6},{3,7},{4,8},{5,9},{6,10},{7,11},{8,12},{9,13},{1... | collective-permute-start | bytes 786440 | tf_op jit(solution)/shard_map/ppermute | solution.py:41
  28.5 6.2 %collective-permute-start.7 = (bf16[2,64,512]{2,1,0:T(8,128)(2,1)S(1)}, bf16[2,64,512]{2,1,0:T(8,128)(2,1)S(1)}, u32[]{:S(2)}, u32[]{:S(2)}) collective-permute-start(bf16[2,64,512]{2,1,0:T(8,128)(2,1)S(1)} %slice.44), channel_id=1, source_target_pairs={{0,24},{1,25},{2,26},{3,27},{4,28},{5,29},{6,30},{7,31},{8,0},{9,1... | collective-permute-start | bytes 393224 | tf_op jit(solution)/shard_map/ppermute | solution.py:41
  34.8 1.9 %collective-permute-start.6 = (bf16[2,64,512]{2,1,0:T(8,128)(2,1)S(1)}, bf16[2,64,512]{2,1,0:T(8,128)(2,1)S(1)}, u32[]{:S(2)}, u32[]{:S(2)}) collective-permute-start(bf16[2,64,512]{2,1,0:T(8,128)(2,1)S(1)} %slice.43), channel_id=1, source_target_pairs={{0,8},{1,9},{2,10},{3,11},{4,12},{5,13},{6,14},{7,15},{8,16},{9,17... | collective-permute-start | bytes 393224 | tf_op jit(solution)/shard_map/ppermute | solution.py:41
  36.7 4.2 %collective-permute-start.5 = (bf16[2,128,512]{2,1,0:T(8,128)(2,1)S(1)}, bf16[2,128,512]{2,1,0:T(8,128)(2,1)S(1)}, u32[]{:S(2)}, u32[]{:S(2)}) collective-permute-start(bf16[2,128,512]{2,1,0:T(8,128)(2,1)S(1)} %collective-permute-done.2.next2.rest_4_), channel_id=1, source_target_pairs={{0,28},{1,29},{2,30},{3,31},{4,0},{5,1},{6,2},{7,3},{8,4},{9,5},{1... | collective-permute-start | bytes 786440 | tf_op jit(solution)/shard_map/ppermute | solution.py:41
  41.0 1.9 %collective-permute-start.4 = (bf16[2,128,512]{2,1,0:T(8,128)(2,1)S(1)}, bf16[2,128,512]{2,1,0:T(8,128)(2,1)S(1)}, u32[]{:S(2)}, u32[]{:S(2)}) collective-permute-start(bf16[2,128,512]{2,1,0:T(8,128)(2,1)S(1)} %collective-permute-done.3.prev2.rest_3_), channel_id=1, source_target_pairs={{0,4},{1,5},{2,6},{3,7},{4,8},{5,9},{6,10},{7,11},{8,12},{9,13},{1... | collective-permute-start | bytes 786440 | tf_op jit(solution)/shard_map/ppermute | solution.py:41
  42.9 8.9 %all-gather.7.cloned.1.call-done = bf16[8,128,512]{2,1,0:T(8,128)(2,1)} async-done(((bf16[2,128,512]{2,1,0:T(8,128)(2,1)}), bf16[8,128,512]{2,1,0:T(8,128)(2,1)}) %all-gather.7.cloned.1.call-update) | async-done | bytes 1048592 | tf_op jit(solution)/shard_map/all_gather | solution.py:242
  52.9 3.7 %forward_near.1.begun = f32[512,512]{1,0:T(8,128)S(1)} custom-call(s32[1]{0:T(128)} %bitcast.place, s32[32,2]{1,0:T(8,128)S(1)} %slice.32.ends, s32[32,128]{1,0:T(8,128)S(1)} %bitcast.32, bf16[4,128,512]{2,1,0:T(8,128)(2,1)S(1)} %slice_bitcast_fusion.q, bf16[2,128,512]{2,1,0:T(8,128)(2,1)S(1)} %pad_maximum_fusion.own.rest_0_, ...), custom_call_target="tpu_custom_call" | custom-call | flops 1000000000 | bytes 2000000 | tf_op jit(solution)/shard_map/forward_near/pallas_call | solution.py:215
  56.6 2.4 %forward_far.1 = (f32[256,512]{1,0:T(8,128)S(1)}, bf16[256,512]{1,0:T(8,128)(2,1)S(1)}, bf16[2,128,512]{2,1,0:T(8,128)(2,1)S(1)}) custom-call(s32[1]{0:T(128)} %bitcast.place, s32[32,2]{1,0:T(8,128)S(1)} %slice.32.ends, s32[32,128]{1,0:T(8,128)S(1)} %bitcast.33, bf16[4,128,512]{2,1,0:T(8,128)(2,1)S(1)} %slice_bitcast_fusion.q, ...), custom_call_target="tpu_custom_call" | custom-call | flops 1000000000 | bytes 2000000 | tf_op jit(solution)/shard_map/forward_far/pallas_call | solution.py:215
  59.1 2.3 %all-gather.1 = bf16[512,512]{1,0:T(8,128)(2,1)S(1)} all-gather(bf16[256,512]{1,0:T(8,128)(2,1)S(1)} %get-tuple-element.21), channel_id=3, replica_groups={{0,1},{2,3},{4,5},{6,7},{8,9},{10,11},{12,13},{14,15},{16,17},{18,19},{..., dimensions={0}, use_global_device_ids=true | all-gather | bytes 786432 | tf_op jit(solution)/shard_map/all_gather | solution.py:275
  61.5 15.5 %all-gather.2 = bf16[512,512]{1,0:T(8,128)(2,1)S(1)} all-gather(bf16[256,512]{1,0:T(8,128)(2,1)S(1)} %get-tuple-element.30), channel_id=4, replica_groups={{0,2},{1,3},{4,6},{5,7},{8,10},{9,11},{12,14},{13,15},{16,18},{17,19},{..., dimensions={0}, use_global_device_ids=true | all-gather | bytes 786432 | tf_op jit(solution)/shard_map/all_gather | solution.py:277
  78.2 2.8 %all-gather.3 = bf16[544,512]{1,0:T(8,128)(2,1)S(1)} all-gather(bf16[272,512]{1,0:T(8,128)(2,1)S(1)} %get-tuple-element.23), channel_id=5, replica_groups={{0,1},{2,3},{4,5},{6,7},{8,9},{10,11},{12,13},{14,15},{16,17},{18,19},{..., dimensions={0}, use_global_device_ids=true | all-gather | bytes 835584 | tf_op jit(solution)/shard_map/all_gather | solution.py:296
  81.1 13.0 %backward_tile.1 = (f32[256,512]{1,0:T(8,128)S(1)}, bf16[256,512]{1,0:T(8,128)(2,1)S(1)}, bf16[16,512]{1,0:T(8,128)(2,1)S(1)}, bf16[2048,512]{1,0:T(8,128)(2,1)}) custom-call(s32[1]{0:T(128)} %bitcast.place, s32[32,2]{1,0:T(8,128)S(1)} %slice.32.ends, s32[32,128]{1,0:T(8,128)S(1)} %bitcast.34, bf16[4,128,512]{2,1,0:T(8,128)(2,1)S(1)} %slice_bitcast_fusion.q, ...), custom_call_target="tpu_custom_call" | custom-call | flops 4499999744 | bytes 9000000 | tf_op jit(solution)/shard_map/backward_tile/pallas_call | solution.py:215
  94.1 2.3 %collective-permute-start.8 = (bf16[256,512]{1,0:T(8,128)(2,1)S(1)}, bf16[256,512]{1,0:T(8,128)(2,1)S(1)}, u32[]{:S(2)}, u32[]{:S(2)}) collective-permute-start(bf16[256,512]{1,0:T(8,128)(2,1)S(1)} %get-tuple-element.26), channel_id=1, source_target_pairs={{0,1},{1,0},{2,3},{3,2},{4,5},{5,4},{6,7},{7,6},{8,9},{9,8},{10,11... | collective-permute-start | bytes 786440 | tf_op jit(solution)/shard_map/ppermute | solution.py:45
  97.6 15.5 %all-gather.4 = bf16[288,512]{1,0:T(8,128)(2,1)S(1)} all-gather(bf16[144,512]{1,0:T(8,128)(2,1)S(1)} %pad_maximum_fusion.2), channel_id=6, replica_groups={{0,2},{1,3},{4,6},{5,7},{8,10},{9,11},{12,14},{13,15},{16,18},{17,19},{..., dimensions={0}, use_global_device_ids=true | all-gather | bytes 442368 | tf_op jit(solution)/shard_map/all_gather | solution.py:310
  113.8 9.2 %all-to-all-start = ((f32[16,1,512]{2,1,0:T(1,128)}), f32[16,1,512]{2,1,0:T(1,128)S(1)}, u32[]{:S(2)}, u32[]{:S(2)}) async-start(f32[16,1,512]{2,1,0:T(1,128)} %broadcast_in_dim.33), calls=%async_computation.1 | async-start | bytes 65536 | tf_op jit(solution)/shard_map/all_to_all | solution.py:50
  123.0 7.0 %all-to-all-done = f32[16,1,512]{2,1,0:T(1,128)S(1)} async-done(((f32[16,1,512]{2,1,0:T(1,128)}), f32[16,1,512]{2,1,0:T(1,128)S(1)}, u32[]{:S(2)}, u32[]{:S(2)}) %all-to-all-start) | async-done | bytes 32800 | tf_op jit(solution)/shard_map/all_to_all | solution.py:50
  130.7 3.3 %all-to-all-start.1 = ((f32[8,1,512]{2,1,0:T(1,128)}), f32[8,1,512]{2,1,0:T(1,128)S(1)}, u32[]{:S(2)}, u32[]{:S(2)}) async-start(f32[8,1,512]{2,1,0:T(1,128)} %broadcast_in_dim.34), calls=%async_computation.2 | async-start | bytes 32768 | tf_op jit(solution)/shard_map/all_to_all | solution.py:50
  134.7 5.9 %all-to-all-done.1 = f32[8,1,512]{2,1,0:T(1,128)S(1)} async-done(((f32[8,1,512]{2,1,0:T(1,128)}), f32[8,1,512]{2,1,0:T(1,128)S(1)}, u32[]{:S(2)}, u32[]{:S(2)}) %all-to-all-start.1) | async-done | bytes 16416 | tf_op jit(solution)/shard_map/all_to_all | solution.py:50
  141.2 1.7 %slice_bitcast_fusion.1 = (bf16[1,128,512]{2,1,0:T(8,128)(2,1)}, bf16[1,128,512]{2,1,0:T(8,128)(2,1)}) fusion(bf16[256,512]{1,0:T(8,128)(2,1)} %reduce-scatter.2.cloned.1.call-done), kind=kLoop, calls=%fused_computation.11 | loop fusion | bytes 524288 | tf_op jit(solution)/shard_map/broadcast_in_dim | solution.py:324
  (41 shorter events, 9.8 us)
Async XLA Ops:
  7.2 45.7 %copy-start.3 = (s32[1,4096]{1,0:T(1,128)S(1)}, s32[1,4096]{1,0:T(1,128)}, u32[]{:S(2)}) copy-start(s32[1,4096]{1,0:T(1,128)} %param.12) | copy-start | bytes 49156
  7.2 44.6 %all-gather.7.cloned.1.call-start = ((), (), s32[]{:S(2)}) async-start(), calls=%async_computation.4 | async-start | bytes 1310720 | tf_op jit(solution)/shard_map/all_gather | solution.py:242
  10.9 130.3 %reduce-scatter.2.cloned.1.call-start = ((), (), s32[]{:S(2)}) async-start(), calls=%async_computation.3 | async-start | bytes 2359296 | tf_op jit(solution)/shard_map/reduce_scatter | solution.py:307
  11.0 9.2 %collective-permute-start.1 = (bf16[2,128,512]{2,1,0:T(8,128)(2,1)S(1)}, bf16[2,128,512]{2,1,0:T(8,128)(2,1)S(1)}, u32[]{:S(2)}, u32[]{:S(2)}) collective-permute-start(bf16[2,128,512]{2,1,0:T(8,128)(2,1)S(1)} %pad_maximum_fusion.own.rest_0_), channel_id=1, source_target_pairs={{0,28},{1,29},{2,30},{3,31},{4,0},{5,1},{6,2},{7,3},{8,4},{9,5},{1... | collective-permute-start | bytes 786440 | tf_op jit(solution)/shard_map/ppermute | solution.py:41
  16.9 8.3 %collective-permute-start = (bf16[2,128,512]{2,1,0:T(8,128)(2,1)S(1)}, bf16[2,128,512]{2,1,0:T(8,128)(2,1)S(1)}, u32[]{:S(2)}, u32[]{:S(2)}) collective-permute-start(bf16[2,128,512]{2,1,0:T(8,128)(2,1)S(1)} %pad_maximum_fusion.own.rest_0_), channel_id=1, source_target_pairs={{0,4},{1,5},{2,6},{3,7},{4,8},{5,9},{6,10},{7,11},{8,12},{9,13},{1... | collective-permute-start | bytes 786440 | tf_op jit(solution)/shard_map/ppermute | solution.py:41
  20.2 8.3 %collective-permute-start.2 = (bf16[2,128,512]{2,1,0:T(8,128)(2,1)S(1)}, bf16[2,128,512]{2,1,0:T(8,128)(2,1)S(1)}, u32[]{:S(2)}, u32[]{:S(2)}) collective-permute-start(bf16[2,128,512]{2,1,0:T(8,128)(2,1)S(1)} %collective-permute-done.1.next_.rest_2_), channel_id=1, source_target_pairs={{0,28},{1,29},{2,30},{3,31},{4,0},{5,1},{6,2},{7,3},{8,4},{9,5},{1... | collective-permute-start | bytes 786440 | tf_op jit(solution)/shard_map/ppermute | solution.py:41
  25.2 9.6 %collective-permute-start.3 = (bf16[2,128,512]{2,1,0:T(8,128)(2,1)S(1)}, bf16[2,128,512]{2,1,0:T(8,128)(2,1)S(1)}, u32[]{:S(2)}, u32[]{:S(2)}) collective-permute-start(bf16[2,128,512]{2,1,0:T(8,128)(2,1)S(1)} %collective-permute-done.prev.rest_1_), channel_id=1, source_target_pairs={{0,4},{1,5},{2,6},{3,7},{4,8},{5,9},{6,10},{7,11},{8,12},{9,13},{1... | collective-permute-start | bytes 786440 | tf_op jit(solution)/shard_map/ppermute | solution.py:41
  28.5 28.1 %collective-permute-start.7 = (bf16[2,64,512]{2,1,0:T(8,128)(2,1)S(1)}, bf16[2,64,512]{2,1,0:T(8,128)(2,1)S(1)}, u32[]{:S(2)}, u32[]{:S(2)}) collective-permute-start(bf16[2,64,512]{2,1,0:T(8,128)(2,1)S(1)} %slice.44), channel_id=1, source_target_pairs={{0,24},{1,25},{2,26},{3,27},{4,28},{5,29},{6,30},{7,31},{8,0},{9,1... | collective-permute-start | bytes 393224 | tf_op jit(solution)/shard_map/ppermute | solution.py:41
  34.8 21.8 %collective-permute-start.6 = (bf16[2,64,512]{2,1,0:T(8,128)(2,1)S(1)}, bf16[2,64,512]{2,1,0:T(8,128)(2,1)S(1)}, u32[]{:S(2)}, u32[]{:S(2)}) collective-permute-start(bf16[2,64,512]{2,1,0:T(8,128)(2,1)S(1)} %slice.43), channel_id=1, source_target_pairs={{0,8},{1,9},{2,10},{3,11},{4,12},{5,13},{6,14},{7,15},{8,16},{9,17... | collective-permute-start | bytes 393224 | tf_op jit(solution)/shard_map/ppermute | solution.py:41
  36.7 19.9 %collective-permute-start.5 = (bf16[2,128,512]{2,1,0:T(8,128)(2,1)S(1)}, bf16[2,128,512]{2,1,0:T(8,128)(2,1)S(1)}, u32[]{:S(2)}, u32[]{:S(2)}) collective-permute-start(bf16[2,128,512]{2,1,0:T(8,128)(2,1)S(1)} %collective-permute-done.2.next2.rest_4_), channel_id=1, source_target_pairs={{0,28},{1,29},{2,30},{3,31},{4,0},{5,1},{6,2},{7,3},{8,4},{9,5},{1... | collective-permute-start | bytes 786440 | tf_op jit(solution)/shard_map/ppermute | solution.py:41
  41.0 15.6 %collective-permute-start.4 = (bf16[2,128,512]{2,1,0:T(8,128)(2,1)S(1)}, bf16[2,128,512]{2,1,0:T(8,128)(2,1)S(1)}, u32[]{:S(2)}, u32[]{:S(2)}) collective-permute-start(bf16[2,128,512]{2,1,0:T(8,128)(2,1)S(1)} %collective-permute-done.3.prev2.rest_3_), channel_id=1, source_target_pairs={{0,4},{1,5},{2,6},{3,7},{4,8},{5,9},{6,10},{7,11},{8,12},{9,13},{1... | collective-permute-start | bytes 786440 | tf_op jit(solution)/shard_map/ppermute | solution.py:41
  59.0 18.0 %copy-start = (bf16[8,128,512]{2,1,0:T(8,128)(2,1)S(1)}, bf16[8,128,512]{2,1,0:T(8,128)(2,1)}, u32[]{:S(2)}) copy-start(bf16[8,128,512]{2,1,0:T(8,128)(2,1)} %all-gather.7.cloned.1.call-done) | copy-start | bytes 3145732
  59.0 18.0 %copy-start.1 = (bf16[1,128,512]{2,1,0:T(8,128)(2,1)S(1)}, bf16[1,128,512]{2,1,0:T(8,128)(2,1)}, u32[]{:S(2)}) copy-start(bf16[1,128,512]{2,1,0:T(8,128)(2,1)} %gate.1) | copy-start | bytes 393220
  59.1 17.9 %copy-start.2 = (bf16[1,128,512]{2,1,0:T(8,128)(2,1)S(1)}, bf16[1,128,512]{2,1,0:T(8,128)(2,1)}, u32[]{:S(2)}) copy-start(bf16[1,128,512]{2,1,0:T(8,128)(2,1)} %grad.1) | copy-start | bytes 393220
  59.1 17.9 %copy-start.4 = (f32[512]{0:T(512)S(1)}, f32[512]{0:T(512)}, u32[]{:S(2)}) copy-start(f32[512]{0:T(512)} %param.13) | copy-start | bytes 6148
  94.1 3.4 %collective-permute-start.8 = (bf16[256,512]{1,0:T(8,128)(2,1)S(1)}, bf16[256,512]{1,0:T(8,128)(2,1)S(1)}, u32[]{:S(2)}, u32[]{:S(2)}) collective-permute-start(bf16[256,512]{1,0:T(8,128)(2,1)S(1)} %get-tuple-element.26), channel_id=1, source_target_pairs={{0,1},{1,0},{2,3},{3,2},{4,5},{5,4},{6,7},{7,6},{8,9},{9,8},{10,11... | collective-permute-start | bytes 786440 | tf_op jit(solution)/shard_map/ppermute | solution.py:45
  113.8 16.2 %all-to-all-start = ((f32[16,1,512]{2,1,0:T(1,128)}), f32[16,1,512]{2,1,0:T(1,128)S(1)}, u32[]{:S(2)}, u32[]{:S(2)}) async-start(f32[16,1,512]{2,1,0:T(1,128)} %broadcast_in_dim.33), calls=%async_computation.1 | async-start | bytes 65536 | tf_op jit(solution)/shard_map/all_to_all | solution.py:50
  130.7 10.0 %all-to-all-start.1 = ((f32[8,1,512]{2,1,0:T(1,128)}), f32[8,1,512]{2,1,0:T(1,128)S(1)}, u32[]{:S(2)}, u32[]{:S(2)}) async-start(f32[8,1,512]{2,1,0:T(1,128)} %broadcast_in_dim.34), calls=%async_computation.2 | async-start | bytes 32768 | tf_op jit(solution)/shard_map/all_to_all | solution.py:50
Sparse Core Ops, SparseCore 0:
  11.0 40.7 all-gather.6
  94.2 43.1 reduce-scatter.1

commit v6 on v5

--- a/solution.py
+++ b/solution.py
@@ -171,7 +171,8 @@
 
 
 def backward_kernel(place, ends, segs, q, da, *rest):
-    kv, (keep, send, extra, dkv, acc, dk, dv, qseg) = rest[:RING], rest[RING:]
+    kv, (keep, send, extra, dkv, acc, dk, dv, qseg, out, sems) = rest[:RING], rest[RING:]
+    copies = []
     segment_rows(place, segs, qseg)
     acc[...] = jnp.zeros_like(acc)
     terms = [da[i, 2 * ROWS :, :].astype(F32) for i in range(2)]
@@ -205,10 +206,17 @@
         for i, block in enumerate(blocks):
             rows = slice(i * ROWS, (i + 1) * ROWS)
             at = pl.multiple_of((block // QUAD) * (2 * ROWS), 2 * ROWS)
-            dkv[pl.ds(at, ROWS), :] = dk[rows, :].astype(BF16)
-            dkv[pl.ds(at + ROWS, ROWS), :] = dv[rows, :].astype(BF16)
+            slot = 2 * pair + i
+            out[slot, :ROWS, :] = dk[rows, :].astype(BF16)
+            out[slot, ROWS:, :] = dv[rows, :].astype(BF16)
+            copies.append(
+                pltpu.make_async_copy(out.at[slot], dkv.at[pl.ds(at, 2 * ROWS)], sems.at[slot])
+            )
+            copies[-1].start()
 
     share_out(place[0], acc, keep, send)
+    for copy in copies:
+        copy.wait()
 
 
 def call(kernel, name, outs, operands, scalars=0, scratch=(), us=1):
@@ -295,15 +303,28 @@
     )(place[None], keep, came, gate_states, out_grad, norm_gain[None, :], gathered)
     grads = lax.all_gather(attn_grad, "ctx", axis_index_groups=CORES)
 
-    keep, send, extra, dkv = call(
+    outs = [(half, F32), (half, BF16), ((EXTRA, HD), BF16), ((RING * 2 * ROWS, HD), BF16)]
+    keep, send, extra, dkv = pl.pallas_call(
         backward_kernel,
-        "backward_tile",
-        [(half, F32), (half, BF16), ((EXTRA, HD), BF16), ((RING * 2 * ROWS, HD), BF16)],
-        (*shared, grads, *blocks[: RING - 1], far),
-        2,
-        [tile, half, half, (TILE, ROWS)],
-        us=9,
-    )
+        out_shape=tuple(jax.ShapeDtypeStruct(shape, dtype) for shape, dtype in outs),
+        in_specs=[pl.BlockSpec(memory_space=pltpu.SMEM)] * 2
+        + [pl.BlockSpec(memory_space=pltpu.VMEM)] * (3 + RING),
+        out_specs=(pl.BlockSpec(memory_space=pltpu.VMEM),) * 3
+        + (pl.BlockSpec(memory_space=pl.ANY),),
+        scratch_shapes=[
+            pltpu.VMEM(tile, F32),
+            pltpu.VMEM(half, F32),
+            pltpu.VMEM(half, F32),
+            pltpu.VMEM((TILE, ROWS), jnp.int32),
+            pltpu.VMEM((RING, 2 * ROWS, HD), BF16),
+            pltpu.SemaphoreType.DMA((RING,)),
+        ],
+        compiler_params=pltpu.CompilerParams(vmem_limit_bytes=VMEM_LIMIT),
+        cost_estimate=pl.CostEstimate(
+            flops=4_500_000_000, bytes_accessed=9_000_000, transcendentals=0
+        ),
+        name="backward_tile",
+    )(*shared, grads, *blocks[: RING - 1], far)
     dkv_sum = lax.psum_scatter(dkv, "ctx", tiled=True, axis_index_groups=RINGS)
     keep = keep + swap(send, CORE).astype(F32)
     send = jnp.concatenate([keep[ROWS:].astype(BF16), extra], axis=0)

time: 151 us -> 151 us (level)
    pallas_call x3 -> x2, Pallas kernels: 19.1 us -> 6.09 us  [call(): pl.pallas_call(kernel, out_shape=tuple((jax.ShapeDtypeStruct(shape, dtype...]
    pallas_call x0 -> x1, Pallas kernels: none -> 12.5 us  [per_device(): pl.pallas_call(backward_kernel, out_shape=tuple((jax.ShapeDtypeStruct(sha...]
where the time goes in v6:
time: 151 us; the launch traced here: 149 us
  starting transfers between devices  43.2 us (29%)
  blocking collectives  36.9 us (24%)
  waiting for transfers between devices  25.1 us (17%)
  Pallas kernels  19.8 us (13%)
  between operations  14.4 us (10%)
  other arithmetic  5.17 us (3%)
  local copies, waits for them, and re-layouts  4.88 us (3%)
    ppermute x8, starting transfers between devices, along(): lax.ppermute(value, 'ctx', [(i, (i + step * QUAD) % CTX) for i in range(C...  29.1 us
    all_gather x1, blocking collectives, per_device(): came = lax.all_gather(keep.astype(BF16), 'ctx', axis_index_groups=ZPAIRS)  16.9 us
    all_gather x1, blocking collectives, per_device(): came = lax.all_gather(send, 'ctx', axis_index_groups=ZPAIRS)  14.8 us
    all_to_all x2, waiting for transfers between devices, everywhere(): lax.all_to_all(value, axis, 0, 0, tiled=True, axis_index_groups=groups)  13.1 us
    pallas_call x1, Pallas kernels, per_device(): pl.pallas_call(backward_kernel, out_shape=tuple((jax.ShapeDtypeStruct(sha...  12.5 us
    all_to_all x2, starting transfers between devices, everywhere(): lax.all_to_all(value, axis, 0, 0, tiled=True, axis_index_groups=groups)  11.7 us
    all_gather x1, waiting for transfers between devices, per_device(): lax.all_gather(jnp.concatenate([first, product], axis=0), 'ctx', axis_ind...  8.89 us
    pallas_call x2, Pallas kernels, call(): pl.pallas_call(kernel, out_shape=tuple((jax.ShapeDtypeStruct(shape, dtype...  6.09 us
  transfers between devices with their start and end apart: 13, of which 6 were waited for; matrix products, arithmetic and copies ran while one was open for 3% of the time, Pallas kernels for 2%

profile of v6, /device:TPU:1, one launch (start us, length us, event | category | flops | bytes accessed | tf_op | source)
XLA Modules:
  0.0 149.3 jit_solution(15072236130262262819)
XLA Ops:
  9.2 1.6 %pad_maximum_fusion.1 = bf16[2,128,512]{2,1,0:T(8,128)(2,1)} fusion(bf16[1,128,512]{2,1,0:T(8,128)(2,1)S(1)} %multiply_convert_fusion, bf16[1,128,512]{2,1,0:T(8,128)(2,1)} %param.7), kind=kLoop, calls=%fused_computation.7 | loop fusion | flops 131072 | bytes 524288 | tf_op jit(solution)/shard_map/concatenate | solution.py:251
  11.0 5.9 %collective-permute-start.1 = (bf16[2,128,512]{2,1,0:T(8,128)(2,1)S(1)}, bf16[2,128,512]{2,1,0:T(8,128)(2,1)S(1)}, u32[]{:S(2)}, u32[]{:S(2)}) collective-permute-start(bf16[2,128,512]{2,1,0:T(8,128)(2,1)S(1)} %pad_maximum_fusion.own.rest_0_), channel_id=1, source_target_pairs={{0,28},{1,29},{2,30},{3,31},{4,0},{5,1},{6,2},{7,3},{8,4},{9,5},{1... | collective-permute-start | bytes 786440 | tf_op jit(solution)/shard_map/ppermute | solution.py:41
  16.9 1.9 %collective-permute-start = (bf16[2,128,512]{2,1,0:T(8,128)(2,1)S(1)}, bf16[2,128,512]{2,1,0:T(8,128)(2,1)S(1)}, u32[]{:S(2)}, u32[]{:S(2)}) collective-permute-start(bf16[2,128,512]{2,1,0:T(8,128)(2,1)S(1)} %pad_maximum_fusion.own.rest_0_), channel_id=1, source_target_pairs={{0,4},{1,5},{2,6},{3,7},{4,8},{5,9},{6,10},{7,11},{8,12},{9,13},{1... | collective-permute-start | bytes 786440 | tf_op jit(solution)/shard_map/ppermute | solution.py:41
  18.8 1.4 collective-permute-done.1.next_.rest_2_
  20.2 5.0 %collective-permute-start.2 = (bf16[2,128,512]{2,1,0:T(8,128)(2,1)S(1)}, bf16[2,128,512]{2,1,0:T(8,128)(2,1)S(1)}, u32[]{:S(2)}, u32[]{:S(2)}) collective-permute-start(bf16[2,128,512]{2,1,0:T(8,128)(2,1)S(1)} %collective-permute-done.1.next_.rest_2_), channel_id=1, source_target_pairs={{0,28},{1,29},{2,30},{3,31},{4,0},{5,1},{6,2},{7,3},{8,4},{9,5},{1... | collective-permute-start | bytes 786440 | tf_op jit(solution)/shard_map/ppermute | solution.py:41
  25.2 1.9 %collective-permute-start.3 = (bf16[2,128,512]{2,1,0:T(8,128)(2,1)S(1)}, bf16[2,128,512]{2,1,0:T(8,128)(2,1)S(1)}, u32[]{:S(2)}, u32[]{:S(2)}) collective-permute-start(bf16[2,128,512]{2,1,0:T(8,128)(2,1)S(1)} %collective-permute-done.prev.rest_1_), channel_id=1, source_target_pairs={{0,4},{1,5},{2,6},{3,7},{4,8},{5,9},{6,10},{7,11},{8,12},{9,13},{1... | collective-permute-start | bytes 786440 | tf_op jit(solution)/shard_map/ppermute | solution.py:41
  28.5 6.2 %collective-permute-start.7 = (bf16[2,64,512]{2,1,0:T(8,128)(2,1)S(1)}, bf16[2,64,512]{2,1,0:T(8,128)(2,1)S(1)}, u32[]{:S(2)}, u32[]{:S(2)}) collective-permute-start(bf16[2,64,512]{2,1,0:T(8,128)(2,1)S(1)} %slice.44), channel_id=1, source_target_pairs={{0,24},{1,25},{2,26},{3,27},{4,28},{5,29},{6,30},{7,31},{8,0},{9,1... | collective-permute-start | bytes 393224 | tf_op jit(solution)/shard_map/ppermute | solution.py:41
  34.8 1.9 %collective-permute-start.6 = (bf16[2,64,512]{2,1,0:T(8,128)(2,1)S(1)}, bf16[2,64,512]{2,1,0:T(8,128)(2,1)S(1)}, u32[]{:S(2)}, u32[]{:S(2)}) collective-permute-start(bf16[2,64,512]{2,1,0:T(8,128)(2,1)S(1)} %slice.43), channel_id=1, source_target_pairs={{0,8},{1,9},{2,10},{3,11},{4,12},{5,13},{6,14},{7,15},{8,16},{9,17... | collective-permute-start | bytes 393224 | tf_op jit(solution)/shard_map/ppermute | solution.py:41
  36.7 4.2 %collective-permute-start.5 = (bf16[2,128,512]{2,1,0:T(8,128)(2,1)S(1)}, bf16[2,128,512]{2,1,0:T(8,128)(2,1)S(1)}, u32[]{:S(2)}, u32[]{:S(2)}) collective-permute-start(bf16[2,128,512]{2,1,0:T(8,128)(2,1)S(1)} %collective-permute-done.2.next2.rest_4_), channel_id=1, source_target_pairs={{0,28},{1,29},{2,30},{3,31},{4,0},{5,1},{6,2},{7,3},{8,4},{9,5},{1... | collective-permute-start | bytes 786440 | tf_op jit(solution)/shard_map/ppermute | solution.py:41
  41.0 1.9 %collective-permute-start.4 = (bf16[2,128,512]{2,1,0:T(8,128)(2,1)S(1)}, bf16[2,128,512]{2,1,0:T(8,128)(2,1)S(1)}, u32[]{:S(2)}, u32[]{:S(2)}) collective-permute-start(bf16[2,128,512]{2,1,0:T(8,128)(2,1)S(1)} %collective-permute-done.3.prev2.rest_3_), channel_id=1, source_target_pairs={{0,4},{1,5},{2,6},{3,7},{4,8},{5,9},{6,10},{7,11},{8,12},{9,13},{1... | collective-permute-start | bytes 786440 | tf_op jit(solution)/shard_map/ppermute | solution.py:41
  42.9 8.9 %all-gather.7.cloned.1.call-done = bf16[8,128,512]{2,1,0:T(8,128)(2,1)} async-done(((bf16[2,128,512]{2,1,0:T(8,128)(2,1)}), bf16[8,128,512]{2,1,0:T(8,128)(2,1)}) %all-gather.7.cloned.1.call-update) | async-done | bytes 1048592 | tf_op jit(solution)/shard_map/all_gather | solution.py:250
  52.9 3.7 %forward_near.1.begun = f32[512,512]{1,0:T(8,128)S(1)} custom-call(s32[1]{0:T(128)} %bitcast.place, s32[32,2]{1,0:T(8,128)S(1)} %slice.32.ends, s32[32,128]{1,0:T(8,128)S(1)} %bitcast.32, bf16[4,128,512]{2,1,0:T(8,128)(2,1)S(1)} %slice_bitcast_fusion.q, bf16[2,128,512]{2,1,0:T(8,128)(2,1)S(1)} %pad_maximum_fusion.own.rest_0_, ...), custom_call_target="tpu_custom_call" | custom-call | flops 1000000000 | bytes 2000000 | tf_op jit(solution)/shard_map/forward_near/pallas_call | solution.py:223
  56.6 2.4 %forward_far.1 = (f32[256,512]{1,0:T(8,128)S(1)}, bf16[256,512]{1,0:T(8,128)(2,1)S(1)}, bf16[2,128,512]{2,1,0:T(8,128)(2,1)S(1)}) custom-call(s32[1]{0:T(128)} %bitcast.place, s32[32,2]{1,0:T(8,128)S(1)} %slice.32.ends, s32[32,128]{1,0:T(8,128)S(1)} %bitcast.33, bf16[4,128,512]{2,1,0:T(8,128)(2,1)S(1)} %slice_bitcast_fusion.q, ...), custom_call_target="tpu_custom_call" | custom-call | flops 1000000000 | bytes 2000000 | tf_op jit(solution)/shard_map/forward_far/pallas_call | solution.py:223
  59.1 2.3 %all-gather.1 = bf16[512,512]{1,0:T(8,128)(2,1)S(1)} all-gather(bf16[256,512]{1,0:T(8,128)(2,1)S(1)} %get-tuple-element.21), channel_id=3, replica_groups={{0,1},{2,3},{4,5},{6,7},{8,9},{10,11},{12,13},{14,15},{16,17},{18,19},{..., dimensions={0}, use_global_device_ids=true | all-gather | bytes 786432 | tf_op jit(solution)/shard_map/all_gather | solution.py:283
  61.5 16.9 %all-gather.2 = bf16[512,512]{1,0:T(8,128)(2,1)S(1)} all-gather(bf16[256,512]{1,0:T(8,128)(2,1)S(1)} %get-tuple-element.30), channel_id=4, replica_groups={{0,2},{1,3},{4,6},{5,7},{8,10},{9,11},{12,14},{13,15},{16,18},{17,19},{..., dimensions={0}, use_global_device_ids=true | all-gather | bytes 786432 | tf_op jit(solution)/shard_map/all_gather | solution.py:285
  79.7 2.9 %all-gather.3 = bf16[544,512]{1,0:T(8,128)(2,1)S(1)} all-gather(bf16[272,512]{1,0:T(8,128)(2,1)S(1)} %get-tuple-element.23), channel_id=5, replica_groups={{0,1},{2,3},{4,5},{6,7},{8,9},{10,11},{12,13},{14,15},{16,17},{18,19},{..., dimensions={0}, use_global_device_ids=true | all-gather | bytes 835584 | tf_op jit(solution)/shard_map/all_gather | solution.py:304
  82.5 12.5 %backward_tile.1 = (f32[256,512]{1,0:T(8,128)S(1)}, bf16[256,512]{1,0:T(8,128)(2,1)S(1)}, bf16[16,512]{1,0:T(8,128)(2,1)S(1)}, bf16[2048,512]{1,0:T(8,128)(2,1)}) custom-call(s32[1]{0:T(128)} %bitcast.place, s32[32,2]{1,0:T(8,128)S(1)} %slice.32.ends, s32[32,128]{1,0:T(8,128)S(1)} %bitcast.34, bf16[4,128,512]{2,1,0:T(8,128)(2,1)S(1)} %slice_bitcast_fusion.q, ...), custom_call_target="tpu_custom_call" | custom-call | flops 4499999744 | bytes 9000000 | tf_op jit(solution)/shard_map/backward_tile/pallas_call | solution.py:307
  95.0 2.3 %collective-permute-start.8 = (bf16[256,512]{1,0:T(8,128)(2,1)S(1)}, bf16[256,512]{1,0:T(8,128)(2,1)S(1)}, u32[]{:S(2)}, u32[]{:S(2)}) collective-permute-start(bf16[256,512]{1,0:T(8,128)(2,1)S(1)} %get-tuple-element.26), channel_id=1, source_target_pairs={{0,1},{1,0},{2,3},{3,2},{4,5},{5,4},{6,7},{7,6},{8,9},{9,8},{10,11... | collective-permute-start | bytes 786440 | tf_op jit(solution)/shard_map/ppermute | solution.py:45
  98.6 14.8 %all-gather.4 = bf16[288,512]{1,0:T(8,128)(2,1)S(1)} all-gather(bf16[144,512]{1,0:T(8,128)(2,1)S(1)} %pad_maximum_fusion.2), channel_id=6, replica_groups={{0,2},{1,3},{4,6},{5,7},{8,10},{9,11},{12,14},{13,15},{16,18},{17,19},{..., dimensions={0}, use_global_device_ids=true | all-gather | bytes 442368 | tf_op jit(solution)/shard_map/all_gather | solution.py:331
  114.0 5.5 %all-to-all-start = ((f32[16,1,512]{2,1,0:T(1,128)}), f32[16,1,512]{2,1,0:T(1,128)S(1)}, u32[]{:S(2)}, u32[]{:S(2)}) async-start(f32[16,1,512]{2,1,0:T(1,128)} %broadcast_in_dim.33), calls=%async_computation.1 | async-start | bytes 65536 | tf_op jit(solution)/shard_map/all_to_all | solution.py:50
  119.6 7.0 %all-to-all-done = f32[16,1,512]{2,1,0:T(1,128)S(1)} async-done(((f32[16,1,512]{2,1,0:T(1,128)}), f32[16,1,512]{2,1,0:T(1,128)S(1)}, u32[]{:S(2)}, u32[]{:S(2)}) %all-to-all-start) | async-done | bytes 32800 | tf_op jit(solution)/shard_map/all_to_all | solution.py:50
  127.2 6.2 %all-to-all-start.1 = ((f32[8,1,512]{2,1,0:T(1,128)}), f32[8,1,512]{2,1,0:T(1,128)S(1)}, u32[]{:S(2)}, u32[]{:S(2)}) async-start(f32[8,1,512]{2,1,0:T(1,128)} %broadcast_in_dim.34), calls=%async_computation.2 | async-start | bytes 32768 | tf_op jit(solution)/shard_map/all_to_all | solution.py:50
  134.1 6.1 %all-to-all-done.1 = f32[8,1,512]{2,1,0:T(1,128)S(1)} async-done(((f32[8,1,512]{2,1,0:T(1,128)}), f32[8,1,512]{2,1,0:T(1,128)S(1)}, u32[]{:S(2)}, u32[]{:S(2)}) %all-to-all-start.1) | async-done | bytes 16416 | tf_op jit(solution)/shard_map/all_to_all | solution.py:50
  140.8 1.7 %slice_bitcast_fusion.1 = (bf16[1,128,512]{2,1,0:T(8,128)(2,1)}, bf16[1,128,512]{2,1,0:T(8,128)(2,1)}) fusion(bf16[256,512]{1,0:T(8,128)(2,1)} %reduce-scatter.2.cloned.1.call-done), kind=kLoop, calls=%fused_computation.11 | loop fusion | bytes 524288 | tf_op jit(solution)/shard_map/broadcast_in_dim | solution.py:345
  (41 shorter events, 9.8 us)
Async XLA Ops:
  7.2 45.7 %copy-start.3 = (s32[1,4096]{1,0:T(1,128)S(1)}, s32[1,4096]{1,0:T(1,128)}, u32[]{:S(2)}) copy-start(s32[1,4096]{1,0:T(1,128)} %param.12) | copy-start | bytes 49156
  7.2 44.6 %all-gather.7.cloned.1.call-start = ((), (), s32[]{:S(2)}) async-start(), calls=%async_computation.4 | async-start | bytes 1310720 | tf_op jit(solution)/shard_map/all_gather | solution.py:250
  10.9 129.9 %reduce-scatter.2.cloned.1.call-start = ((), (), s32[]{:S(2)}) async-start(), calls=%async_computation.3 | async-start | bytes 2359296 | tf_op jit(solution)/shard_map/reduce_scatter | solution.py:328
  11.0 9.2 %collective-permute-start.1 = (bf16[2,128,512]{2,1,0:T(8,128)(2,1)S(1)}, bf16[2,128,512]{2,1,0:T(8,128)(2,1)S(1)}, u32[]{:S(2)}, u32[]{:S(2)}) collective-permute-start(bf16[2,128,512]{2,1,0:T(8,128)(2,1)S(1)} %pad_maximum_fusion.own.rest_0_), channel_id=1, source_target_pairs={{0,28},{1,29},{2,30},{3,31},{4,0},{5,1},{6,2},{7,3},{8,4},{9,5},{1... | collective-permute-start | bytes 786440 | tf_op jit(solution)/shard_map/ppermute | solution.py:41
  16.9 8.3 %collective-permute-start = (bf16[2,128,512]{2,1,0:T(8,128)(2,1)S(1)}, bf16[2,128,512]{2,1,0:T(8,128)(2,1)S(1)}, u32[]{:S(2)}, u32[]{:S(2)}) collective-permute-start(bf16[2,128,512]{2,1,0:T(8,128)(2,1)S(1)} %pad_maximum_fusion.own.rest_0_), channel_id=1, source_target_pairs={{0,4},{1,5},{2,6},{3,7},{4,8},{5,9},{6,10},{7,11},{8,12},{9,13},{1... | collective-permute-start | bytes 786440 | tf_op jit(solution)/shard_map/ppermute | solution.py:41
  20.2 8.3 %collective-permute-start.2 = (bf16[2,128,512]{2,1,0:T(8,128)(2,1)S(1)}, bf16[2,128,512]{2,1,0:T(8,128)(2,1)S(1)}, u32[]{:S(2)}, u32[]{:S(2)}) collective-permute-start(bf16[2,128,512]{2,1,0:T(8,128)(2,1)S(1)} %collective-permute-done.1.next_.rest_2_), channel_id=1, source_target_pairs={{0,28},{1,29},{2,30},{3,31},{4,0},{5,1},{6,2},{7,3},{8,4},{9,5},{1... | collective-permute-start | bytes 786440 | tf_op jit(solution)/shard_map/ppermute | solution.py:41
  25.2 9.6 %collective-permute-start.3 = (bf16[2,128,512]{2,1,0:T(8,128)(2,1)S(1)}, bf16[2,128,512]{2,1,0:T(8,128)(2,1)S(1)}, u32[]{:S(2)}, u32[]{:S(2)}) collective-permute-start(bf16[2,128,512]{2,1,0:T(8,128)(2,1)S(1)} %collective-permute-done.prev.rest_1_), channel_id=1, source_target_pairs={{0,4},{1,5},{2,6},{3,7},{4,8},{5,9},{6,10},{7,11},{8,12},{9,13},{1... | collective-permute-start | bytes 786440 | tf_op jit(solution)/shard_map/ppermute | solution.py:41
  28.5 28.1 %collective-permute-start.7 = (bf16[2,64,512]{2,1,0:T(8,128)(2,1)S(1)}, bf16[2,64,512]{2,1,0:T(8,128)(2,1)S(1)}, u32[]{:S(2)}, u32[]{:S(2)}) collective-permute-start(bf16[2,64,512]{2,1,0:T(8,128)(2,1)S(1)} %slice.44), channel_id=1, source_target_pairs={{0,24},{1,25},{2,26},{3,27},{4,28},{5,29},{6,30},{7,31},{8,0},{9,1... | collective-permute-start | bytes 393224 | tf_op jit(solution)/shard_map/ppermute | solution.py:41
  34.8 21.8 %collective-permute-start.6 = (bf16[2,64,512]{2,1,0:T(8,128)(2,1)S(1)}, bf16[2,64,512]{2,1,0:T(8,128)(2,1)S(1)}, u32[]{:S(2)}, u32[]{:S(2)}) collective-permute-start(bf16[2,64,512]{2,1,0:T(8,128)(2,1)S(1)} %slice.43), channel_id=1, source_target_pairs={{0,8},{1,9},{2,10},{3,11},{4,12},{5,13},{6,14},{7,15},{8,16},{9,17... | collective-permute-start | bytes 393224 | tf_op jit(solution)/shard_map/ppermute | solution.py:41
  36.7 19.9 %collective-permute-start.5 = (bf16[2,128,512]{2,1,0:T(8,128)(2,1)S(1)}, bf16[2,128,512]{2,1,0:T(8,128)(2,1)S(1)}, u32[]{:S(2)}, u32[]{:S(2)}) collective-permute-start(bf16[2,128,512]{2,1,0:T(8,128)(2,1)S(1)} %collective-permute-done.2.next2.rest_4_), channel_id=1, source_target_pairs={{0,28},{1,29},{2,30},{3,31},{4,0},{5,1},{6,2},{7,3},{8,4},{9,5},{1... | collective-permute-start | bytes 786440 | tf_op jit(solution)/shard_map/ppermute | solution.py:41
  41.0 15.6 %collective-permute-start.4 = (bf16[2,128,512]{2,1,0:T(8,128)(2,1)S(1)}, bf16[2,128,512]{2,1,0:T(8,128)(2,1)S(1)}, u32[]{:S(2)}, u32[]{:S(2)}) collective-permute-start(bf16[2,128,512]{2,1,0:T(8,128)(2,1)S(1)} %collective-permute-done.3.prev2.rest_3_), channel_id=1, source_target_pairs={{0,4},{1,5},{2,6},{3,7},{4,8},{5,9},{6,10},{7,11},{8,12},{9,13},{1... | collective-permute-start | bytes 786440 | tf_op jit(solution)/shard_map/ppermute | solution.py:41
  59.0 19.4 %copy-start = (bf16[8,128,512]{2,1,0:T(8,128)(2,1)S(1)}, bf16[8,128,512]{2,1,0:T(8,128)(2,1)}, u32[]{:S(2)}) copy-start(bf16[8,128,512]{2,1,0:T(8,128)(2,1)} %all-gather.7.cloned.1.call-done) | copy-start | bytes 3145732
  59.0 19.4 %copy-start.1 = (bf16[1,128,512]{2,1,0:T(8,128)(2,1)S(1)}, bf16[1,128,512]{2,1,0:T(8,128)(2,1)}, u32[]{:S(2)}) copy-start(bf16[1,128,512]{2,1,0:T(8,128)(2,1)} %gate.1) | copy-start | bytes 393220
  59.1 19.4 %copy-start.2 = (bf16[1,128,512]{2,1,0:T(8,128)(2,1)S(1)}, bf16[1,128,512]{2,1,0:T(8,128)(2,1)}, u32[]{:S(2)}) copy-start(bf16[1,128,512]{2,1,0:T(8,128)(2,1)} %grad.1) | copy-start | bytes 393220
  59.1 19.4 %copy-start.4 = (f32[512]{0:T(512)S(1)}, f32[512]{0:T(512)}, u32[]{:S(2)}) copy-start(f32[512]{0:T(512)} %param.13) | copy-start | bytes 6148
  95.0 3.4 %collective-permute-start.8 = (bf16[256,512]{1,0:T(8,128)(2,1)S(1)}, bf16[256,512]{1,0:T(8,128)(2,1)S(1)}, u32[]{:S(2)}, u32[]{:S(2)}) collective-permute-start(bf16[256,512]{1,0:T(8,128)(2,1)S(1)} %get-tuple-element.26), channel_id=1, source_target_pairs={{0,1},{1,0},{2,3},{3,2},{4,5},{5,4},{6,7},{7,6},{8,9},{9,8},{10,11... | collective-permute-start | bytes 786440 | tf_op jit(solution)/shard_map/ppermute | solution.py:45
  114.0 12.5 %all-to-all-start = ((f32[16,1,512]{2,1,0:T(1,128)}), f32[16,1,512]{2,1,0:T(1,128)S(1)}, u32[]{:S(2)}, u32[]{:S(2)}) async-start(f32[16,1,512]{2,1,0:T(1,128)} %broadcast_in_dim.33), calls=%async_computation.1 | async-start | bytes 65536 | tf_op jit(solution)/shard_map/all_to_all | solution.py:50
  127.2 13.0 %all-to-all-start.1 = ((f32[8,1,512]{2,1,0:T(1,128)}), f32[8,1,512]{2,1,0:T(1,128)S(1)}, u32[]{:S(2)}, u32[]{:S(2)}) async-start(f32[8,1,512]{2,1,0:T(1,128)} %broadcast_in_dim.34), calls=%async_computation.2 | async-start | bytes 32768 | tf_op jit(solution)/shard_map/all_to_all | solution.py:50
Sparse Core Ops, SparseCore 0:
  11.0 40.7 all-gather.6
  95.1 42.4 reduce-scatter.1
